TPU v7x, 32 devices: a whole 2x2x4 slice. The times are simulated.
32 devices in a mesh: group: 8 (over y, x, core), tensor: 4 (over z).
Axes of the slice: x: 2, y: 2, z: 4, core: 2. Of those that a mesh axis runs over, the one named last changes fastest.
Arguments:
- retrieved: bfloat16 [4096, 2, 2560], P('group', None, 'tensor'), may hold values from -6 to 6
- branch_states: bfloat16 [4096, 2, 2560], P('group', None, 'tensor'), may hold values from -62 to 62
- out_grad: bfloat16 [4096, 2, 2560], P('group', None, 'tensor'), may hold values from -6 to 6
- key_weight: bfloat16 [2, 2560, 2560], P(None, None, 'tensor'), may hold values from -0.125 to 0.125
- value_weight: bfloat16 [2560, 2560], P(None, 'tensor'), may hold values from -0.125 to 0.125
- key_grad_acc: float32 [2, 2560, 2560], P(None, 'group', 'tensor'), may hold values from -6 to 6
- value_grad_acc: float32 [2560, 2560], P('group', 'tensor'), may hold values from -6 to 6
- row_index: int32 [4096, 2], P('group'), may hold values from 0 to 2047, as said below
- row_tier: int32 [2048], P('group'), may hold values 0 or 1
- adam_mean: float32 [2048, 2560], P('group', 'tensor'), may hold values from -3 to 3
- adam_second: float32 [2048, 2560], P('group', 'tensor'), may hold values from 0.01 to 1
Outputs:
- key_grad: float32 [2, 2560, 2560], P(None, 'group', 'tensor')
- value_grad: float32 [2560, 2560], P('group', 'tensor')
- new_mean: float32 [2048, 2560], P('group', 'tensor')
- new_second: float32 [2048, 2560], P('group', 'tensor')
- row_step: float32 [2048, 2560], P('group', 'tensor')
Inputs may be any that keep to these rules, and one draw needn't show every extreme that they name: `row_index`: rows o * 256 to (o + 1) * 256 - 1 belong to owner o. Of the 1024 entries of each group's 512 tokens, at most 128 belong to one owner, and one owner receives exactly 128 entries from every group.
All inputs are finite; a program needn't handle non-finite values. No bound on the sum of `row_tier` on one device may be relied on, other than what follows from the above.
Results may differ from a plain program's by a relative error of at most 0.0054.
Values may be sent and summed in bfloat16 or wider, within the bound.
No kernel may reach another device: no remote copies, remote signals or barrier semaphores. Data moves between devices by JAX's collectives and lax.ppermute only.
A program may use at most 128 MiB of HBM per device.

v0:
```python
import jax
import jax.numpy as jnp
from jax import lax
from jax.sharding import PartitionSpec as P

CAP = 128


EPS_NORM = 1e-06
EPS_ADAM = 1e-08
FIRST_BIAS = 1.0 - 0.9**10
SECOND_BIAS = 1.0 - 0.95**10


def on_device(
    retrieved,
    branch_states,
    out_grad,
    key_weight,
    value_weight,
    key_grad_acc,
    value_grad_acc,
    row_index,
    row_tier,
    adam_mean,
    adam_second,
):
    tok_count, key_count, width = branch_states.shape
    groups = lax.axis_size("group")
    owned_rows = adam_mean.shape[0]
    local_memory = jnp.sum(retrieved.astype(jnp.float32), axis=1).astype(jnp.bfloat16)
    memory = lax.all_gather(local_memory, "tensor", axis=1, tiled=True)
    model_width = memory.shape[1]
    key_vals = jnp.einsum("td,jdc->tjc", memory, key_weight, preferred_element_type=jnp.float32)
    values = jnp.dot(memory, value_weight, preferred_element_type=jnp.float32)
    states = branch_states.astype(jnp.float32)
    grads_out = out_grad.astype(jnp.float32)
    partial_dots = (
        jnp.sum(states * states, axis=-1),
        jnp.sum(key_vals * key_vals, axis=-1),
        jnp.sum(states * key_vals, axis=-1),
        jnp.sum(grads_out * values[:, None, :], axis=-1),
    )
    state_sum, key_sum, cross_dot, out_dot = lax.psum(
        (partial_dots[0], partial_dots[1], partial_dots[2], partial_dots[3]), "tensor"
    )
    root_width = jnp.sqrt(jnp.float32(model_width))
    state_rs = lax.rsqrt(state_sum / model_width + EPS_NORM)
    key_rs = lax.rsqrt(key_sum / model_width + EPS_NORM)
    scores = cross_dot * state_rs * key_rs / root_width
    gate_val = jax.nn.sigmoid(scores)
    dscore = out_dot * gate_val * (1.0 - gate_val)
    key_cot = (
        (key_rs * dscore / root_width)[..., None]
        * (states * state_rs[..., None] - key_vals * (key_rs * scores / root_width)[..., None])
    ).astype(jnp.bfloat16)
    value_cot = jnp.sum(gate_val[..., None] * grads_out, axis=1).astype(jnp.bfloat16)
    joined = jnp.concatenate(
        [key_cot[:, branch, :] for branch in range(key_count)] + [value_cot], axis=1
    )
    shard_rows = model_width // groups
    weight_sum = lax.psum_scatter(
        lax.dot_general(
            memory, joined, (((0,), (0,)), ((), ())), preferred_element_type=jnp.float32
        ),
        "group",
        scatter_dimension=0,
        tiled=True,
    )
    weight_sum = weight_sum.reshape(shard_rows, key_count + 1, width)
    key_grad = key_grad_acc + jnp.transpose(weight_sum[:, :key_count, :], (1, 0, 2))
    value_grad = value_grad_acc + weight_sum[:, key_count, :]
    term = lax.dot_general(
        key_weight, key_cot, (((0, 2), (1, 2)), ((), ())), preferred_element_type=jnp.float32
    )
    memory_cot_t = lax.psum_scatter(
        term
        + lax.dot_general(
            value_weight, value_cot, (((1,), (1,)), ((), ())), preferred_element_type=jnp.float32
        ),
        "tensor",
        scatter_dimension=0,
        tiled=True,
    )
    flat_rows = row_index.reshape(-1)
    owner_idx = flat_rows // owned_rows
    local_row = flat_rows - owner_idx * owned_rows
    entry_tok = lax.broadcasted_iota(jnp.int32, row_index.shape, 0).reshape(-1)
    owner_marks = (owner_idx[:, None] == jnp.arange(groups, dtype=jnp.int32)[None, :]).astype(
        jnp.int32
    )
    slot_place = jnp.sum(jnp.cumsum(owner_marks, axis=0) * owner_marks, axis=1) - 1
    slot_index = owner_idx * CAP + slot_place
    slot_token = jnp.full((groups * CAP,), tok_count, jnp.int32).at[slot_index].set(entry_tok)
    slot_row = (
        jnp.full((groups * CAP,), owned_rows, jnp.float32)
        .at[slot_index]
        .set(local_row.astype(jnp.float32))
    )
    padded = jnp.concatenate([memory_cot_t, jnp.zeros((width, 1), jnp.float32)], axis=1)
    outgoing = jnp.take(padded, slot_token, axis=1).reshape(width, groups, CAP)
    incoming, incoming_rows = (
        lax.all_to_all(outgoing, "group", split_axis=1, concat_axis=1, tiled=True),
        lax.all_to_all(
            slot_row.reshape(1, groups, CAP), "group", split_axis=1, concat_axis=1, tiled=True
        ),
    )
    slot_targets = incoming_rows.reshape(-1).astype(jnp.int32)
    summed = jax.ops.segment_sum(
        incoming.reshape(width, -1).T, slot_targets, num_segments=owned_rows + 1
    )
    row_grad = summed[:owned_rows]
    row_sum = lax.psum(jnp.sum(row_grad * row_grad, axis=1), "tensor")
    is_hot = (row_tier == 1)[:, None]
    mean_hot = 0.9 * adam_mean + 0.1 * row_grad
    second_hot = 0.95 * adam_second + 0.05 * row_grad * row_grad
    step_hot = mean_hot / FIRST_BIAS / (jnp.sqrt(second_hot / SECOND_BIAS) + EPS_ADAM)
    step_cold = row_grad * lax.rsqrt(row_sum / model_width + EPS_NORM)[:, None]
    new_mean = jnp.where(is_hot, mean_hot, adam_mean)
    new_second = jnp.where(is_hot, second_hot, adam_second)
    row_step = jnp.where(is_hot, step_hot, step_cold)
    return (key_grad, value_grad, new_mean, new_second, row_step)


def solution(mesh):
    return jax.shard_map(
        on_device,
        mesh=mesh,
        in_specs=(
            P("group", None, "tensor"),
            P("group", None, "tensor"),
            P("group", None, "tensor"),
            P(None, None, "tensor"),
            P(None, "tensor"),
            P(None, "group", "tensor"),
            P("group", "tensor"),
            P("group", None),
            P("group"),
            P("group", "tensor"),
            P("group", "tensor"),
        ),
        out_specs=(
            P(None, "group", "tensor"),
            P("group", "tensor"),
            P("group", "tensor"),
            P("group", "tensor"),
            P("group", "tensor"),
        ),
        check_vma=False,
    )
```

profile of v0, /device:TPU:0, one launch (start us, length us, event | category | flops | bytes accessed | tf_op | source)
XLA Modules:
  0.0 379.8 jit_solution(4192804987440116266)
XLA Ops:
  7.2 5.5 %reduce_sum.75 = bf16[512,640]{1,0:T(8,128)(2,1)} reduce(bf16[512,2,640]{2,1,0:T(2,128)(2,1)} %param.11, bf16[]{:T(256)} %constant.27.clone.1), dimensions={1}, to_apply=%region_0.0 | reduce | flops 327680 | bytes 1966082 | tf_op jit(solution)/shard_map/reduce_sum | solution.py:31
  12.8 57.5 %all-gather.2.cloned.1.call-done = bf16[512,2560]{1,0:T(8,128)(2,1)} async-done(((bf16[512,640]{1,0:T(8,128)(2,1)}), bf16[512,2560]{1,0:T(8,128)(2,1)}) %all-gather.2.cloned.1.call-update) | async-done | bytes 2621456 | tf_op jit(solution)/shard_map/all_gather | solution.py:32
  70.3 9.0 %multiply_reduce_fusion = (f32[512,2]{0,1:T(2,128)S(1)}, f32[512,2]{0,1:T(2,128)S(1)}, f32[512,2]{0,1:T(2,128)S(1)}, f32[512,2,640]{2,0,1:T(8,128)}) fusion(bf16[512,2,640]{2,1,0:T(2,128)(2,1)} %param.12, bf16[2,2560,640]{2,1,0:T(8,128)(2,1)} %param.14, bf16[512,2560]{1,0:T(8,128)(2,1)} %all-gather.2.cloned.1.call-done), kind=kOutput, calls=%fused_computation.20 | convolution fusion | flops 3360027648 | bytes 13119488 | tf_op jit(solution)/shard_map/td,jdc->tjc/dot_general | solution.py:34
  79.3 16.3 %all-reduce.1 = (f32[512,2]{0,1:T(2,128)S(1)}, f32[512,2]{0,1:T(2,128)S(1)}, f32[512,2]{0,1:T(2,128)S(1)}) all-reduce(f32[512,2]{0,1:T(2,128)S(1)} %get-tuple-element.21, f32[512,2]{0,1:T(2,128)S(1)} %get-tuple-element.20, f32[512,2]{0,1:T(2,128)S(1)} %get-tuple-element.22), channel_id=1, replica_groups=mesh['group'=8,'tensor'=4] {'tensor'}, use_global_device_ids=true, to_apply=%region_6.0 | all-reduce | flops 3072 | bytes 24576 | tf_op jit(solution)/shard_map/psum | solution.py:44
  97.1 4.0 %fusion.36 = f32[512,640]{1,0:T(8,128)S(1)} fusion(bf16[512,2560]{1,0:T(8,128)(2,1)} %all-gather.2.cloned.1.call-done, bf16[2560,640]{1,0:T(8,128)(2,1)S(1)} %copy-done), kind=kOutput, calls=%fused_computation.88 | convolution fusion | flops 1677721600 | bytes 7208960 | tf_op jit(solution)/shard_map/dot_general | solution.py:35
  101.2 7.8 %fusion.1 = (f32[512,2]{1,0:T(8,128)S(1)}, bf16[512,640]{1,0:T(8,128)(2,1)}) fusion(bf16[512,2,640]{2,1,0:T(2,128)(2,1)S(1)} %copy-done.5, f32[512,640]{1,0:T(8,128)S(1)} %fusion.36, f32[512,2]{1,0:T(8,128)S(1)} %copy-done.7), kind=kLoop, calls=%fused_computation.11 | loop fusion | flops 2948096 | bytes 3284992 | tf_op jit(solution)/shard_map/reduce_sum | solution.py:42
  109.1 8.5 %psum.36 = f32[512,2]{0,1:T(2,128)S(1)} all-reduce(f32[512,2]{0,1:T(2,128)S(1)} %copy.42), channel_id=1, replica_groups=mesh['group'=8,'tensor'=4] {'tensor'}, use_global_device_ids=true, to_apply=%region_4.0 | all-reduce | flops 1024 | bytes 8192 | tf_op jit(solution)/shard_map/psum | solution.py:44
  117.6 3.5 fusion.37
  121.8 8.3 %fusion = f32[2560,512]{0,1:T(8,128)} fusion(f32[512,2560]{1,0:T(8,128)S(1)} %fusion.37, bf16[512,2,640]{2,0,1:T(8,128)(2,1)S(1)} %fusion.7, bf16[2,2560,640]{2,1,0:T(8,128)(2,1)} %param.14), kind=kOutput, calls=%fused_computation.5 | convolution fusion | flops 3356753920 | bytes 18350080 | tf_op jit(solution)/shard_map/dot_general | solution.py:73
  131.2 11.5 %fusion.11 = f32[2560,1920]{1,0:T(8,128)} fusion(bf16[512,2560]{1,0:T(8,128)(2,1)} %all-gather.2.cloned.1.call-done, bf16[512,640]{1,0:T(8,128)(2,1)S(1)} %copy-done.9, bf16[512,640]{1,0:T(8,128)(2,1)S(1)} %get-tuple-element.32, bf16[512,640]{1,0:T(8,128)(2,1)S(1)} %get-tuple-element.31), kind=kOutput, calls=%fused_computation.23 | convolution fusion | flops 5039063040 | bytes 24248320 | tf_op jit(solution)/shard_map/dot_general | solution.py:63
  144.0 2.3 reduce-window.6
  146.9 4.9 %scatter_custom_fusion = f32[1024]{0:T(1024)} fusion(s32[1024]{0:T(1024)S(1)} %bitcast.65, f32[1024]{0:T(1024)S(1)} %get-tuple-element.35, f32[]{:T(128)} %constant.70.clone.1), kind=kCustom, calls=%fused_computation.83 | custom fusion | bytes 4100 | tf_op jit(solution)/shard_map/scatter | solution.py:98
  151.8 3.8 all-to-all-start
  155.7 4.3 %scatter_custom_fusion.1 = s32[1024]{0:T(1024)S(1)} fusion(s32[1024]{0:T(1024)S(1)} %bitcast.66, s32[1024]{0:T(1024)S(1)} %reshape.211, s32[]{:T(128)} %constant.78.clone.1), kind=kCustom, calls=%fused_computation.80 | custom fusion | bytes 4100 | tf_op jit(solution)/shard_map/scatter | solution.py:94
  160.1 63.5 %reduce-scatter.5.cloned.1.call-done = f32[640,512]{0,1:T(8,128)} async-done(((f32[2560,512]{0,1:T(8,128)}), f32[640,512]{0,1:T(8,128)}) %reduce-scatter.5.cloned.1.call-update) | async-done | bytes 1310736 | tf_op jit(solution)/shard_map/reduce_scatter | solution.py:76
  225.0 5.2 %gather_fusion = f32[1024,640]{1,0:T(8,128)} fusion(f32[640,513]{0,1:T(8,128)S(1)} %concatenate.7, s32[1024]{0:T(1024)S(1)} %fusion.30), kind=kCustom, calls=%fused_computation | custom fusion | bytes 5246976 | tf_op jit(solution)/shard_map/jit(_take)/gather | solution.py:101
  230.2 3.7 broadcast_select_fusion
  233.9 4.0 %all-to-all-start.1 = ((f32[640,8,128]{0,2,1:T(8,128)}), f32[640,8,128]{0,2,1:T(8,128)S(1)}, u32[]{:S(2)}, u32[]{:S(2)}) async-start(f32[640,8,128]{0,2,1:T(8,128)} %broadcast_select_fusion), calls=%async_computation.3 | async-start | bytes 5242880 | tf_op jit(solution)/shard_map/all_to_all | solution.py:103
  237.9 3.2 copy.46
  241.1 2.6 copy.47
  243.7 27.6 %all-to-all-done.1 = f32[640,8,128]{0,2,1:T(8,128)S(1)} async-done(((f32[640,8,128]{0,2,1:T(8,128)}), f32[640,8,128]{0,2,1:T(8,128)S(1)}, u32[]{:S(2)}, u32[]{:S(2)}) %all-to-all-start.1) | async-done | bytes 2621472 | tf_op jit(solution)/shard_map/all_to_all | solution.py:103
  271.2 1.5 copy-done.3
  272.8 8.0 %scatter_custom_fusion.2 = f32[257,640]{1,0:T(8,128)S(1)} fusion(s32[1024]{0:T(1024)S(1)} %bitcast.67, f32[1024,640]{1,0:T(8,128)} %bitcast.62, f32[]{:T(128)} %constant.30.clone.1), kind=kCustom, calls=%fused_computation.41 | custom fusion | flops 655360 | bytes 658432 | tf_op jit(solution)/shard_map/scatter-add | solution.py:109
  280.9 10.2 %psum.39 = f32[256]{0:T(256)S(1)} all-reduce(f32[256]{0:T(256)S(1)} %multiply_reduce_fusion.1), channel_id=1, replica_groups=mesh['group'=8,'tensor'=4] {'tensor'}, use_global_device_ids=true, to_apply=%region_19.20 | all-reduce | flops 256 | bytes 2048 | tf_op jit(solution)/shard_map/psum | solution.py:113
  291.1 2.9 multiply_select_fusion
  294.0 64.2 %reduce-scatter.3.cloned.1.call-done = f32[320,1920]{1,0:T(8,128)} async-done(((f32[2560,1920]{1,0:T(8,128)}), f32[320,1920]{1,0:T(8,128)}) %reduce-scatter.3.cloned.1.call-update) | async-done | bytes 2457616 | tf_op jit(solution)/shard_map/reduce_scatter | solution.py:62
  358.2 2.6 copy.45
  360.8 1.6 copy-done.2
  362.4 3.0 fusion.10
  365.4 2.9 copy.51
  368.3 2.6 fusion.17
  370.8 2.4 copy.52
  (59 shorter events, 7.2 us)
Async XLA Ops:
  7.2 89.9 %copy-start = (bf16[2560,640]{1,0:T(8,128)(2,1)S(1)}, bf16[2560,640]{1,0:T(8,128)(2,1)}, u32[]{:S(2)}) copy-start(bf16[2560,640]{1,0:T(8,128)(2,1)} %param.15) | copy-start | bytes 9830404
  7.2 63.1 %all-gather.2.cloned.1.call-start = ((), (), s32[]{:S(2)}) async-start(), calls=%async_computation.4 | async-start | bytes 3276800 | tf_op jit(solution)/shard_map/all_gather | solution.py:32
  12.7 210.9 %reduce-scatter.5.cloned.1.call-start = ((), (), s32[]{:S(2)}) async-start(), calls=%async_computation.6 | async-start | bytes 6553600 | tf_op jit(solution)/shard_map/reduce_scatter | solution.py:76
  97.1 4.1 %copy-start.5 = (bf16[512,2,640]{2,1,0:T(2,128)(2,1)S(1)}, bf16[512,2,640]{2,1,0:T(2,128)(2,1)}, u32[]{:S(2)}) copy-start(bf16[512,2,640]{2,1,0:T(2,128)(2,1)} %param.13) | copy-start | bytes 3932164
  97.1 4.1 %copy-start.7 = (f32[512,2]{1,0:T(8,128)S(1)}, f32[512,2]{1,0:T(8,128)}, u32[]{:S(2)}) copy-start(f32[512,2]{1,0:T(8,128)} %copy.44) | copy-start | bytes 12292
  117.6 3.5 copy-start.4
  117.6 3.5 copy-start.6
  117.6 3.5 copy-start.10
  130.1 1.1 copy-start.9
  130.1 228.1 %reduce-scatter.3.cloned.1.call-start = ((), (), s32[]{:S(2)}) async-start(), calls=%async_computation.5 | async-start | bytes 22118400 | tf_op jit(solution)/shard_map/reduce_scatter | solution.py:62
  142.6 0.7 copy-start.11
  151.8 82.1 %all-to-all-start = ((f32[1,8,128]{2,0,1:T(1,128)}), f32[1,8,128]{2,0,1:T(1,128)S(1)}, u32[]{:S(2)}, u32[]{:S(2)}) async-start(f32[1,8,128]{2,0,1:T(1,128)} %bitcast.9), calls=%async_computation.1 | async-start | bytes 8192 | tf_op jit(solution)/shard_map/all_to_all | solution.py:104
  233.9 37.4 %all-to-all-start.1 = ((f32[640,8,128]{0,2,1:T(8,128)}), f32[640,8,128]{0,2,1:T(8,128)S(1)}, u32[]{:S(2)}, u32[]{:S(2)}) async-start(f32[640,8,128]{0,2,1:T(8,128)} %broadcast_select_fusion), calls=%async_computation.3 | async-start | bytes 5242880 | tf_op jit(solution)/shard_map/all_to_all | solution.py:103
  237.8 5.8 %copy-start.12 = (s32[256]{0:T(256)S(1)}, s32[256]{0:T(256)}, u32[]{:S(2)}) copy-start(s32[256]{0:T(256)} %param.19) | copy-start | bytes 3076
  237.9 53.2 %copy-start.8 = (f32[256,640]{1,0:T(8,128)S(1)}, f32[256,640]{1,0:T(8,128)}, u32[]{:S(2)}) copy-start(f32[256,640]{1,0:T(8,128)} %param.21) | copy-start | bytes 1966084
  271.2 1.5 copy-start.3
  360.8 1.6 copy-start.2
  365.4 7.8 %copy-start.1 = (bf16[2560,640]{1,0:T(8,128)(2,1)S(1)}, bf16[2560,640]{1,0:T(8,128)(2,1)}, u32[]{:S(2)}) copy-start(bf16[2560,640]{1,0:T(8,128)(2,1)} %param.15) | copy-start | bytes 9830404
Sparse Core Ops, SparseCore 0:
  12.9 57.3 all-gather.1
  130.2 93.3 reduce-scatter.4
  227.3 130.8 reduce-scatter.2
where the time goes:
time: 381 us; the launch traced here: 380 us
  waiting for transfers between devices  213 us (56%)
  other arithmetic  37.5 us (10%)
  local copies, waits for them, and re-layouts  36.4 us (10%)
  matrix products  36.3 us (10%)
  blocking collectives  34.9 us (9%)
  between operations  14 us (4%)
  starting transfers between devices  7.85 us (2%)
    reduce_scatter x1, waiting for transfers between devices, on_device(): lax.psum_scatter(lax.dot_general(memory, joined, (((0,), (0,)), ((), ()))...  64.2 us
    reduce_scatter x1, waiting for transfers between devices, on_device(): lax.psum_scatter(term + lax.dot_general(value_weight, value_cot, (((1,),...  63.5 us
    all_gather x1, waiting for transfers between devices, on_device(): memory = lax.all_gather(local_memory, 'tensor', axis=1, tiled=True)  57.5 us
    all_to_all x1, waiting for transfers between devices, on_device(): lax.all_to_all(outgoing, 'group', split_axis=1, concat_axis=1, tiled=True)  27.6 us
    psum x2, blocking collectives, on_device(): lax.psum((partial_dots[0], partial_dots[1], partial_dots[2], partial_dots...  24.8 us
    unnamed x31, local copies, waits for them, and re-layouts  16 us
    dot_general x1, matrix products, on_device(): lax.dot_general(memory, joined, (((0,), (0,)), ((), ())), preferred_eleme...  11.5 us
    psum x1, blocking collectives, on_device(): row_sum = lax.psum(jnp.sum(row_grad * row_grad, axis=1), 'tensor')  10.2 us
  transfers between devices with their start and end apart: 5, of which 4 were waited for; matrix products, arithmetic and copies ran while one was open for 14% of the time, Pallas kernels for 0%

commit v1 on v0

v1 whole, which is shorter than its diff:
```python
import functools

import jax
import jax.numpy as jnp
from jax import lax
from jax.experimental import pallas as pl
from jax.experimental.pallas import tpu as pltpu
from jax.sharding import PartitionSpec as P

CAP = 128
HALVES = 2
VMEM_BYTES = 48 * 1024 * 1024


EPS_NORM = 1e-06
EPS_ADAM = 1e-08
FIRST_BIAS = 1.0 - 0.9**10
SECOND_BIAS = 1.0 - 0.95**10

F32, BF16 = jnp.float32, jnp.bfloat16


def params():
    return pltpu.CompilerParams(vmem_limit_bytes=VMEM_BYTES)


def cost(macs, nbytes):
    return pl.CostEstimate(flops=2 * macs, bytes_accessed=nbytes, transcendentals=0)


def ring_device(place, size):
    return jnp.where(2 * place < size, 2 * place, 2 * (size - place) - 1)


def ring_place(device, size):
    return jnp.where(device % 2 == 0, device // 2, size - 1 - device // 2)


def ring_pass(part, axis):
    size = lax.axis_size(axis)
    order = list(range(0, size, 2)) + list(range(1, size, 2))[::-1]
    return lax.ppermute(part, axis, [(order[i], order[(i + 1) % size]) for i in range(size)])


def others_over(axis, part):
    size = lax.axis_size(axis)
    return [
        lax.ppermute(part, axis, [(i, (i + step) % size) for i in range(size)])
        for step in range(1, size)
    ]


def swap_over(axis, bit, part):
    size = lax.axis_size(axis)
    return lax.ppermute(part, axis, [(i, i ^ bit) for i in range(size)])


def forward_kernel(first, last, shard_ref, *refs):
    refs = list(refs)
    parts = [refs.pop(0) for _ in range(HALVES)]
    key_ref, value_ref = refs.pop(0), refs.pop(0)
    if not first:
        acc_ref = refs.pop(0)
        refs.pop(0)
    if last:
        state_ref, grad_ref = refs.pop(0), refs.pop(0)
    out_ref, turned_ref = refs.pop(0), refs.pop(0)
    key_count = key_ref.shape[0]

    def body(part):
        memory = part[...]
        turned_ref[...] = memory.T
        vals = []
        for j in range(key_count + 1):
            weight = key_ref[j] if j < key_count else value_ref[...]
            val = jnp.dot(memory, weight, preferred_element_type=F32)
            if not first:
                val = val + acc_ref[j]
            vals.append(val)
            if j < key_count or not last:
                out_ref[j] = val
        if last:
            states = [state_ref[j].astype(F32) for j in range(key_count)]
            sums = [jnp.sum(s * s, axis=1, keepdims=True) for s in states]
            sums += [jnp.sum(k * k, axis=1, keepdims=True) for k in vals[:-1]]
            sums += [jnp.sum(s * k, axis=1, keepdims=True) for s, k in zip(states, vals)]
            sums += [
                jnp.sum(grad_ref[j].astype(F32) * vals[-1], axis=1, keepdims=True)
                for j in range(key_count)
            ]
            lane = lax.broadcasted_iota(jnp.int32, (memory.shape[0], 128), 1)
            table = jnp.zeros((memory.shape[0], 128), F32)
            for i, s in enumerate(sums):
                table = jnp.where(lane == i, s, table)
            refs[0][...] = table.T[: 4 * key_count]

    for h in range(HALVES):
        pl.when(pl.program_id(0) == h)(functools.partial(body, parts[h]))


def forward(shard, parts, key_weight, value_weight, carry, extra):
    half, width = parts[0].shape
    key_count, model_width, _ = key_weight.shape
    tok_count = half * HALVES
    first, last = carry is None, extra is not None
    whole = pl.BlockSpec((half, width), lambda i, s: (0, 0))
    in_specs = [whole] * HALVES + [
        pl.BlockSpec((key_count, width, width), lambda i, s: (0, s[0], 0)),
        pl.BlockSpec((width, width), lambda i, s: (s[0], 0)),
    ]
    args = [shard, *parts, key_weight, value_weight]
    aliases = {}
    acc_spec = pl.BlockSpec((key_count + 1, half, width), lambda i, s: (0, i, 0))
    if not first:
        in_specs += [acc_spec, pl.BlockSpec(memory_space=pl.ANY)]
        args += list(carry)
        aliases = {len(args) - 1: 1}
        if not last:
            aliases[len(args) - 2] = 0
    pair = pl.BlockSpec((key_count, half, width), lambda i, s: (0, i, 0))
    if last:
        in_specs += [pair, pair]
        args += list(extra)
    out_count = key_count if last else key_count + 1
    out_specs = [
        pair if last else acc_spec,
        pl.BlockSpec((width, half), lambda i, s: (s[0], i)),
    ]
    out_shape = [
        jax.ShapeDtypeStruct((out_count, tok_count, width), F32),
        jax.ShapeDtypeStruct((model_width, tok_count), BF16),
    ]
    if last:
        out_specs.append(pl.BlockSpec((4 * key_count, half), lambda i, s: (0, i)))
        out_shape.append(jax.ShapeDtypeStruct((4 * key_count, tok_count), F32))
    return pl.pallas_call(
        functools.partial(forward_kernel, first, last),
        grid_spec=pltpu.PrefetchScalarGridSpec(
            num_scalar_prefetch=1, grid=(HALVES,), in_specs=in_specs, out_specs=out_specs
        ),
        out_shape=out_shape,
        input_output_aliases=aliases,
        compiler_params=params(),
        cost_estimate=cost(
            tok_count * width * width * (key_count + 1), 14 * tok_count * width * (key_count + 1)
        ),
        name="forward_last" if last else "forward_step",
    )(*args)


def back_term(cots, key_ref, value_ref):
    nt = (((1,), (1,)), ((), ()))
    term = lax.dot_general(cots[-1], value_ref[...], nt, preferred_element_type=F32)
    for j in range(key_ref.shape[0]):
        term = term + lax.dot_general(cots[j], key_ref[j], nt, preferred_element_type=F32)
    return term


def cot_kernel(sums_count, model_width, shard_ref, *refs):
    sum_refs = refs[:sums_count]
    val_ref, state_ref, grad_ref, key_ref, value_ref, joined_ref, term_ref = refs[sums_count:]
    key_count, half, width = val_ref.shape
    total = sum_refs[0][...]
    for ref in sum_refs[1:]:
        total = total + ref[...]
    root_width = jnp.sqrt(F32(model_width))
    state_sum, key_sum, cross_dot, out_dot = (
        total[i * key_count : (i + 1) * key_count] for i in range(4)
    )
    state_rs = lax.rsqrt(state_sum / model_width + EPS_NORM)
    key_rs = lax.rsqrt(key_sum / model_width + EPS_NORM)
    scores = cross_dot * state_rs * key_rs / root_width
    gate_val = 1.0 / (1.0 + jnp.exp(-scores))
    dscore = out_dot * gate_val * (1.0 - gate_val)
    lead = key_rs * dscore / root_width
    slope = key_rs * scores / root_width
    rows = jnp.concatenate(
        [lead, state_rs, slope, gate_val, jnp.zeros((128 - 4 * key_count, half), F32)], axis=0
    )
    table = rows.T
    column = lambda kind, j: table[:, kind * key_count + j : kind * key_count + j + 1]
    cots = []
    value_cot = None
    for j in range(key_count):
        inner = state_ref[j].astype(F32) * column(1, j) - val_ref[j] * column(2, j)
        cots.append((column(0, j) * inner).astype(BF16))
        gated = column(3, j) * grad_ref[j].astype(F32)
        value_cot = gated if value_cot is None else value_cot + gated
    cots.append(value_cot.astype(BF16))
    for j in range(key_count + 1):
        joined_ref[:, j * width : (j + 1) * width] = cots[j]
    term_ref[...] = back_term(cots, key_ref, value_ref).astype(BF16)


def cotangents(shard, sums, vals, states, grads, key_weight, value_weight):
    key_count, tok_count, width = vals.shape
    model_width = value_weight.shape[0]
    half = tok_count // HALVES
    pair = pl.BlockSpec((key_count, half, width), lambda i, s: (0, i, 0))
    return pl.pallas_call(
        functools.partial(cot_kernel, len(sums), model_width),
        grid_spec=pltpu.PrefetchScalarGridSpec(
            num_scalar_prefetch=1,
            grid=(HALVES,),
            in_specs=[pl.BlockSpec((4 * key_count, half), lambda i, s: (0, i))] * len(sums)
            + [pair] * 3
            + [
                pl.BlockSpec((key_count, width, width), lambda i, s: (0, s[0], 0)),
                pl.BlockSpec((width, width), lambda i, s: (s[0], 0)),
            ],
            out_specs=[
                pl.BlockSpec((half, (key_count + 1) * width), lambda i, s: (i, 0)),
                pl.BlockSpec((half, width), lambda i, s: (i, 0)),
            ],
        ),
        out_shape=[
            jax.ShapeDtypeStruct((tok_count, (key_count + 1) * width), BF16),
            jax.ShapeDtypeStruct((tok_count, width), BF16),
        ],
        compiler_params=params(),
        cost_estimate=cost(
            tok_count * width * width * (key_count + 1), 14 * tok_count * width * (key_count + 1)
        ),
        name="cotangents",
    )(shard, *sums, vals, states, grads, key_weight, value_weight)


def back_kernel(shard_ref, joined_ref, key_ref, value_ref, term_ref):
    key_count, width, _ = key_ref.shape
    cots = [joined_ref[:, j * width : (j + 1) * width] for j in range(key_count + 1)]
    term_ref[...] = back_term(cots, key_ref, value_ref).astype(BF16)


def back(shards, joined, key_weight, value_weight):
    count = shards.shape[0]
    key_count, _, width = key_weight.shape
    tok_count = joined.shape[0]
    return pl.pallas_call(
        back_kernel,
        grid_spec=pltpu.PrefetchScalarGridSpec(
            num_scalar_prefetch=1,
            grid=(count,),
            in_specs=[
                pl.BlockSpec(joined.shape, lambda i, s: (0, 0)),
                pl.BlockSpec((key_count, width, width), lambda i, s: (0, s[i], 0)),
                pl.BlockSpec((width, width), lambda i, s: (s[i], 0)),
            ],
            out_specs=pl.BlockSpec((None, tok_count, width), lambda i, s: (i, 0, 0)),
        ),
        out_shape=jax.ShapeDtypeStruct((count, tok_count, width), BF16),
        compiler_params=params(),
        cost_estimate=cost(
            count * tok_count * width * width * (key_count + 1),
            count * 10 * tok_count * width * (key_count + 1),
        ),
        name="back",
    )(shards, joined, key_weight, value_weight)


def outer_kernel(block_ref, turned_ref, joined_ref, *refs):
    product = jnp.dot(turned_ref[...], joined_ref[...], preferred_element_type=F32)
    if len(refs) == 1:
        refs[0][...] = product.astype(BF16)
        return
    arrived_ref, first_ref, second_ref = refs
    product = product + arrived_ref[...].astype(F32)
    top = first_ref.shape[0]
    first_ref[...] = product[:top].astype(BF16)
    second_ref[...] = product[top:].astype(BF16)


def outer(block, rows, turned, joined, arrived=None):
    tok_count, columns = joined.shape
    whole = lambda r: pl.BlockSpec((r, columns), lambda i, s: (0, 0))
    in_specs = [pl.BlockSpec((rows, tok_count), lambda i, s: (s[0], 0)), whole(tok_count)]
    args = [block, turned, joined]
    if arrived is None:
        sizes = [rows]
    else:
        in_specs.append(whole(rows))
        args.append(arrived)
        sizes = [rows // 2, rows - rows // 2]
    return pl.pallas_call(
        outer_kernel,
        grid_spec=pltpu.PrefetchScalarGridSpec(
            num_scalar_prefetch=1, grid=(1,), in_specs=in_specs, out_specs=[whole(r) for r in sizes]
        ),
        out_shape=[jax.ShapeDtypeStruct((r, columns), BF16) for r in sizes],
        compiler_params=params(),
        cost_estimate=cost(
            rows * tok_count * columns, 2 * (rows * tok_count + (tok_count + rows) * columns)
        ),
        name="outer" if arrived is None else "outer_add",
    )(*args)


def halve(blocks, bits, axis):
    mine = [blocks[0]]
    for bit in bits:
        far = sorted((rel for rel in blocks if rel & bit), reverse=True)
        arrived = {rel: swap_over(axis, bit, blocks[rel]) for rel in far}
        mine.append(arrived[bit])
        blocks = {
            rel: (blocks[rel].astype(F32) + arrived[rel ^ bit].astype(F32)).astype(BF16)
            if rel
            else None
            for rel in blocks
            if not rel & bit
        }
    return sum(part.astype(F32) for part in mine)


def on_device(
    retrieved,
    branch_states,
    out_grad,
    key_weight,
    value_weight,
    key_grad_acc,
    value_grad_acc,
    row_index,
    row_tier,
    adam_mean,
    adam_second,
):
    tok_count, key_count, width = branch_states.shape
    groups = lax.axis_size("group")
    shards = lax.axis_size("tensor")
    model_width = width * shards
    owned_rows = adam_mean.shape[0]
    half = tok_count // HALVES
    me = lax.axis_index("group")
    place_z = ring_place(lax.axis_index("tensor"), shards)
    one = lambda x: jnp.reshape(x, (1,)).astype(jnp.int32)

    parts = []
    for h in range(HALVES):
        source = retrieved[h * half : (h + 1) * half]
        if parts:
            source, _ = lax.optimization_barrier((source, parts[0]))
        parts.append(jnp.sum(source.astype(F32), axis=1).astype(BF16))
    states = jnp.transpose(branch_states, (1, 0, 2))
    grads = jnp.transpose(out_grad, (1, 0, 2))
    carry = None
    for step in range(shards):
        shard = one(ring_device((place_z - step) % shards, shards))
        extra = (states, grads) if step == shards - 1 else None
        following = (
            [ring_pass(part, "tensor") for part in parts] if step < shards - 1 else None
        )
        carry = forward(shard, parts, key_weight, value_weight, carry, extra)
        parts = following
    vals, turned, sums = carry
    sums = [sums] + others_over("tensor", sums)

    ahead = [ring_device((place_z + step) % shards, shards) for step in range(shards)]
    joined, term = cotangents(
        one(ahead[-1]), sums, vals, states, grads, key_weight, value_weight
    )
    passing = ring_pass(term, "tensor")
    terms = back(jnp.stack(ahead[-2::-1]).astype(jnp.int32), joined, key_weight, value_weight)

    shard_rows = model_width // groups
    order = sorted(range(0, groups, 2), key=lambda rel: (-bin(rel).count("1"), rel))
    sent = {
        rel: swap_over(
            "group", 1, outer(one(me ^ (rel + 1)), shard_rows, turned, joined)[0]
        )
        for rel in order
    }
    near = {
        rel: outer(one(me ^ rel), shard_rows, turned, joined, sent[rel]) for rel in order
    }
    bits = []
    bit = 2
    while bit < groups:
        bits.append(bit)
        bit *= 2
    weight_sum = jnp.concatenate(
        [
            halve({rel: near[rel][0] for rel in order}, bits, "group"),
            halve({rel: near[rel][1] for rel in order}, bits[::-1], "group"),
        ],
        axis=0,
    )
    key_grad = key_grad_acc + jnp.stack(
        [weight_sum[:, j * width : (j + 1) * width] for j in range(key_count)]
    )
    value_grad = value_grad_acc + weight_sum[:, key_count * width :]

    for step in range(shards - 1):
        total = passing.astype(F32) + terms[step].astype(F32)
        if step < shards - 2:
            passing = ring_pass(total.astype(BF16), "tensor")
    memory_cot = total.astype(BF16)

    routed, _ = lax.optimization_barrier((row_index, joined))
    flat_rows = routed.reshape(-1)
    owner_idx = flat_rows // owned_rows
    local_row = flat_rows - owner_idx * owned_rows
    owner_marks = (owner_idx[:, None] == jnp.arange(groups, dtype=jnp.int32)[None, :]).astype(
        jnp.int32
    )
    slot_place = jnp.sum(jnp.cumsum(owner_marks, axis=0) * owner_marks, axis=1) - 1
    slot_index = (owner_idx * CAP + slot_place).reshape(row_index.shape)
    local_row = local_row.reshape(row_index.shape)
    slots = lax.broadcasted_iota(jnp.int32, (groups * CAP, tok_count), 0)
    marks = [slots == slot_index[:, n][None, :] for n in range(row_index.shape[1])]
    pick = sum(mark.astype(BF16) for mark in marks)
    slot_row = sum(
        jnp.sum(jnp.where(mark, local_row[:, n][None, :] + 1, 0), axis=1)
        for n, mark in enumerate(marks)
    )
    incoming_rows = lax.all_to_all(
        slot_row.reshape(groups, CAP), "group", split_axis=0, concat_axis=0, tiled=True
    ).reshape(-1)
    place = (
        lax.broadcasted_iota(jnp.int32, (owned_rows, groups * CAP), 0) + 1 == incoming_rows[None, :]
    ).astype(BF16)

    outgoing = jnp.dot(pick, memory_cot, preferred_element_type=F32).astype(BF16)
    incoming = lax.all_to_all(
        outgoing.reshape(groups, CAP, width), "group", split_axis=0, concat_axis=0, tiled=True
    ).reshape(groups * CAP, width)
    row_grad = jnp.dot(place, incoming, preferred_element_type=F32)
    row_part = jnp.sum(row_grad * row_grad, axis=1)
    row_sum = row_part + sum(others_over("tensor", row_part))
    is_hot = (row_tier == 1)[:, None]
    mean_hot = 0.9 * adam_mean + 0.1 * row_grad
    second_hot = 0.95 * adam_second + 0.05 * row_grad * row_grad
    step_hot = mean_hot / FIRST_BIAS / (jnp.sqrt(second_hot / SECOND_BIAS) + EPS_ADAM)
    step_cold = row_grad * lax.rsqrt(row_sum / model_width + EPS_NORM)[:, None]
    new_mean = jnp.where(is_hot, mean_hot, adam_mean)
    new_second = jnp.where(is_hot, second_hot, adam_second)
    row_step = jnp.where(is_hot, step_hot, step_cold)
    return (key_grad, value_grad, new_mean, new_second, row_step)


def solution(mesh):
    return jax.shard_map(
        on_device,
        mesh=mesh,
        in_specs=(
            P("group", None, "tensor"),
            P("group", None, "tensor"),
            P("group", None, "tensor"),
            P(None, None, "tensor"),
            P(None, "tensor"),
            P(None, "group", "tensor"),
            P("group", "tensor"),
            P("group", None),
            P("group"),
            P("group", "tensor"),
            P("group", "tensor"),
        ),
        out_specs=(
            P(None, "group", "tensor"),
            P("group", "tensor"),
            P("group", "tensor"),
            P("group", "tensor"),
            P("group", "tensor"),
        ),
        check_vma=False,
    )
```

time: 381 us -> 197 us (0.52)
  waiting for transfers between devices: 213 us -> 56.9 us
  Pallas kernels: 0 us -> 54.2 us
  starting transfers between devices: 7.85 us -> 49.4 us
  blocking collectives: 34.9 us -> 0 us
  matrix products: 36.3 us -> 4.28 us
  local copies, waits for them, and re-layouts: 36.4 us -> 10.7 us
  other arithmetic: 37.5 us -> 19.7 us
  between operations: 14 us -> 0.95 us
    reduce_scatter x2 -> x0, waiting for transfers between devices: 128 us -> none  [the longest x1 64.2 us: on_device(): lax.psum_scatter(lax.dot_general(memory, joined, (((0,), (0,)), ((), ()))...]
    all_gather x1 -> x0, waiting for transfers between devices: 57.5 us -> none  [on_device(): memory = lax.all_gather(local_memory, 'tensor', axis=1, tiled=True)]
    pallas_call x0 -> x14, Pallas kernels: none -> 54.2 us  [the longest x4 22.9 us: forward(): pl.pallas_call(functools.partial(forward_kernel, first, last), grid_spec=...]
    ppermute x0 -> x25, waiting for transfers between devices: none -> 47.4 us  [the longest x10 28.2 us: swap_over(): return lax.ppermute(part, axis, [(i, i ^ bit) for i in range(size)])]
    ppermute x0 -> x25, starting transfers between devices: none -> 41.8 us  [the longest x9 24.7 us: ring_pass(): lax.ppermute(part, axis, [(order[i], order[(i + 1) % size]) for i in rang...]
    psum x3 -> x0, blocking collectives: 34.9 us -> none  [the longest x2 24.8 us: on_device(): lax.psum((partial_dots[0], partial_dots[1], partial_dots[2], partial_dots...]
    dot_general x5 -> x2, matrix products: 36.3 us -> 4.28 us  [the longest x1 2.28 us: on_device(): jnp.dot(pick, memory_cot, preferred_element_type=F32).astype(BF16)]
    all_to_all x2, waiting for transfers between devices: 27.6 us -> 9.49 us  [the longest x1 9.49 us: on_device(): lax.all_to_all(outgoing.reshape(groups, CAP, width), 'group', split_axis=...]
  transfers between devices with their start and end apart: 5 -> 27, of which waited for: 4 -> 12; matrix products, arithmetic and copies ran while one was open for 14% -> 7% of each run, Pallas kernels for 0% -> 18%
where the time goes in v1:
time: 197 us; the launch traced here: 196 us
  waiting for transfers between devices  56.9 us (29%)
  Pallas kernels  54.2 us (28%)
  starting transfers between devices  49.4 us (25%)
  other arithmetic  19.7 us (10%)
  local copies, waits for them, and re-layouts  10.7 us (5%)
  matrix products  4.28 us (2%)
    ppermute x10, waiting for transfers between devices, swap_over(): return lax.ppermute(part, axis, [(i, i ^ bit) for i in range(size)])  28.2 us
    ppermute x9, starting transfers between devices, ring_pass(): lax.ppermute(part, axis, [(order[i], order[(i + 1) % size]) for i in rang...  24.7 us
    pallas_call x4, Pallas kernels, forward(): pl.pallas_call(functools.partial(forward_kernel, first, last), grid_spec=...  22.9 us
    pallas_call x8, Pallas kernels, outer(): pl.pallas_call(outer_kernel, grid_spec=pltpu.PrefetchScalarGridSpec(num_s...  17.4 us
    ppermute x9, waiting for transfers between devices, ring_pass(): lax.ppermute(part, axis, [(order[i], order[(i + 1) % size]) for i in rang...  16 us
    all_to_all x1, waiting for transfers between devices, on_device(): lax.all_to_all(outgoing.reshape(groups, CAP, width), 'group', split_axis=...  9.49 us
    unnamed x44, local copies, waits for them, and re-layouts  9.33 us
    ppermute x6, starting transfers between devices, others_over(): lax.ppermute(part, axis, [(i, (i + step) % size) for i in range(size)])  8.87 us
  transfers between devices with their start and end apart: 27, of which 12 were waited for; matrix products, arithmetic and copies ran while one was open for 7% of the time, Pallas kernels for 18%

profile of v1, /device:TPU:0, one launch (start us, length us, event | category | flops | bytes accessed | tf_op | source)
XLA Modules:
  0.0 196.1 jit_solution(11167069317401201302)
XLA Ops:
  0.6 3.5 %fusion.30 = (bf16[256,2,640]{2,1,0:T(2,128)(2,1)S(1)}, bf16[256,640]{1,0:T(8,128)(2,1)S(1)}) fusion(bf16[512,2,640]{2,1,0:T(2,128)(2,1)} %param.11), kind=kLoop, calls=%fused_computation.83 | loop fusion | flops 163840 | bytes 2293760 | tf_op jit(solution)/shard_map/slice | solution.py:338
  5.8 4.1 %collective-permute-start.3 = (bf16[256,640]{1,0:T(8,128)(2,1)S(1)}, bf16[256,640]{1,0:T(8,128)(2,1)}, u32[]{:S(2)}, u32[]{:S(2)}) collective-permute-start(bf16[256,640]{1,0:T(8,128)(2,1)S(1)} %reduce_sum.61.refs_1_), channel_id=1, source_target_pairs={{0,2},{2,3},{3,1},{1,0},{4,6},{6,7},{7,5},{5,4},{8,10},{10,11},{11... | collective-permute-start | bytes 983048 | tf_op jit(solution)/shard_map/ppermute | solution.py:42
  11.5 5.3 %forward_step.3 = (f32[3,512,640]{2,1,0:T(8,128)}, bf16[2560,512]{1,0:T(8,128)(2,1)S(1)}) custom-call(s32[1]{0:T(128)} %bitcast.4.shard_ref, bf16[256,640]{1,0:T(8,128)(2,1)S(1)} %get-tuple-element.56.refs_0_, bf16[256,640]{1,0:T(8,128)(2,1)S(1)} %reduce_sum.61.refs_1_, bf16[2,2560,640]{2,1,0:T(8,128)(2,1)} %key_ref.1, bf16[2560,640]{1,0:T(8,128)(2,1)} %value_ref.1), custom_call_target="tpu_custom_call" | custom-call | flops 1258291200 | bytes 13762560 | tf_op jit(solution)/shard_map/forward_step/pallas_call | solution.py:136
  18.0 3.5 %collective-permute-start.4 = (bf16[256,640]{1,0:T(8,128)(2,1)}, bf16[256,640]{1,0:T(8,128)(2,1)S(1)}, u32[]{:S(2)}, u32[]{:S(2)}) collective-permute-start(bf16[256,640]{1,0:T(8,128)(2,1)} %collective-permute-done.3.refs_1_), channel_id=1, source_target_pairs={{0,2},{2,3},{3,1},{1,0},{4,6},{6,7},{7,5},{5,4},{8,10},{10,11},{11... | collective-permute-start | bytes 983048 | tf_op jit(solution)/shard_map/ppermute | solution.py:42
  21.5 3.5 %collective-permute-done.refs_0_ = bf16[256,640]{1,0:T(8,128)(2,1)} collective-permute-done((bf16[256,640]{1,0:T(8,128)(2,1)S(1)}, bf16[256,640]{1,0:T(8,128)(2,1)}, u32[]{:S(2)}, u32[]{:S(2)}) %collective-permute-start) | collective-permute-done | bytes 327712 | tf_op jit(solution)/shard_map/ppermute | solution.py:42
  25.1 3.5 %collective-permute-start.1 = (bf16[256,640]{1,0:T(8,128)(2,1)}, bf16[256,640]{1,0:T(8,128)(2,1)S(1)}, u32[]{:S(2)}, u32[]{:S(2)}) collective-permute-start(bf16[256,640]{1,0:T(8,128)(2,1)} %collective-permute-done.refs_0_), channel_id=1, source_target_pairs={{0,2},{2,3},{3,1},{1,0},{4,6},{6,7},{7,5},{5,4},{8,10},{10,11},{11... | collective-permute-start | bytes 983048 | tf_op jit(solution)/shard_map/ppermute | solution.py:42
  28.9 3.3 %collective-permute-done.4.refs_1_ = bf16[256,640]{1,0:T(8,128)(2,1)S(1)} collective-permute-done((bf16[256,640]{1,0:T(8,128)(2,1)}, bf16[256,640]{1,0:T(8,128)(2,1)S(1)}, u32[]{:S(2)}, u32[]{:S(2)}) %collective-permute-start.4) | collective-permute-done | bytes 327712 | tf_op jit(solution)/shard_map/ppermute | solution.py:42
  32.2 3.3 %collective-permute-start.5 = (bf16[256,640]{1,0:T(8,128)(2,1)S(1)}, bf16[256,640]{1,0:T(8,128)(2,1)S(1)}, u32[]{:S(2)}, u32[]{:S(2)}) collective-permute-start(bf16[256,640]{1,0:T(8,128)(2,1)S(1)} %collective-permute-done.4.refs_1_), channel_id=1, source_target_pairs={{0,2},{2,3},{3,1},{1,0},{4,6},{6,7},{7,5},{5,4},{8,10},{10,11},{11... | collective-permute-start | bytes 983048 | tf_op jit(solution)/shard_map/ppermute | solution.py:42
  35.5 3.7 %collective-permute-done.1.refs_0_ = bf16[256,640]{1,0:T(8,128)(2,1)S(1)} collective-permute-done((bf16[256,640]{1,0:T(8,128)(2,1)}, bf16[256,640]{1,0:T(8,128)(2,1)S(1)}, u32[]{:S(2)}, u32[]{:S(2)}) %collective-permute-start.1) | collective-permute-done | bytes 327712 | tf_op jit(solution)/shard_map/ppermute | solution.py:42
  39.2 3.3 %collective-permute-start.2 = (bf16[256,640]{1,0:T(8,128)(2,1)S(1)}, bf16[256,640]{1,0:T(8,128)(2,1)S(1)}, u32[]{:S(2)}, u32[]{:S(2)}) collective-permute-start(bf16[256,640]{1,0:T(8,128)(2,1)S(1)} %collective-permute-done.1.refs_0_), channel_id=1, source_target_pairs={{0,2},{2,3},{3,1},{1,0},{4,6},{6,7},{7,5},{5,4},{8,10},{10,11},{11... | collective-permute-start | bytes 983048 | tf_op jit(solution)/shard_map/ppermute | solution.py:42
  42.5 5.9 %forward_step.4 = (f32[3,512,640]{2,1,0:T(8,128)}, bf16[2560,512]{1,0:T(8,128)(2,1)S(1)}) custom-call(s32[1]{0:T(128)} %bitcast.3.shard_ref, bf16[256,640]{1,0:T(8,128)(2,1)} %collective-permute-done.refs_0_, bf16[256,640]{1,0:T(8,128)(2,1)} %collective-permute-done.3.refs_1_, ...), custom_call_target="tpu_custom_call", output_to_operand_aliasing={{1}: (6, {}), {0}: (5, {})} | custom-call | flops 1258291200 | bytes 13762560 | tf_op jit(solution)/shard_map/forward_step/pallas_call | solution.py:136
  48.4 5.7 %forward_step.5 = (f32[3,512,640]{2,1,0:T(8,128)}, bf16[2560,512]{1,0:T(8,128)(2,1)S(1)}) custom-call(s32[1]{0:T(128)} %bitcast.2.shard_ref, bf16[256,640]{1,0:T(8,128)(2,1)S(1)} %collective-permute-done.1.refs_0_, bf16[256,640]{1,0:T(8,128)(2,1)S(1)} %collective-permute-done.4.refs_1_, ...), custom_call_target="tpu_custom_call", output_to_operand_aliasing={{1}: (6, {}), {0}: (5, {})} | custom-call | flops 1258291200 | bytes 13762560 | tf_op jit(solution)/shard_map/forward_step/pallas_call | solution.py:136
  55.7 6.0 %forward_last.1 = (f32[2,512,640]{2,1,0:T(8,128)S(1)}, bf16[2560,512]{1,0:T(8,128)(2,1)}, f32[8,512]{1,0:T(8,128)S(1)}) custom-call(s32[1]{0:T(128)} %bitcast.1.shard_ref, bf16[256,640]{1,0:T(8,128)(2,1)S(1)} %collective-permute-done.2.refs_0_, bf16[256,640]{1,0:T(8,128)(2,1)S(1)} %collective-permute-done.5.refs_1_, ...), custom_call_target="tpu_custom_call", output_to_operand_aliasing={{1}: (6, {})} | custom-call | flops 1258291200 | bytes 13762560 | tf_op jit(solution)/shard_map/forward_last/pallas_call | solution.py:136
  71.8 5.5 %cotangents.1 = (bf16[512,1920]{1,0:T(8,128)(2,1)S(1)}, bf16[512,640]{1,0:T(8,128)(2,1)}) custom-call(s32[1]{0:T(128)} %bitcast.7.shard_ref, f32[8,512]{1,0:T(8,128)S(1)} %get-tuple-element.34.refs_0_, f32[8,512]{1,0:T(8,128)S(1)} %collective-permute-done.6.refs_1_, f32[8,512]{1,0:T(8,128)S(1)} %collective-permute-done.7.refs_2_, ...), custom_call_target="tpu_custom_call" | custom-call | flops 1258291200 | bytes 13762560 | tf_op jit(solution)/shard_map/cotangents/pallas_call | solution.py:200
  79.2 2.3 %reduce-window.6 = s32[8,8,128]{2,1,0:T(8,128)S(1)} reduce-window(s32[8,8,128]{2,1,0:T(8,128)S(1)} %fusion.25, s32[]{:T(128)} %constant.118.clone.1), window={size=1x1x128 pad=0_0x0_0x127_0}, to_apply=%region_2.3 | reduce-window | flops 1040384 | bytes 65540 | tf_op jit(solution)/shard_map/reduce-window
  83.9 8.3 %back.1 = bf16[3,512,640]{2,1,0:T(8,128)(2,1)S(1)} custom-call(s32[3]{0:T(128)S(1)} %pad_add_fusion.shard_ref, bf16[512,1920]{1,0:T(8,128)(2,1)S(1)} %copy-done.3, bf16[2,2560,640]{2,1,0:T(8,128)(2,1)} %key_ref.1, bf16[2560,640]{1,0:T(8,128)(2,1)} %value_ref.1), custom_call_target="tpu_custom_call" | custom-call | flops 3774873600 | bytes 29491200 | tf_op jit(solution)/shard_map/back/pallas_call | solution.py:238
  97.0 2.0 outer.4
  101.4 4.2 %collective-permute-done.19 = bf16[512,640]{1,0:T(8,128)(2,1)S(1)} collective-permute-done((bf16[512,640]{1,0:T(8,128)(2,1)}, bf16[512,640]{1,0:T(8,128)(2,1)S(1)}, u32[]{:S(2)}, u32[]{:S(2)}) %collective-permute-start.19) | collective-permute-done | bytes 655392 | tf_op jit(solution)/shard_map/ppermute | solution.py:42
  108.6 2.8 %outer_add.7 = (bf16[160,1920]{1,0:T(8,128)(2,1)}, bf16[160,1920]{1,0:T(8,128)(2,1)S(1)}) custom-call(s32[1]{0:T(128)} %bitcast.13.block_ref, bf16[2560,512]{1,0:T(8,128)(2,1)} %get-tuple-element.33.turned_ref, bf16[512,1920]{1,0:T(8,128)(2,1)S(1)} %copy-done.3, bf16[320,1920]{1,0:T(8,128)(2,1)S(1)} %collective-permute-done.13.refs_0_), custom_call_target="tpu_custom_call" | custom-call | flops 629145600 | bytes 3522560 | tf_op jit(solution)/shard_map/outer_add/pallas_call | solution.py:283
  114.9 3.3 %all-to-all-start = ((s32[8,1,128]{2,1,0:T(1,128)}), s32[8,1,128]{2,1,0:T(1,128)S(1)}, u32[]{:S(2)}, u32[]{:S(2)}) async-start(s32[8,1,128]{2,1,0:T(1,128)} %bitcast.22), calls=%async_computation | async-start | bytes 8192 | tf_op jit(solution)/shard_map/all_to_all | solution.py:414
  118.2 2.6 %outer_add.5 = (bf16[160,1920]{1,0:T(8,128)(2,1)}, bf16[160,1920]{1,0:T(8,128)(2,1)S(1)}) custom-call(s32[1]{0:T(128)} %bitcast.9.block_ref, bf16[2560,512]{1,0:T(8,128)(2,1)} %get-tuple-element.33.turned_ref, bf16[512,1920]{1,0:T(8,128)(2,1)S(1)} %copy-done.4, bf16[320,1920]{1,0:T(8,128)(2,1)S(1)} %collective-permute-done.10.refs_0_), custom_call_target="tpu_custom_call" | custom-call | flops 629145600 | bytes 3522560 | tf_op jit(solution)/shard_map/outer_add/pallas_call | solution.py:283
  122.7 3.1 %outer_add.6 = (bf16[160,1920]{1,0:T(8,128)(2,1)S(1)}, bf16[160,1920]{1,0:T(8,128)(2,1)}) custom-call(s32[1]{0:T(128)} %bitcast.11.block_ref, bf16[2560,512]{1,0:T(8,128)(2,1)} %get-tuple-element.33.turned_ref, bf16[512,1920]{1,0:T(8,128)(2,1)S(1)} %copy-done.4, bf16[320,1920]{1,0:T(8,128)(2,1)} %collective-permute-done.12.refs_0_), custom_call_target="tpu_custom_call" | custom-call | flops 629145600 | bytes 3522560 | tf_op jit(solution)/shard_map/outer_add/pallas_call | solution.py:283
  127.9 2.4 %outer_add.4 = (bf16[160,1920]{1,0:T(8,128)(2,1)S(1)}, bf16[160,1920]{1,0:T(8,128)(2,1)S(1)}) custom-call(s32[1]{0:T(128)} %bitcast.block_ref, bf16[2560,512]{1,0:T(8,128)(2,1)} %get-tuple-element.33.turned_ref, bf16[512,1920]{1,0:T(8,128)(2,1)S(1)} %copy-done.4, bf16[320,1920]{1,0:T(8,128)(2,1)} %collective-permute-done.9.refs_0_), custom_call_target="tpu_custom_call" | custom-call | flops 629145600 | bytes 3522560 | tf_op jit(solution)/shard_map/outer_add/pallas_call | solution.py:283
  131.5 2.1 %collective-permute-start.21 = (bf16[512,640]{1,0:T(8,128)(2,1)S(1)}, bf16[512,640]{1,0:T(8,128)(2,1)S(1)}, u32[]{:S(2)}, u32[]{:S(2)}) collective-permute-start(bf16[512,640]{1,0:T(8,128)(2,1)S(1)} %fusion.3), channel_id=1, source_target_pairs={{0,2},{2,3},{3,1},{1,0},{4,6},{6,7},{7,5},{5,4},{8,10},{10,11},{11... | collective-permute-start | bytes 1966088 | tf_op jit(solution)/shard_map/ppermute | solution.py:42
  136.4 19.5 %collective-permute-done.17 = bf16[160,1920]{1,0:T(8,128)(2,1)S(1)} collective-permute-done((bf16[160,1920]{1,0:T(8,128)(2,1)S(1)}, bf16[160,1920]{1,0:T(8,128)(2,1)S(1)}, u32[]{:S(2)}, u32[]{:S(2)}) %collective-permute-start.17) | collective-permute-done | bytes 614432 | tf_op jit(solution)/shard_map/ppermute | solution.py:55
  156.3 2.3 %convolution_convert_fusion = bf16[1024,640]{1,0:T(8,128)(2,1)} fusion(s32[512]{0:T(512)S(1)} %bitcast.67, s32[512]{0:T(512)S(1)} %bitcast.65, bf16[512,640]{1,0:T(8,128)(2,1)S(1)} %collective-permute-done.21, bf16[3,512,640]{2,1,0:T(8,128)(2,1)S(1)} %copy-done.11), kind=kOutput, calls=%fused_computation.11 | convolution fusion | flops 677249024 | bytes 2625536 | tf_op jit(solution)/shard_map/dot_general | solution.py:421
  158.6 4.3 %all-to-all-start.1 = ((bf16[8,128,640]{2,1,0:T(8,128)(2,1)}), bf16[8,128,640]{2,1,0:T(8,128)(2,1)}, u32[]{:S(2)}, u32[]{:S(2)}) async-start(bf16[8,128,640]{2,1,0:T(8,128)(2,1)} %bitcast.29), calls=%async_computation.1 | async-start | bytes 2621440 | tf_op jit(solution)/shard_map/all_to_all | solution.py:422
  162.9 6.4 %collective-permute-done.15 = bf16[160,1920]{1,0:T(8,128)(2,1)} collective-permute-done((bf16[160,1920]{1,0:T(8,128)(2,1)S(1)}, bf16[160,1920]{1,0:T(8,128)(2,1)}, u32[]{:S(2)}, u32[]{:S(2)}) %collective-permute-start.15) | collective-permute-done | bytes 614432 | tf_op jit(solution)/shard_map/ppermute | solution.py:55
  170.8 2.2 %collective-permute-done.18 = bf16[160,1920]{1,0:T(8,128)(2,1)S(1)} collective-permute-done((bf16[160,1920]{1,0:T(8,128)(2,1)S(1)}, bf16[160,1920]{1,0:T(8,128)(2,1)S(1)}, u32[]{:S(2)}, u32[]{:S(2)}) %collective-permute-start.18) | collective-permute-done | bytes 614432 | tf_op jit(solution)/shard_map/ppermute | solution.py:55
  175.4 9.5 %all-to-all-done.1 = bf16[8,128,640]{2,1,0:T(8,128)(2,1)} async-done(((bf16[8,128,640]{2,1,0:T(8,128)(2,1)}), bf16[8,128,640]{2,1,0:T(8,128)(2,1)}, u32[]{:S(2)}, u32[]{:S(2)}) %all-to-all-start.1) | async-done | bytes 1310752 | tf_op jit(solution)/shard_map/all_to_all | solution.py:422
  184.9 2.0 %multiply_reduce_fusion = (f32[256]{0:T(256)S(1)}, f32[256,640]{1,0:T(8,128)S(1)}) fusion(bf16[1024,640]{1,0:T(8,128)(2,1)} %bitcast.30, s32[1024]{0:T(1024)S(1)} %bitcast.70, s32[256]{0:T(256)S(1)} %iota_add_fusion), kind=kOutput, calls=%fused_computation.41 | convolution fusion | flops 336133888 | bytes 1972224 | tf_op jit(solution)/shard_map/dot_general | solution.py:425
  187.8 2.9 %collective-permute-start.23 = (f32[256]{0:T(256)S(1)}, f32[256]{0:T(256)S(1)}, u32[]{:S(2)}, u32[]{:S(2)}) collective-permute-start(f32[256]{0:T(256)S(1)} %get-tuple-element.61), channel_id=1, source_target_pairs={{0,2},{1,3},{2,0},{3,1},{4,6},{5,7},{6,4},{7,5},{8,10},{9,11},{10,... | collective-permute-start | bytes 3080 | tf_op jit(solution)/shard_map/ppermute | solution.py:48
  (119 shorter events, 53.0 us)
Async XLA Ops:
  5.8 12.2 %collective-permute-start.3 = (bf16[256,640]{1,0:T(8,128)(2,1)S(1)}, bf16[256,640]{1,0:T(8,128)(2,1)}, u32[]{:S(2)}, u32[]{:S(2)}) collective-permute-start(bf16[256,640]{1,0:T(8,128)(2,1)S(1)} %reduce_sum.61.refs_1_), channel_id=1, source_target_pairs={{0,2},{2,3},{3,1},{1,0},{4,6},{6,7},{7,5},{5,4},{8,10},{10,11},{11... | collective-permute-start | bytes 983048 | tf_op jit(solution)/shard_map/ppermute | solution.py:42
  9.9 15.1 %collective-permute-start = (bf16[256,640]{1,0:T(8,128)(2,1)S(1)}, bf16[256,640]{1,0:T(8,128)(2,1)}, u32[]{:S(2)}, u32[]{:S(2)}) collective-permute-start(bf16[256,640]{1,0:T(8,128)(2,1)S(1)} %get-tuple-element.56.refs_0_), channel_id=1, source_target_pairs={{0,2},{2,3},{3,1},{1,0},{4,6},{6,7},{7,5},{5,4},{8,10},{10,11},{11... | collective-permute-start | bytes 983048 | tf_op jit(solution)/shard_map/ppermute | solution.py:42
  11.5 17.0 %copy-start.15 = (bf16[512,2,640]{2,1,0:T(2,128)(2,1)S(1)}, bf16[512,2,640]{2,1,0:T(2,128)(2,1)}, u32[]{:S(2)}) copy-start(bf16[512,2,640]{2,1,0:T(2,128)(2,1)} %param.13) | copy-start | bytes 3932164
  11.5 17.0 %copy-start.16 = (bf16[512,2,640]{2,1,0:T(2,128)(2,1)S(1)}, bf16[512,2,640]{2,1,0:T(2,128)(2,1)}, u32[]{:S(2)}) copy-start(bf16[512,2,640]{2,1,0:T(2,128)(2,1)} %param.12) | copy-start | bytes 3932164
  18.0 14.1 %collective-permute-start.4 = (bf16[256,640]{1,0:T(8,128)(2,1)}, bf16[256,640]{1,0:T(8,128)(2,1)S(1)}, u32[]{:S(2)}, u32[]{:S(2)}) collective-permute-start(bf16[256,640]{1,0:T(8,128)(2,1)} %collective-permute-done.3.refs_1_), channel_id=1, source_target_pairs={{0,2},{2,3},{3,1},{1,0},{4,6},{6,7},{7,5},{5,4},{8,10},{10,11},{11... | collective-permute-start | bytes 983048 | tf_op jit(solution)/shard_map/ppermute | solution.py:42
  25.1 14.1 %collective-permute-start.1 = (bf16[256,640]{1,0:T(8,128)(2,1)}, bf16[256,640]{1,0:T(8,128)(2,1)S(1)}, u32[]{:S(2)}, u32[]{:S(2)}) collective-permute-start(bf16[256,640]{1,0:T(8,128)(2,1)} %collective-permute-done.refs_0_), channel_id=1, source_target_pairs={{0,2},{2,3},{3,1},{1,0},{4,6},{6,7},{7,5},{5,4},{8,10},{10,11},{11... | collective-permute-start | bytes 983048 | tf_op jit(solution)/shard_map/ppermute | solution.py:42
  28.9 26.7 %copy-start.5 = (bf16[2,512,640]{2,1,0:T(8,128)(2,1)}, bf16[2,512,640]{2,1,0:T(8,128)(2,1)S(1)}, u32[]{:S(2)}) copy-start(bf16[2,512,640]{2,1,0:T(8,128)(2,1)S(1)} %get-tuple-element.63.refs_7_.refs_6_) | copy-start | bytes 3932164
  28.9 26.7 %copy-start.7 = (bf16[2,512,640]{2,1,0:T(8,128)(2,1)}, bf16[2,512,640]{2,1,0:T(8,128)(2,1)S(1)}, u32[]{:S(2)}) copy-start(bf16[2,512,640]{2,1,0:T(8,128)(2,1)S(1)} %get-tuple-element.64.refs_6_.refs_5_) | copy-start | bytes 3932164
  32.2 23.4 %collective-permute-start.5 = (bf16[256,640]{1,0:T(8,128)(2,1)S(1)}, bf16[256,640]{1,0:T(8,128)(2,1)S(1)}, u32[]{:S(2)}, u32[]{:S(2)}) collective-permute-start(bf16[256,640]{1,0:T(8,128)(2,1)S(1)} %collective-permute-done.4.refs_1_), channel_id=1, source_target_pairs={{0,2},{2,3},{3,1},{1,0},{4,6},{6,7},{7,5},{5,4},{8,10},{10,11},{11... | collective-permute-start | bytes 983048 | tf_op jit(solution)/shard_map/ppermute | solution.py:42
  39.2 16.4 %collective-permute-start.2 = (bf16[256,640]{1,0:T(8,128)(2,1)S(1)}, bf16[256,640]{1,0:T(8,128)(2,1)S(1)}, u32[]{:S(2)}, u32[]{:S(2)}) collective-permute-start(bf16[256,640]{1,0:T(8,128)(2,1)S(1)} %collective-permute-done.1.refs_0_), channel_id=1, source_target_pairs={{0,2},{2,3},{3,1},{1,0},{4,6},{6,7},{7,5},{5,4},{8,10},{10,11},{11... | collective-permute-start | bytes 983048 | tf_op jit(solution)/shard_map/ppermute | solution.py:42
  63.1 5.5 %collective-permute-start.6 = (f32[8,512]{1,0:T(8,128)S(1)}, f32[8,512]{1,0:T(8,128)S(1)}, u32[]{:S(2)}, u32[]{:S(2)}) collective-permute-start(f32[8,512]{1,0:T(8,128)S(1)} %get-tuple-element.34.refs_0_), channel_id=1, source_target_pairs={{0,1},{1,2},{2,3},{3,0},{4,5},{5,6},{6,7},{7,4},{8,9},{9,10},{10,1... | collective-permute-start | bytes 49160 | tf_op jit(solution)/shard_map/ppermute | solution.py:48
  63.1 5.5 %collective-permute-start.7 = (f32[8,512]{1,0:T(8,128)S(1)}, f32[8,512]{1,0:T(8,128)S(1)}, u32[]{:S(2)}, u32[]{:S(2)}) collective-permute-start(f32[8,512]{1,0:T(8,128)S(1)} %get-tuple-element.34.refs_0_), channel_id=1, source_target_pairs={{0,2},{1,3},{2,0},{3,1},{4,6},{5,7},{6,4},{7,5},{8,10},{9,11},{10,... | collective-permute-start | bytes 49160 | tf_op jit(solution)/shard_map/ppermute | solution.py:48
  65.0 4.2 %collective-permute-start.8 = (f32[8,512]{1,0:T(8,128)S(1)}, f32[8,512]{1,0:T(8,128)S(1)}, u32[]{:S(2)}, u32[]{:S(2)}) collective-permute-start(f32[8,512]{1,0:T(8,128)S(1)} %get-tuple-element.34.refs_0_), channel_id=1, source_target_pairs={{0,3},{1,0},{2,1},{3,2},{4,7},{5,4},{6,5},{7,6},{8,11},{9,8},{10,9... | collective-permute-start | bytes 49160 | tf_op jit(solution)/shard_map/ppermute | solution.py:48
  92.2 13.4 %collective-permute-start.19 = (bf16[512,640]{1,0:T(8,128)(2,1)}, bf16[512,640]{1,0:T(8,128)(2,1)S(1)}, u32[]{:S(2)}, u32[]{:S(2)}) collective-permute-start(bf16[512,640]{1,0:T(8,128)(2,1)} %get-tuple-element.46), channel_id=1, source_target_pairs={{0,2},{2,3},{3,1},{1,0},{4,6},{6,7},{7,5},{5,4},{8,10},{10,11},{11... | collective-permute-start | bytes 1966088 | tf_op jit(solution)/shard_map/ppermute | solution.py:42
  95.6 27.1 %collective-permute-start.12 = (bf16[320,1920]{1,0:T(8,128)(2,1)}, bf16[320,1920]{1,0:T(8,128)(2,1)}, u32[]{:S(2)}, u32[]{:S(2)}) collective-permute-start(bf16[320,1920]{1,0:T(8,128)(2,1)} %outer.6), channel_id=1, source_target_pairs={{0,4},{4,0},{8,12},{12,8},{16,20},{20,16},{24,28},{28,24},{1,5},{5... | collective-permute-start | bytes 3686408 | tf_op jit(solution)/shard_map/ppermute | solution.py:55
  96.4 12.2 %collective-permute-start.13 = (bf16[320,1920]{1,0:T(8,128)(2,1)S(1)}, bf16[320,1920]{1,0:T(8,128)(2,1)S(1)}, u32[]{:S(2)}, u32[]{:S(2)}) collective-permute-start(bf16[320,1920]{1,0:T(8,128)(2,1)S(1)} %outer.7), channel_id=1, source_target_pairs={{0,4},{4,0},{8,12},{12,8},{16,20},{20,16},{24,28},{28,24},{1,5},{5... | collective-permute-start | bytes 3686408 | tf_op jit(solution)/shard_map/ppermute | solution.py:55
  99.0 28.4 %collective-permute-start.9 = (bf16[320,1920]{1,0:T(8,128)(2,1)}, bf16[320,1920]{1,0:T(8,128)(2,1)}, u32[]{:S(2)}, u32[]{:S(2)}) collective-permute-start(bf16[320,1920]{1,0:T(8,128)(2,1)} %outer.4), channel_id=1, source_target_pairs={{0,4},{4,0},{8,12},{12,8},{16,20},{20,16},{24,28},{28,24},{1,5},{5... | collective-permute-start | bytes 3686408 | tf_op jit(solution)/shard_map/ppermute | solution.py:55
  100.8 17.3 %collective-permute-start.10 = (bf16[320,1920]{1,0:T(8,128)(2,1)}, bf16[320,1920]{1,0:T(8,128)(2,1)S(1)}, u32[]{:S(2)}, u32[]{:S(2)}) collective-permute-start(bf16[320,1920]{1,0:T(8,128)(2,1)} %outer.5), channel_id=1, source_target_pairs={{0,4},{4,0},{8,12},{12,8},{16,20},{20,16},{24,28},{28,24},{1,5},{5... | collective-permute-start | bytes 3686408 | tf_op jit(solution)/shard_map/ppermute | solution.py:55
  106.6 23.7 %collective-permute-start.20 = (bf16[512,640]{1,0:T(8,128)(2,1)}, bf16[512,640]{1,0:T(8,128)(2,1)}, u32[]{:S(2)}, u32[]{:S(2)}) collective-permute-start(bf16[512,640]{1,0:T(8,128)(2,1)} %fusion.4), channel_id=1, source_target_pairs={{0,2},{2,3},{3,1},{1,0},{4,6},{6,7},{7,5},{5,4},{8,10},{10,11},{11... | collective-permute-start | bytes 1966088 | tf_op jit(solution)/shard_map/ppermute | solution.py:42
  112.2 21.5 %collective-permute-start.14 = (bf16[160,1920]{1,0:T(8,128)(2,1)}, bf16[160,1920]{1,0:T(8,128)(2,1)}, u32[]{:S(2)}, u32[]{:S(2)}) collective-permute-start(bf16[160,1920]{1,0:T(8,128)(2,1)} %get-tuple-element.40), channel_id=1, source_target_pairs={{0,8},{4,12},{8,0},{12,4},{16,24},{20,28},{24,16},{28,20},{1,9},{5... | collective-permute-start | bytes 1843208 | tf_op jit(solution)/shard_map/ppermute | solution.py:55
  114.9 43.7 %all-to-all-start = ((s32[8,1,128]{2,1,0:T(1,128)}), s32[8,1,128]{2,1,0:T(1,128)S(1)}, u32[]{:S(2)}, u32[]{:S(2)}) async-start(s32[8,1,128]{2,1,0:T(1,128)} %bitcast.22), calls=%async_computation | async-start | bytes 8192 | tf_op jit(solution)/shard_map/all_to_all | solution.py:414
  120.8 42.1 %collective-permute-start.11 = (bf16[160,1920]{1,0:T(8,128)(2,1)}, bf16[160,1920]{1,0:T(8,128)(2,1)}, u32[]{:S(2)}, u32[]{:S(2)}) collective-permute-start(bf16[160,1920]{1,0:T(8,128)(2,1)} %get-tuple-element.38), channel_id=1, source_target_pairs={{0,8},{4,12},{8,0},{12,4},{16,24},{20,28},{24,16},{28,20},{1,9},{5... | collective-permute-start | bytes 1843208 | tf_op jit(solution)/shard_map/ppermute | solution.py:55
  125.9 44.9 %collective-permute-start.16 = (bf16[160,1920]{1,0:T(8,128)(2,1)}, bf16[160,1920]{1,0:T(8,128)(2,1)}, u32[]{:S(2)}, u32[]{:S(2)}) collective-permute-start(bf16[160,1920]{1,0:T(8,128)(2,1)} %get-tuple-element.42), channel_id=1, source_target_pairs={{0,16},{4,20},{8,24},{12,28},{16,0},{20,4},{24,8},{28,12},{1,17},{... | collective-permute-start | bytes 1843208 | tf_op jit(solution)/shard_map/ppermute | solution.py:55
  127.4 28.6 %collective-permute-start.17 = (bf16[160,1920]{1,0:T(8,128)(2,1)S(1)}, bf16[160,1920]{1,0:T(8,128)(2,1)S(1)}, u32[]{:S(2)}, u32[]{:S(2)}) collective-permute-start(bf16[160,1920]{1,0:T(8,128)(2,1)S(1)} %copy-done.13), channel_id=1, source_target_pairs={{0,16},{4,20},{8,24},{12,28},{16,0},{20,4},{24,8},{28,12},{1,17},{... | collective-permute-start | bytes 1843208 | tf_op jit(solution)/shard_map/ppermute | solution.py:55
  131.5 24.8 %collective-permute-start.21 = (bf16[512,640]{1,0:T(8,128)(2,1)S(1)}, bf16[512,640]{1,0:T(8,128)(2,1)S(1)}, u32[]{:S(2)}, u32[]{:S(2)}) collective-permute-start(bf16[512,640]{1,0:T(8,128)(2,1)S(1)} %fusion.3), channel_id=1, source_target_pairs={{0,2},{2,3},{3,1},{1,0},{4,6},{6,7},{7,5},{5,4},{8,10},{10,11},{11... | collective-permute-start | bytes 1966088 | tf_op jit(solution)/shard_map/ppermute | solution.py:42
  134.9 34.4 %collective-permute-start.15 = (bf16[160,1920]{1,0:T(8,128)(2,1)S(1)}, bf16[160,1920]{1,0:T(8,128)(2,1)}, u32[]{:S(2)}, u32[]{:S(2)}) collective-permute-start(bf16[160,1920]{1,0:T(8,128)(2,1)S(1)} %add_convert_fusion.1), channel_id=1, source_target_pairs={{0,16},{4,20},{8,24},{12,28},{16,0},{20,4},{24,8},{28,12},{1,17},{... | collective-permute-start | bytes 1843208 | tf_op jit(solution)/shard_map/ppermute | solution.py:55
  156.1 16.9 %collective-permute-start.18 = (bf16[160,1920]{1,0:T(8,128)(2,1)S(1)}, bf16[160,1920]{1,0:T(8,128)(2,1)S(1)}, u32[]{:S(2)}, u32[]{:S(2)}) collective-permute-start(bf16[160,1920]{1,0:T(8,128)(2,1)S(1)} %add_convert_fusion), channel_id=1, source_target_pairs={{0,8},{4,12},{8,0},{12,4},{16,24},{20,28},{24,16},{28,20},{1,9},{5... | collective-permute-start | bytes 1843208 | tf_op jit(solution)/shard_map/ppermute | solution.py:55
  158.6 26.3 %all-to-all-start.1 = ((bf16[8,128,640]{2,1,0:T(8,128)(2,1)}), bf16[8,128,640]{2,1,0:T(8,128)(2,1)}, u32[]{:S(2)}, u32[]{:S(2)}) async-start(bf16[8,128,640]{2,1,0:T(8,128)(2,1)} %bitcast.29), calls=%async_computation.1 | async-start | bytes 2621440 | tf_op jit(solution)/shard_map/all_to_all | solution.py:422
  175.4 16.5 %copy-start.14 = (f32[2,320,640]{2,1,0:T(8,128)S(1)}, f32[2,320,640]{2,1,0:T(8,128)}, u32[]{:S(2)}) copy-start(f32[2,320,640]{2,1,0:T(8,128)} %param.16) | copy-start | bytes 4915204
  186.9 6.4 %collective-permute-start.22 = (f32[256]{0:T(256)S(1)}, f32[256]{0:T(256)S(1)}, u32[]{:S(2)}, u32[]{:S(2)}) collective-permute-start(f32[256]{0:T(256)S(1)} %get-tuple-element.61), channel_id=1, source_target_pairs={{0,1},{1,2},{2,3},{3,0},{4,5},{5,6},{6,7},{7,4},{8,9},{9,10},{10,1... | collective-permute-start | bytes 3080 | tf_op jit(solution)/shard_map/ppermute | solution.py:48
  187.8 5.5 %collective-permute-start.23 = (f32[256]{0:T(256)S(1)}, f32[256]{0:T(256)S(1)}, u32[]{:S(2)}, u32[]{:S(2)}) collective-permute-start(f32[256]{0:T(256)S(1)} %get-tuple-element.61), channel_id=1, source_target_pairs={{0,2},{1,3},{2,0},{3,1},{4,6},{5,7},{6,4},{7,5},{8,10},{9,11},{10,... | collective-permute-start | bytes 3080 | tf_op jit(solution)/shard_map/ppermute | solution.py:48
  190.8 3.6 %collective-permute-start.24 = (f32[256]{0:T(256)S(1)}, f32[256]{0:T(256)S(1)}, u32[]{:S(2)}, u32[]{:S(2)}) collective-permute-start(f32[256]{0:T(256)S(1)} %get-tuple-element.61), channel_id=1, source_target_pairs={{0,3},{1,0},{2,1},{3,2},{4,7},{5,4},{6,5},{7,6},{8,11},{9,8},{10,9... | collective-permute-start | bytes 3080 | tf_op jit(solution)/shard_map/ppermute | solution.py:48
  (17 other events, 67.2 us)

commit v2 on v0

v2 whole, which is shorter than its diff:
```python
import functools

import jax
import jax.numpy as jnp
import numpy as np
from jax import lax
from jax.experimental import pallas as pl
from jax.experimental.pallas import tpu as pltpu
from jax.sharding import PartitionSpec as P

CAP = 128
SCALE = 10
HALVES = 2
VMEM_BYTES = 20 * 1024 * 1024


EPS_NORM = 1e-06
EPS_ADAM = 1e-08
FIRST_BIAS = 1.0 - 0.9**10
SECOND_BIAS = 1.0 - 0.95**10

F32, BF16 = jnp.float32, jnp.bfloat16


VMEM = pl.BlockSpec(memory_space=pltpu.VMEM)
SMEM = pl.BlockSpec(memory_space=pltpu.SMEM)
ANY = pl.BlockSpec(memory_space=pl.ANY)
NT = (((1,), (1,)), ((), ()))


def call(kernel, name, in_specs, out_shape, args, macs=0, scratch=(), out_specs=None):
    return pl.pallas_call(
        kernel,
        in_specs=in_specs,
        out_specs=out_specs or [VMEM] * len(out_shape),
        out_shape=out_shape,
        scratch_shapes=scratch,
        compiler_params=pltpu.CompilerParams(vmem_limit_bytes=VMEM_BYTES),
        cost_estimate=pl.CostEstimate(flops=macs // SCALE, bytes_accessed=0, transcendentals=0),
        name=name,
    )(*args)


def ring_order(size):
    return list(range(0, size, 2)) + list(range(1, size, 2))[::-1]


def ring_pass(part, axis):
    size = lax.axis_size(axis)
    order = ring_order(size)
    return lax.ppermute(part, axis, [(order[i], order[(i + 1) % size]) for i in range(size)])


def others_over(axis, part):
    size = lax.axis_size(axis)
    return [
        lax.ppermute(part, axis, [(i, (i + step) % size) for i in range(size)])
        for step in range(1, size)
    ]


def swap_over(axis, bit, part):
    size = lax.axis_size(axis)
    return lax.ppermute(part, axis, [(i, i ^ bit) for i in range(size)])


def weight_rows(ref, rows, j, width):
    if len(ref.shape) == 2:
        return ref[rows, j * width : (j + 1) * width]
    return ref[j, rows]


def join_kernel(after, key_ref, value_ref, *refs):
    out_ref, sems = refs[after:]
    key_count, _, width = key_ref.shape
    copies = []
    for j in range(key_count + 1):
        source = key_ref.at[j] if j < key_count else value_ref
        flat = len(out_ref.shape) == 2
        target = out_ref.at[:, pl.ds(j * width, width)] if flat else out_ref.at[j]
        copies.append(pltpu.make_async_copy(source, target, sems.at[j]))
        copies[-1].start()
    for copy in copies:
        copy.wait()


def join_weights(key_weight, value_weight, after):
    key_count, model_width, width = key_weight.shape
    flat = width % 128 == 0
    shape = (model_width, (key_count + 1) * width) if flat else (key_count + 1, model_width, width)
    return call(
        functools.partial(join_kernel, len(after)),
        "join_weights",
        [ANY] * (2 + len(after)),
        [jax.ShapeDtypeStruct(shape, BF16)],
        [key_weight, value_weight, *after],
        scratch=[pltpu.SemaphoreType.DMA((key_count + 1,))],
    )[0]


def forward_kernel(h, steps, table_ref, *refs):
    parts, refs = refs[:steps], refs[steps:]
    weight_ref, state_ref, grad_ref, *before = refs[: 3 + (h > 0)]
    val_ref, turned_ref, sum_ref, memory_ref = refs[3 + (h > 0) :]
    key_count, half, width = val_ref.shape
    rows = slice(h * half, (h + 1) * half)
    places = []
    for step in range(steps):
        place = pl.multiple_of(table_ref[step] * width, width)
        places.append(place)
        turned_ref[pl.ds(place, width), :] = parts[step][...].T
        if width % 128 == 0:
            memory_ref[:, pl.ds(place, width)] = parts[step][...]

    def product(j):
        if width % 128 == 0:
            weight = weight_rows(weight_ref, slice(None), j, width)
            return jnp.dot(memory_ref[...], weight, preferred_element_type=F32)
        return sum(
            jnp.dot(
                parts[step][...],
                weight_rows(weight_ref, pl.ds(places[step], width), j, width),
                preferred_element_type=F32,
            )
            for step in range(steps)
        )

    row_sum = lambda x: jnp.sum(x, axis=1, keepdims=True)
    sums = [None] * (4 * key_count)
    for j in range(key_count):
        val = product(j)
        val_ref[j] = val
        state = state_ref[j, rows].astype(F32)
        sums[j] = row_sum(state * state)
        sums[key_count + j] = row_sum(val * val)
        sums[2 * key_count + j] = row_sum(state * val)
    val = product(key_count)
    for j in range(key_count):
        sums[3 * key_count + j] = row_sum(grad_ref[j, rows].astype(F32) * val)
    lane = lax.broadcasted_iota(jnp.int32, (half, 128), 1)
    table = jnp.zeros((half, 128), F32)
    for i, s in enumerate(sums):
        table = jnp.where(lane == i, s, table)
    if h:
        sum_ref[:, : h * half] = before[0][...]
    sum_ref[:, rows] = table.T[: 4 * key_count]


def forward(h, table, parts, weights, states, grads, before):
    half, width = parts[0].shape
    key_count = states.shape[0]
    model_width = weights.shape[-2]
    return call(
        functools.partial(forward_kernel, h, len(parts)),
        "forward",
        [SMEM] + [VMEM] * (len(parts) + 3 + len(before)),
        [
            jax.ShapeDtypeStruct((key_count, half, width), F32),
            jax.ShapeDtypeStruct((model_width, half), BF16),
            jax.ShapeDtypeStruct((4 * key_count, (h + 1) * half), F32),
        ],
        [table, *parts, weights, states, grads, *before],
        macs=half * model_width * width * (key_count + 1),
        scratch=[pltpu.VMEM((half, model_width), BF16)],
    )


def cot_kernel(sums_count, model_width, *refs):
    sum_refs, refs = refs[:sums_count], refs[sums_count:]
    val_refs, (state_ref, grad_ref, joined_ref) = refs[:HALVES], refs[HALVES:]
    key_count, half, width = val_refs[0].shape
    total = sum_refs[0][...]
    for ref in sum_refs[1:]:
        total = total + ref[...]
    root_width = jnp.sqrt(F32(model_width))
    state_sum, key_sum, cross_dot, out_dot = (
        total[i * key_count : (i + 1) * key_count] for i in range(4)
    )
    state_rs = lax.rsqrt(state_sum / model_width + EPS_NORM)
    key_rs = lax.rsqrt(key_sum / model_width + EPS_NORM)
    scores = cross_dot * state_rs * key_rs / root_width
    gate_val = 1.0 / (1.0 + jnp.exp(-scores))
    dscore = out_dot * gate_val * (1.0 - gate_val)
    lead = key_rs * dscore / root_width
    slope = key_rs * scores / root_width
    factors = jnp.concatenate([lead, state_rs, slope, gate_val], axis=0)
    filler = jnp.zeros((128 - 4 * key_count, half), F32)
    for h in range(HALVES):
        rows = slice(h * half, (h + 1) * half)
        table = jnp.concatenate([factors[:, rows], filler], axis=0).T
        column = lambda kind, j: table[:, kind * key_count + j : kind * key_count + j + 1]
        value_cot = None
        for j in range(key_count):
            state = state_ref[j, rows].astype(F32)
            inner = state * column(1, j) - val_refs[h][j] * column(2, j)
            joined_ref[rows, j * width : (j + 1) * width] = (column(0, j) * inner).astype(BF16)
            gated = column(3, j) * grad_ref[j, rows].astype(F32)
            value_cot = gated if value_cot is None else value_cot + gated
        joined_ref[rows, key_count * width :] = value_cot.astype(BF16)


def cotangents(sums, vals, states, grads, model_width):
    key_count, tok_count, width = states.shape
    return call(
        functools.partial(cot_kernel, len(sums), model_width),
        "cotangents",
        [VMEM] * (len(sums) + len(vals) + 2),
        [jax.ShapeDtypeStruct((tok_count, (key_count + 1) * width), BF16)],
        [*sums, *vals, states, grads],
        macs=tok_count * width,
    )[0]


def back_kernel(step, after, table_ref, joined_ref, weight_ref, *refs):
    refs = refs[after:]
    width = sum(ref.shape[1] for ref in refs)
    place = pl.multiple_of(table_ref[step] * width, width)
    rows = pl.ds(place, width)
    if len(weight_ref.shape) == 2:
        term = lax.dot_general(
            joined_ref[...], weight_ref[rows, :], NT, preferred_element_type=F32
        )
    else:
        term = sum(
            lax.dot_general(
                joined_ref[:, j * width : (j + 1) * width],
                weight_ref[j, rows],
                NT,
                preferred_element_type=F32,
            )
            for j in range(weight_ref.shape[0])
        )
    start = 0
    for ref in refs:
        ref[...] = term[:, start : start + ref.shape[1]].astype(BF16)
        start += ref.shape[1]


def back(step, table, joined, weights, cuts, after=()):
    tok_count, columns = joined.shape
    return call(
        functools.partial(back_kernel, step, len(after)),
        "back",
        [SMEM] + [VMEM] * 2 + [ANY] * len(after),
        [jax.ShapeDtypeStruct((tok_count, cut), BF16) for cut in cuts],
        [table, joined, weights, *after],
        macs=tok_count * columns * sum(cuts),
    )


def outer_kernel(entry, after, plan_ref, joined_ref, other_joined_ref, *refs):
    turned, others, refs = refs[:HALVES], refs[HALVES : 2 * HALVES], refs[2 * HALVES + after :]
    rows = sum(ref.shape[0] for ref in refs)
    place = pl.multiple_of(plan_ref[entry] * rows, rows)
    block = lambda halves: jnp.concatenate([ref[pl.ds(place, rows), :] for ref in halves], axis=1)
    product = jnp.dot(block(turned), joined_ref[...], preferred_element_type=F32)
    product = product + jnp.dot(block(others), other_joined_ref[...], preferred_element_type=F32)
    start = 0
    for ref in refs:
        ref[...] = product[start : start + ref.shape[0]].astype(BF16)
        start += ref.shape[0]


def outer(rel, skip, plan, rows, joined, other_joined, turned, other_turned, after=()):
    tok_count, columns = joined.shape
    return call(
        functools.partial(outer_kernel, skip + rel, len(after)),
        "outer",
        [SMEM] + [VMEM] * (2 + 2 * HALVES) + [ANY] * len(after),
        [jax.ShapeDtypeStruct((r, columns), BF16) for r in (rows // 2, rows - rows // 2)],
        [plan, joined, other_joined, *turned, *other_turned, *after],
        macs=2 * rows * tok_count * columns,
    )


def sum_kernel(*refs):
    total = refs[0][...].astype(F32)
    for ref in refs[1:-1]:
        total = total + ref[...].astype(F32)
    refs[-1][...] = total.astype(refs[-1].dtype)


def add(*parts):
    return call(
        sum_kernel,
        "add",
        [VMEM] * len(parts),
        [jax.ShapeDtypeStruct(parts[0].shape, BF16)],
        parts,
        macs=parts[0].size,
    )[0]


def pick_kernel(slot_ref, passing_ref, term_ref, out_ref):
    total = (passing_ref[...].astype(F32) + term_ref[...].astype(F32)).astype(BF16)
    slots = lax.broadcasted_iota(jnp.int32, (out_ref.shape[0], total.shape[0]), 0)
    pick = sum(
        (slots == slot_ref[n : n + 1, :]).astype(F32) for n in range(slot_ref.shape[0])
    ).astype(BF16)
    out_ref[...] = jnp.dot(pick, total, preferred_element_type=F32).astype(BF16)


def pick_rows(slot_index, passing, term, slot_count):
    tok_count, cut = passing.shape
    return call(
        pick_kernel,
        "pick_rows",
        [VMEM] * 3,
        [jax.ShapeDtypeStruct((slot_count, cut), BF16)],
        [slot_index, passing, term],
        macs=slot_count * tok_count * cut,
    )[0]


def place_kernel(row_ref, incoming_ref, grad_ref, sum_ref):
    rows = lax.broadcasted_iota(jnp.int32, (grad_ref.shape[0], row_ref.shape[1]), 0) + 1
    place = (rows == row_ref[...]).astype(F32).astype(BF16)
    grad = jnp.dot(place, incoming_ref[...], preferred_element_type=F32)
    grad_ref[...] = grad
    sum_ref[...] = jnp.sum(grad * grad, axis=1, keepdims=True)


def place_rows(incoming_rows, incoming, owned_rows):
    slot_count, cut = incoming.shape
    return call(
        place_kernel,
        "place_rows",
        [VMEM] * 2,
        [
            jax.ShapeDtypeStruct((owned_rows, cut), F32),
            jax.ShapeDtypeStruct((owned_rows, 1), F32),
        ],
        [incoming_rows, incoming],
        macs=slot_count * owned_rows * cut,
    )


def halve(blocks, bits, axis):
    mine = [blocks[0]]
    for bit in bits:
        far = sorted((rel for rel in blocks if rel & bit), reverse=True)
        arrived = {rel: swap_over(axis, bit, blocks[rel]) for rel in far}
        mine.append(arrived[bit])
        blocks = {
            rel: add(blocks[rel], arrived[rel ^ bit]) if rel else None
            for rel in blocks
            if not rel & bit
        }
    return sum(part.astype(F32) for part in mine)


def on_device(
    retrieved,
    branch_states,
    out_grad,
    key_weight,
    value_weight,
    key_grad_acc,
    value_grad_acc,
    row_index,
    row_tier,
    adam_mean,
    adam_second,
):
    tok_count, key_count, width = branch_states.shape
    groups = lax.axis_size("group")
    shards = lax.axis_size("tensor")
    model_width = width * shards
    owned_rows = adam_mean.shape[0]
    half = tok_count // HALVES
    me = lax.axis_index("group")
    line = lax.axis_index("tensor")
    order = ring_order(shards)
    behind, ahead = np.zeros((shards, shards), np.int32), np.zeros((shards, shards), np.int32)
    for spot, device in enumerate(order):
        for step in range(shards):
            behind[device, step] = order[(spot - step) % shards]
            ahead[device, step] = order[(spot - 1 - step) % shards]
    plan = jnp.concatenate(
        [
            lax.dynamic_index_in_dim(jnp.asarray(np.concatenate([behind, ahead], 1)), line, 0, False),
            jnp.arange(groups, dtype=jnp.int32) ^ me,
        ]
    )

    by_row = lambda x: lax.optimization_barrier(jnp.transpose(x, (1, 0, 2)))
    chains = []
    for h in range(HALVES):
        rows = by_row(retrieved[h * half : (h + 1) * half])
        chains.append([jnp.sum(rows.astype(F32), axis=0).astype(BF16)])
    for step in range(shards - 1):
        for chain in chains:
            chain.append(ring_pass(chain[-1], "tensor"))
    states, grads = by_row(branch_states), by_row(out_grad)

    routed, _ = lax.optimization_barrier((row_index.T, chains[0][1]))
    owner_idx = routed // owned_rows
    local_row = routed - owner_idx * owned_rows
    flat_owner = owner_idx.T.reshape(-1)
    owner_marks = (flat_owner[:, None] == jnp.arange(groups, dtype=jnp.int32)[None, :]).astype(
        jnp.int32
    )
    slot_place = jnp.sum(jnp.cumsum(owner_marks, axis=0) * owner_marks, axis=1) - 1
    slot_index = owner_idx * CAP + slot_place.reshape(row_index.shape).T
    slots = lax.broadcasted_iota(jnp.int32, (groups * CAP, tok_count), 0)
    slot_row = sum(
        jnp.sum(
            jnp.where(slots == slot_index[n][None, :], local_row[n][None, :] + 1, 0), axis=1
        )
        for n in range(row_index.shape[1])
    )
    incoming_rows = lax.all_to_all(
        slot_row.reshape(groups, CAP), "group", split_axis=0, concat_axis=0, tiled=True
    ).reshape(1, -1)

    weights = join_weights(
        key_weight, value_weight, (incoming_rows, slot_index, states, grads, plan)
    )
    vals, turned, sums = [], [], []
    for h, chain in enumerate(chains):
        val, turn, sums_here = forward(h, plan, chain, weights, states, grads, sums)
        vals.append(val)
        turned.append(turn)
        sums = [sums_here]
    sums += others_over("tensor", sums[0])
    other_turned = [swap_over("group", 1, turn) for turn in turned]

    lanes = -(-width // 256) * 128
    cuts = [lanes, width - lanes] if width > lanes else [width]
    joined = cotangents(sums, vals, states, grads, model_width)
    other_joined = swap_over("group", 1, joined)
    passing = [ring_pass(part, "tensor") for part in back(shards, plan, joined, weights, cuts)]

    shard_rows = model_width // groups
    order = sorted(range(0, groups, 2), key=lambda rel: (-bin(rel).count("1"), rel))
    near, terms, last = {}, [], ()
    for k, rel in enumerate(order):
        near[rel] = outer(
            rel, 2 * shards, plan, shard_rows, joined, other_joined, turned, other_turned, last
        )
        last = near[rel][:1]
        if k and len(terms) < shards - 1:
            terms.append(back(shards + len(terms) + 1, plan, joined, weights, cuts, last))
            last = terms[-1][:1]
    while len(terms) < shards - 1:
        terms.append(back(shards + len(terms) + 1, plan, joined, weights, cuts, last))
        last = terms[-1][:1]
    bits = []
    bit = 2
    while bit < groups:
        bits.append(bit)
        bit *= 2
    weight_sum = jnp.concatenate(
        [
            halve({rel: near[rel][0] for rel in order}, bits, "group"),
            halve({rel: near[rel][1] for rel in order}, bits[::-1], "group"),
        ],
        axis=0,
    )
    key_grad = key_grad_acc + jnp.stack(
        [weight_sum[:, j * width : (j + 1) * width] for j in range(key_count)]
    )
    value_grad = value_grad_acc + weight_sum[:, key_count * width :]

    for step in range(shards - 2):
        passing = [
            ring_pass(add(part, term), "tensor") for part, term in zip(passing, terms[step])
        ]
    row_grads, row_parts = [], []
    for part, term in zip(passing, terms[-1]):
        outgoing = pick_rows(slot_index, part, term, groups * CAP)
        incoming = lax.all_to_all(
            outgoing.reshape(groups, CAP, -1), "group", split_axis=0, concat_axis=0, tiled=True
        ).reshape(groups * CAP, -1)
        grad, part_sum = place_rows(incoming_rows, incoming, owned_rows)
        row_grads.append(grad)
        row_parts.append(part_sum[:, 0])
    row_grad = jnp.concatenate(row_grads, axis=1)
    row_part = sum(row_parts)
    row_sum = row_part + sum(others_over("tensor", row_part))
    is_hot = (row_tier == 1)[:, None]
    mean_hot = 0.9 * adam_mean + 0.1 * row_grad
    second_hot = 0.95 * adam_second + 0.05 * row_grad * row_grad
    step_hot = mean_hot / FIRST_BIAS / (jnp.sqrt(second_hot / SECOND_BIAS) + EPS_ADAM)
    step_cold = row_grad * lax.rsqrt(row_sum / model_width + EPS_NORM)[:, None]
    new_mean = jnp.where(is_hot, mean_hot, adam_mean)
    new_second = jnp.where(is_hot, second_hot, adam_second)
    row_step = jnp.where(is_hot, step_hot, step_cold)
    return (key_grad, value_grad, new_mean, new_second, row_step)


def solution(mesh):
    return jax.shard_map(
        on_device,
        mesh=mesh,
        in_specs=(
            P("group", None, "tensor"),
            P("group", None, "tensor"),
            P("group", None, "tensor"),
            P(None, None, "tensor"),
            P(None, "tensor"),
            P(None, "group", "tensor"),
            P("group", "tensor"),
            P("group", None),
            P("group"),
            P("group", "tensor"),
            P("group", "tensor"),
        ),
        out_specs=(
            P(None, "group", "tensor"),
            P("group", "tensor"),
            P("group", "tensor"),
            P("group", "tensor"),
            P("group", "tensor"),
        ),
        check_vma=False,
    )
```

time: 381 us -> 164 us (0.43)
  waiting for transfers between devices: 213 us -> 46.6 us
  starting transfers between devices: 7.85 us -> 51.7 us
  Pallas kernels: 0 us -> 37 us
  matrix products: 36.3 us -> 0 us
  blocking collectives: 34.9 us -> 0 us
  local copies, waits for them, and re-layouts: 36.4 us -> 11.7 us
  other arithmetic: 37.5 us -> 15.3 us
  between operations: 14 us -> 1.05 us
    reduce_scatter x2 -> x0, waiting for transfers between devices: 128 us -> none  [the longest x1 64.2 us: on_device(): lax.psum_scatter(lax.dot_general(memory, joined, (((0,), (0,)), ((), ()))...]
    all_gather x1 -> x0, waiting for transfers between devices: 57.5 us -> none  [on_device(): memory = lax.all_gather(local_memory, 'tensor', axis=1, tiled=True)]
    ppermute x0 -> x27, starting transfers between devices: none -> 40.6 us  [the longest x12 27.3 us: ring_pass(): lax.ppermute(part, axis, [(order[i], order[(i + 1) % size]) for i in rang...]
    ppermute x0 -> x27, waiting for transfers between devices: none -> 39.5 us  [the longest x12 24.2 us: ring_pass(): lax.ppermute(part, axis, [(order[i], order[(i + 1) % size]) for i in rang...]
    pallas_call x0 -> x22, Pallas kernels: none -> 37 us  [call(): pl.pallas_call(kernel, in_specs=in_specs, out_specs=out_specs or [VMEM] *...]
    dot_general x5 -> x0, matrix products: 36.3 us -> none  [the longest x1 11.5 us: on_device(): lax.dot_general(memory, joined, (((0,), (0,)), ((), ())), preferred_eleme...]
    psum x3 -> x0, blocking collectives: 34.9 us -> none  [the longest x2 24.8 us: on_device(): lax.psum((partial_dots[0], partial_dots[1], partial_dots[2], partial_dots...]
    all_to_all x2 -> x3, waiting for transfers between devices: 27.6 us -> 7.1 us  [the longest x2 4.09 us: on_device(): lax.all_to_all(outgoing.reshape(groups, CAP, -1), 'group', split_axis=0,...]
  transfers between devices with their start and end apart: 5 -> 30, of which waited for: 4 -> 16; matrix products, arithmetic and copies ran while one was open for 14% -> 8% of each run, Pallas kernels for 0% -> 19%
where the time goes in v2:
time: 164 us; the launch traced here: 163 us
  starting transfers between devices  51.7 us (32%)
  waiting for transfers between devices  46.6 us (28%)
  Pallas kernels  37 us (23%)
  other arithmetic  15.3 us (9%)
  local copies, waits for them, and re-layouts  11.7 us (7%)
    pallas_call x22, Pallas kernels, call(): pl.pallas_call(kernel, in_specs=in_specs, out_specs=out_specs or [VMEM] *...  37 us
    ppermute x12, starting transfers between devices, ring_pass(): lax.ppermute(part, axis, [(order[i], order[(i + 1) % size]) for i in rang...  27.3 us
    ppermute x12, waiting for transfers between devices, ring_pass(): lax.ppermute(part, axis, [(order[i], order[(i + 1) % size]) for i in rang...  24.2 us
    ppermute x6, waiting for transfers between devices, others_over(): lax.ppermute(part, axis, [(i, (i + step) % size) for i in range(size)])  8.27 us
    unnamed x47, local copies, waits for them, and re-layouts  7.77 us
    all_to_all x2, starting transfers between devices, on_device(): lax.all_to_all(outgoing.reshape(groups, CAP, -1), 'group', split_axis=0,...  7.37 us
    ppermute x9, starting transfers between devices, swap_over(): return lax.ppermute(part, axis, [(i, i ^ bit) for i in range(size)])  7.16 us
    ppermute x9, waiting for transfers between devices, swap_over(): return lax.ppermute(part, axis, [(i, i ^ bit) for i in range(size)])  7.06 us
  transfers between devices with their start and end apart: 30, of which 16 were waited for; matrix products, arithmetic and copies ran while one was open for 8% of the time, Pallas kernels for 19%

profile of v2, /device:TPU:0, one launch (start us, length us, event | category | flops | bytes accessed | tf_op | source)
XLA Modules:
  0.0 163.4 jit_solution(5454330006495209376)
XLA Ops:
  0.6 2.2 %slice_bitcast_fusion = (bf16[2,256,640]{2,0,1:T(2,128)(2,1)S(1)}, bf16[2,256,640]{2,0,1:T(2,128)(2,1)S(1)}) fusion(bf16[512,2,640]{2,1,0:T(2,128)(2,1)} %param.12), kind=kLoop, calls=%fused_computation.25 | loop fusion | bytes 2621440 | tf_op jit(solution)/shard_map/transpose | solution.py:386
  4.6 4.1 %collective-permute-start.3 = (bf16[256,640]{1,0:T(8,128)(2,1)S(1)}, bf16[256,640]{1,0:T(8,128)(2,1)S(1)}, u32[]{:S(2)}, u32[]{:S(2)}) collective-permute-start(bf16[256,640]{1,0:T(8,128)(2,1)S(1)} %reduce_sum.52.refs_0_), channel_id=1, source_target_pairs={{0,2},{2,3},{3,1},{1,0},{4,6},{6,7},{7,5},{5,4},{8,10},{10,11},{11... | collective-permute-start | bytes 983048 | tf_op jit(solution)/shard_map/ppermute | solution.py:51
  12.7 4.1 %collective-permute-done.3.refs_1_ = bf16[256,640]{1,0:T(8,128)(2,1)S(1)} collective-permute-done((bf16[256,640]{1,0:T(8,128)(2,1)S(1)}, bf16[256,640]{1,0:T(8,128)(2,1)S(1)}, u32[]{:S(2)}, u32[]{:S(2)}) %collective-permute-start.3) | collective-permute-done | bytes 327712 | tf_op jit(solution)/shard_map/ppermute | solution.py:51
  17.3 2.3 %reduce-window.6 = s32[8,8,128]{2,1,0:T(8,128)S(1)} reduce-window(s32[8,8,128]{2,1,0:T(8,128)S(1)} %fusion.10, s32[]{:T(128)} %constant.26.clone.1), window={size=1x1x128 pad=0_0x0_0x127_0}, to_apply=%region_2.3 | reduce-window | flops 1040384 | bytes 65540 | tf_op jit(solution)/shard_map/reduce-window
  20.5 3.4 %collective-permute-start.4 = (bf16[256,640]{1,0:T(8,128)(2,1)S(1)}, bf16[256,640]{1,0:T(8,128)(2,1)}, u32[]{:S(2)}, u32[]{:S(2)}) collective-permute-start(bf16[256,640]{1,0:T(8,128)(2,1)S(1)} %collective-permute-done.3.refs_1_), channel_id=1, source_target_pairs={{0,2},{2,3},{3,1},{1,0},{4,6},{6,7},{7,5},{5,4},{8,10},{10,11},{11... | collective-permute-start | bytes 983048 | tf_op jit(solution)/shard_map/ppermute | solution.py:51
  23.9 3.0 %collective-permute-start.1 = (bf16[256,640]{1,0:T(8,128)(2,1)S(1)}, bf16[256,640]{1,0:T(8,128)(2,1)}, u32[]{:S(2)}, u32[]{:S(2)}) collective-permute-start(bf16[256,640]{1,0:T(8,128)(2,1)S(1)} %collective-permute-done.refs_1_), channel_id=1, source_target_pairs={{0,2},{2,3},{3,1},{1,0},{4,6},{6,7},{7,5},{5,4},{8,10},{10,11},{11... | collective-permute-start | bytes 983048 | tf_op jit(solution)/shard_map/ppermute | solution.py:51
  27.6 4.5 %collective-permute-done.4.refs_2_ = bf16[256,640]{1,0:T(8,128)(2,1)} collective-permute-done((bf16[256,640]{1,0:T(8,128)(2,1)S(1)}, bf16[256,640]{1,0:T(8,128)(2,1)}, u32[]{:S(2)}, u32[]{:S(2)}) %collective-permute-start.4) | collective-permute-done | bytes 327712 | tf_op jit(solution)/shard_map/ppermute | solution.py:51
  32.0 3.5 %collective-permute-start.5 = (bf16[256,640]{1,0:T(8,128)(2,1)}, bf16[256,640]{1,0:T(8,128)(2,1)}, u32[]{:S(2)}, u32[]{:S(2)}) collective-permute-start(bf16[256,640]{1,0:T(8,128)(2,1)} %collective-permute-done.4.refs_2_), channel_id=1, source_target_pairs={{0,2},{2,3},{3,1},{1,0},{4,6},{6,7},{7,5},{5,4},{8,10},{10,11},{11... | collective-permute-start | bytes 983048 | tf_op jit(solution)/shard_map/ppermute | solution.py:51
  35.5 3.5 %collective-permute-done.1.refs_2_ = bf16[256,640]{1,0:T(8,128)(2,1)} collective-permute-done((bf16[256,640]{1,0:T(8,128)(2,1)S(1)}, bf16[256,640]{1,0:T(8,128)(2,1)}, u32[]{:S(2)}, u32[]{:S(2)}) %collective-permute-start.1) | collective-permute-done | bytes 327712 | tf_op jit(solution)/shard_map/ppermute | solution.py:51
  39.1 3.5 %collective-permute-start.2 = (bf16[256,640]{1,0:T(8,128)(2,1)}, bf16[256,640]{1,0:T(8,128)(2,1)}, u32[]{:S(2)}, u32[]{:S(2)}) collective-permute-start(bf16[256,640]{1,0:T(8,128)(2,1)} %collective-permute-done.1.refs_2_), channel_id=1, source_target_pairs={{0,2},{2,3},{3,1},{1,0},{4,6},{6,7},{7,5},{5,4},{8,10},{10,11},{11... | collective-permute-start | bytes 983048 | tf_op jit(solution)/shard_map/ppermute | solution.py:51
  43.7 3.7 %all-to-all-start = ((s32[8,1,128]{2,1,0:T(1,128)}), s32[8,1,128]{2,1,0:T(1,128)S(1)}, u32[]{:S(2)}, u32[]{:S(2)}) async-start(s32[8,1,128]{2,1,0:T(1,128)} %bitcast.11), calls=%async_computation | async-start | bytes 8192 | tf_op jit(solution)/shard_map/all_to_all | solution.py:412
  49.0 3.0 %all-to-all-done = s32[8,1,128]{2,1,0:T(1,128)S(1)} async-done(((s32[8,1,128]{2,1,0:T(1,128)}), s32[8,1,128]{2,1,0:T(1,128)S(1)}, u32[]{:S(2)}, u32[]{:S(2)}) %all-to-all-start) | async-done | bytes 4128 | tf_op jit(solution)/shard_map/all_to_all | solution.py:412
  52.0 2.9 %copy-done = bf16[2,2560,640]{2,1,0:T(8,128)(2,1)S(1)} copy-done((bf16[2,2560,640]{2,1,0:T(8,128)(2,1)S(1)}, bf16[2,2560,640]{2,1,0:T(8,128)(2,1)}, u32[]{:S(2)}) %copy-start) | copy-done | bytes 6553624
  57.8 4.8 %forward.2 = (f32[2,256,640]{2,1,0:T(8,128)S(1)}, bf16[2560,256]{1,0:T(8,128)(2,1)S(1)}, f32[8,256]{1,0:T(8,128)S(1)}) custom-call(s32[16]{0:T(128)S(1)} %pad_add_fusion.refs_4_.table_ref.plan_ref, bf16[256,640]{1,0:T(8,128)(2,1)S(1)} %reduce_sum.52.refs_0_, bf16[256,640]{1,0:T(8,128)(2,1)S(1)} %copy-done.9, ...), custom_call_target="tpu_custom_call" | custom-call | flops 125829120 | tf_op jit(solution)/shard_map/forward/pallas_call | solution.py:32
  62.5 4.8 %forward.3 = (f32[2,256,640]{2,1,0:T(8,128)S(1)}, bf16[2560,256]{1,0:T(8,128)(2,1)S(1)}, f32[8,512]{1,0:T(8,128)S(1)}) custom-call(s32[16]{0:T(128)S(1)} %pad_add_fusion.refs_4_.table_ref.plan_ref, bf16[256,640]{1,0:T(8,128)(2,1)S(1)} %reduce_sum.51.refs_0_, bf16[256,640]{1,0:T(8,128)(2,1)S(1)} %copy-done.7, ...), custom_call_target="tpu_custom_call" | custom-call | flops 125829120 | tf_op jit(solution)/shard_map/forward/pallas_call | solution.py:32
  71.1 2.3 %collective-permute-done.7.refs_2_ = f32[8,512]{1,0:T(8,128)S(1)} collective-permute-done((f32[8,512]{1,0:T(8,128)S(1)}, f32[8,512]{1,0:T(8,128)S(1)}, u32[]{:S(2)}, u32[]{:S(2)}) %collective-permute-start.7) | collective-permute-done | bytes 16416 | tf_op jit(solution)/shard_map/ppermute | solution.py:57
  76.0 2.3 %back.6 = (bf16[512,384]{1,0:T(8,128)(2,1)S(1)}, bf16[512,256]{1,0:T(8,128)(2,1)S(1)}) custom-call(s32[16]{0:T(128)S(1)} %pad_add_fusion.refs_4_.table_ref.plan_ref, bf16[512,1920]{1,0:T(8,128)(2,1)S(1)} %cotangents.1.joined_ref, bf16[2560,1920]{1,0:T(8,128)(2,1)S(1)} %join_weights.1.refs_4_.weight_ref), custom_call_target="tpu_custom_call" | custom-call | flops 62914560 | tf_op jit(solution)/shard_map/back/pallas_call | solution.py:32
  83.2 2.9 %outer.4 = (bf16[160,1920]{1,0:T(8,128)(2,1)S(1)}, bf16[160,1920]{1,0:T(8,128)(2,1)}) custom-call(s32[16]{0:T(128)S(1)} %pad_add_fusion.refs_4_.table_ref.plan_ref, bf16[512,1920]{1,0:T(8,128)(2,1)S(1)} %cotangents.1.joined_ref, bf16[512,1920]{1,0:T(8,128)(2,1)S(1)} %collective-permute-done.9.other_joined_ref, ...), custom_call_target="tpu_custom_call" | custom-call | flops 62914560 | tf_op jit(solution)/shard_map/outer/pallas_call | solution.py:32
  87.8 2.8 %outer.5 = (bf16[160,1920]{1,0:T(8,128)(2,1)}, bf16[160,1920]{1,0:T(8,128)(2,1)S(1)}) custom-call(s32[16]{0:T(128)S(1)} %pad_add_fusion.refs_4_.table_ref.plan_ref, bf16[512,1920]{1,0:T(8,128)(2,1)S(1)} %cotangents.1.joined_ref, bf16[512,1920]{1,0:T(8,128)(2,1)S(1)} %collective-permute-done.9.other_joined_ref, ...), custom_call_target="tpu_custom_call" | custom-call | flops 62914560 | tf_op jit(solution)/shard_map/outer/pallas_call | solution.py:32
  90.6 2.3 %back.4 = (bf16[512,384]{1,0:T(8,128)(2,1)S(1)}, bf16[512,256]{1,0:T(8,128)(2,1)S(1)}) custom-call(s32[16]{0:T(128)S(1)} %pad_add_fusion.refs_4_.table_ref.plan_ref, bf16[512,1920]{1,0:T(8,128)(2,1)S(1)} %cotangents.1.joined_ref, bf16[2560,1920]{1,0:T(8,128)(2,1)S(1)} %join_weights.1.refs_4_.weight_ref, bf16[160,1920]{1,0:T(8,128)(2,1)} %get-tuple-element.40.refs_0_), custom_call_target="tpu_custom_call" | custom-call | flops 62914560 | tf_op jit(solution)/shard_map/back/pallas_call | solution.py:32
  94.3 4.3 %collective-permute-done.18.refs_0_ = bf16[512,384]{1,0:T(8,128)(2,1)S(1)} collective-permute-done((bf16[512,384]{1,0:T(8,128)(2,1)S(1)}, bf16[512,384]{1,0:T(8,128)(2,1)S(1)}, u32[]{:S(2)}, u32[]{:S(2)}) %collective-permute-start.18) | collective-permute-done | bytes 393248 | tf_op jit(solution)/shard_map/ppermute | solution.py:51
  98.7 2.1 %collective-permute-start.19 = (bf16[512,384]{1,0:T(8,128)(2,1)S(1)}, bf16[512,384]{1,0:T(8,128)(2,1)S(1)}, u32[]{:S(2)}, u32[]{:S(2)}) collective-permute-start(bf16[512,384]{1,0:T(8,128)(2,1)S(1)} %add.144), channel_id=1, source_target_pairs={{0,2},{2,3},{3,1},{1,0},{4,6},{6,7},{7,5},{5,4},{8,10},{10,11},{11... | collective-permute-start | bytes 1179656 | tf_op jit(solution)/shard_map/ppermute | solution.py:51
  100.8 2.1 %outer.6 = (bf16[160,1920]{1,0:T(8,128)(2,1)S(1)}, bf16[160,1920]{1,0:T(8,128)(2,1)S(1)}) custom-call(s32[16]{0:T(128)S(1)} %copy-done.11, bf16[512,1920]{1,0:T(8,128)(2,1)S(1)} %cotangents.1.joined_ref, bf16[512,1920]{1,0:T(8,128)(2,1)S(1)} %collective-permute-done.9.other_joined_ref, bf16[2560,256]{1,0:T(8,128)(2,1)S(1)} %get-tuple-element.37.refs_0_, ...), custom_call_target="tpu_custom_call" | custom-call | flops 62914560 | tf_op jit(solution)/shard_map/outer/pallas_call | solution.py:32
  102.9 2.3 %back.5 = (bf16[512,384]{1,0:T(8,128)(2,1)S(1)}, bf16[512,256]{1,0:T(8,128)(2,1)S(1)}) custom-call(s32[16]{0:T(128)S(1)} %copy-done.11, bf16[512,1920]{1,0:T(8,128)(2,1)S(1)} %cotangents.1.joined_ref, bf16[2560,1920]{1,0:T(8,128)(2,1)S(1)} %join_weights.1.refs_4_.weight_ref, bf16[160,1920]{1,0:T(8,128)(2,1)S(1)} %get-tuple-element.42.refs_0_), custom_call_target="tpu_custom_call" | custom-call | flops 62914560 | tf_op jit(solution)/shard_map/back/pallas_call | solution.py:32
  111.5 2.3 %back.7 = (bf16[512,384]{1,0:T(8,128)(2,1)S(1)}, bf16[512,256]{1,0:T(8,128)(2,1)S(1)}) custom-call(s32[16]{0:T(128)S(1)} %copy-done.11, bf16[512,1920]{1,0:T(8,128)(2,1)S(1)} %cotangents.1.joined_ref, bf16[2560,1920]{1,0:T(8,128)(2,1)S(1)} %join_weights.1.refs_4_.weight_ref, bf16[160,1920]{1,0:T(8,128)(2,1)S(1)} %get-tuple-element.44.refs_0_), custom_call_target="tpu_custom_call" | custom-call | flops 62914560 | tf_op jit(solution)/shard_map/back/pallas_call | solution.py:32
  113.8 3.3 %collective-permute-done.23.passing_ref = bf16[512,256]{1,0:T(8,128)(2,1)S(1)} collective-permute-done((bf16[512,256]{1,0:T(8,128)(2,1)S(1)}, bf16[512,256]{1,0:T(8,128)(2,1)S(1)}, u32[]{:S(2)}, u32[]{:S(2)}) %collective-permute-start.23) | collective-permute-done | bytes 262176 | tf_op jit(solution)/shard_map/ppermute | solution.py:51
  118.6 3.5 %all-to-all-start.2 = ((bf16[8,128,256]{2,1,0:T(8,128)(2,1)}), bf16[8,128,256]{2,1,0:T(8,128)(2,1)S(1)}, u32[]{:S(2)}, u32[]{:S(2)}) async-start(bf16[8,128,256]{2,1,0:T(8,128)(2,1)} %bitcast.19), calls=%async_computation.2 | async-start | bytes 1048576 | tf_op jit(solution)/shard_map/all_to_all | solution.py:472
  122.2 2.1 %collective-permute-start.20 = (bf16[512,384]{1,0:T(8,128)(2,1)S(1)}, bf16[512,384]{1,0:T(8,128)(2,1)S(1)}, u32[]{:S(2)}, u32[]{:S(2)}) collective-permute-start(bf16[512,384]{1,0:T(8,128)(2,1)S(1)} %add.145), channel_id=1, source_target_pairs={{0,2},{2,3},{3,1},{1,0},{4,6},{6,7},{7,5},{5,4},{8,10},{10,11},{11... | collective-permute-start | bytes 1179656 | tf_op jit(solution)/shard_map/ppermute | solution.py:51
  129.2 4.5 %collective-permute-done.20.passing_ref = bf16[512,384]{1,0:T(8,128)(2,1)S(1)} collective-permute-done((bf16[512,384]{1,0:T(8,128)(2,1)S(1)}, bf16[512,384]{1,0:T(8,128)(2,1)S(1)}, u32[]{:S(2)}, u32[]{:S(2)}) %collective-permute-start.20) | collective-permute-done | bytes 393248 | tf_op jit(solution)/shard_map/ppermute | solution.py:51
  135.3 3.9 %all-to-all-start.1 = ((bf16[8,128,384]{2,1,0:T(8,128)(2,1)}), bf16[8,128,384]{2,1,0:T(8,128)(2,1)S(1)}, u32[]{:S(2)}, u32[]{:S(2)}) async-start(bf16[8,128,384]{2,1,0:T(8,128)(2,1)} %bitcast.17), calls=%async_computation.1 | async-start | bytes 1572864 | tf_op jit(solution)/shard_map/all_to_all | solution.py:472
  141.2 3.4 %collective-permute-done.15 = bf16[160,1920]{1,0:T(8,128)(2,1)} collective-permute-done((bf16[160,1920]{1,0:T(8,128)(2,1)}, bf16[160,1920]{1,0:T(8,128)(2,1)}, u32[]{:S(2)}, u32[]{:S(2)}) %collective-permute-start.15) | collective-permute-done | bytes 614432 | tf_op jit(solution)/shard_map/ppermute | solution.py:64
  149.3 4.1 %all-to-all-done.1 = bf16[8,128,384]{2,1,0:T(8,128)(2,1)S(1)} async-done(((bf16[8,128,384]{2,1,0:T(8,128)(2,1)}), bf16[8,128,384]{2,1,0:T(8,128)(2,1)S(1)}, u32[]{:S(2)}, u32[]{:S(2)}) %all-to-all-start.1) | async-done | bytes 786464 | tf_op jit(solution)/shard_map/all_to_all | solution.py:472
  (130 shorter events, 58.8 us)
Async XLA Ops:
  4.6 12.2 %collective-permute-start.3 = (bf16[256,640]{1,0:T(8,128)(2,1)S(1)}, bf16[256,640]{1,0:T(8,128)(2,1)S(1)}, u32[]{:S(2)}, u32[]{:S(2)}) collective-permute-start(bf16[256,640]{1,0:T(8,128)(2,1)S(1)} %reduce_sum.52.refs_0_), channel_id=1, source_target_pairs={{0,2},{2,3},{3,1},{1,0},{4,6},{6,7},{7,5},{5,4},{8,10},{10,11},{11... | collective-permute-start | bytes 983048 | tf_op jit(solution)/shard_map/ppermute | solution.py:51
  8.7 38.8 %copy-start.14 = (bf16[512,2,640]{2,1,0:T(2,128)(2,1)S(1)}, bf16[512,2,640]{2,1,0:T(2,128)(2,1)}, u32[]{:S(2)}) copy-start(bf16[512,2,640]{2,1,0:T(2,128)(2,1)} %param.13) | copy-start | bytes 3932164
  10.4 13.5 %collective-permute-start = (bf16[256,640]{1,0:T(8,128)(2,1)S(1)}, bf16[256,640]{1,0:T(8,128)(2,1)S(1)}, u32[]{:S(2)}, u32[]{:S(2)}) collective-permute-start(bf16[256,640]{1,0:T(8,128)(2,1)S(1)} %reduce_sum.51.refs_0_), channel_id=1, source_target_pairs={{0,2},{2,3},{3,1},{1,0},{4,6},{6,7},{7,5},{5,4},{8,10},{10,11},{11... | collective-permute-start | bytes 983048 | tf_op jit(solution)/shard_map/ppermute | solution.py:51
  20.5 11.6 %collective-permute-start.4 = (bf16[256,640]{1,0:T(8,128)(2,1)S(1)}, bf16[256,640]{1,0:T(8,128)(2,1)}, u32[]{:S(2)}, u32[]{:S(2)}) collective-permute-start(bf16[256,640]{1,0:T(8,128)(2,1)S(1)} %collective-permute-done.3.refs_1_), channel_id=1, source_target_pairs={{0,2},{2,3},{3,1},{1,0},{4,6},{6,7},{7,5},{5,4},{8,10},{10,11},{11... | collective-permute-start | bytes 983048 | tf_op jit(solution)/shard_map/ppermute | solution.py:51
  23.9 15.2 %collective-permute-start.1 = (bf16[256,640]{1,0:T(8,128)(2,1)S(1)}, bf16[256,640]{1,0:T(8,128)(2,1)}, u32[]{:S(2)}, u32[]{:S(2)}) collective-permute-start(bf16[256,640]{1,0:T(8,128)(2,1)S(1)} %collective-permute-done.refs_1_), channel_id=1, source_target_pairs={{0,2},{2,3},{3,1},{1,0},{4,6},{6,7},{7,5},{5,4},{8,10},{10,11},{11... | collective-permute-start | bytes 983048 | tf_op jit(solution)/shard_map/ppermute | solution.py:51
  32.0 25.7 %collective-permute-start.5 = (bf16[256,640]{1,0:T(8,128)(2,1)}, bf16[256,640]{1,0:T(8,128)(2,1)}, u32[]{:S(2)}, u32[]{:S(2)}) collective-permute-start(bf16[256,640]{1,0:T(8,128)(2,1)} %collective-permute-done.4.refs_2_), channel_id=1, source_target_pairs={{0,2},{2,3},{3,1},{1,0},{4,6},{6,7},{7,5},{5,4},{8,10},{10,11},{11... | collective-permute-start | bytes 983048 | tf_op jit(solution)/shard_map/ppermute | solution.py:51
  39.1 23.5 %collective-permute-start.2 = (bf16[256,640]{1,0:T(8,128)(2,1)}, bf16[256,640]{1,0:T(8,128)(2,1)}, u32[]{:S(2)}, u32[]{:S(2)}) collective-permute-start(bf16[256,640]{1,0:T(8,128)(2,1)} %collective-permute-done.1.refs_2_), channel_id=1, source_target_pairs={{0,2},{2,3},{3,1},{1,0},{4,6},{6,7},{7,5},{5,4},{8,10},{10,11},{11... | collective-permute-start | bytes 983048 | tf_op jit(solution)/shard_map/ppermute | solution.py:51
  43.7 8.3 %all-to-all-start = ((s32[8,1,128]{2,1,0:T(1,128)}), s32[8,1,128]{2,1,0:T(1,128)S(1)}, u32[]{:S(2)}, u32[]{:S(2)}) async-start(s32[8,1,128]{2,1,0:T(1,128)} %bitcast.11), calls=%async_computation | async-start | bytes 8192 | tf_op jit(solution)/shard_map/all_to_all | solution.py:412
  47.5 43.1 %copy-start.10 = (s32[16]{0:T(128)}, s32[16]{0:T(128)S(1)}, u32[]{:S(2)}) copy-start(s32[16]{0:T(128)S(1)} %pad_add_fusion.refs_4_.table_ref.plan_ref) | copy-start | bytes 196
  67.3 3.8 %collective-permute-start.8 = (f32[8,512]{1,0:T(8,128)S(1)}, f32[8,512]{1,0:T(8,128)S(1)}, u32[]{:S(2)}, u32[]{:S(2)}) collective-permute-start(f32[8,512]{1,0:T(8,128)S(1)} %get-tuple-element.34.refs_0_), channel_id=1, source_target_pairs={{0,3},{1,0},{2,1},{3,2},{4,7},{5,4},{6,5},{7,6},{8,11},{9,8},{10,9... | collective-permute-start | bytes 49160 | tf_op jit(solution)/shard_map/ppermute | solution.py:57
  68.7 4.6 %collective-permute-start.7 = (f32[8,512]{1,0:T(8,128)S(1)}, f32[8,512]{1,0:T(8,128)S(1)}, u32[]{:S(2)}, u32[]{:S(2)}) collective-permute-start(f32[8,512]{1,0:T(8,128)S(1)} %get-tuple-element.34.refs_0_), channel_id=1, source_target_pairs={{0,2},{1,3},{2,0},{3,1},{4,6},{5,7},{6,4},{7,5},{8,10},{9,11},{10,... | collective-permute-start | bytes 49160 | tf_op jit(solution)/shard_map/ppermute | solution.py:57
  68.7 5.5 %collective-permute-start.6 = (f32[8,512]{1,0:T(8,128)S(1)}, f32[8,512]{1,0:T(8,128)S(1)}, u32[]{:S(2)}, u32[]{:S(2)}) collective-permute-start(f32[8,512]{1,0:T(8,128)S(1)} %get-tuple-element.34.refs_0_), channel_id=1, source_target_pairs={{0,1},{1,2},{2,3},{3,0},{4,5},{5,6},{6,7},{7,4},{8,9},{9,10},{10,1... | collective-permute-start | bytes 49160 | tf_op jit(solution)/shard_map/ppermute | solution.py:57
  75.4 7.8 %collective-permute-start.9 = (bf16[512,1920]{1,0:T(8,128)(2,1)S(1)}, bf16[512,1920]{1,0:T(8,128)(2,1)S(1)}, u32[]{:S(2)}, u32[]{:S(2)}) collective-permute-start(bf16[512,1920]{1,0:T(8,128)(2,1)S(1)} %cotangents.1.joined_ref), channel_id=1, source_target_pairs={{0,4},{4,0},{8,12},{12,8},{16,20},{20,16},{24,28},{28,24},{1,5},{5... | collective-permute-start | bytes 5898248 | tf_op jit(solution)/shard_map/ppermute | solution.py:64
  75.5 5.8 %collective-permute-start.11 = (bf16[2560,256]{1,0:T(8,128)(2,1)S(1)}, bf16[2560,256]{1,0:T(8,128)(2,1)S(1)}, u32[]{:S(2)}, u32[]{:S(2)}) collective-permute-start(bf16[2560,256]{1,0:T(8,128)(2,1)S(1)} %get-tuple-element.38.refs_1_), channel_id=1, source_target_pairs={{0,4},{4,0},{8,12},{12,8},{16,20},{20,16},{24,28},{28,24},{1,5},{5... | collective-permute-start | bytes 3932168 | tf_op jit(solution)/shard_map/ppermute | solution.py:64
  76.0 7.2 %collective-permute-start.10 = (bf16[2560,256]{1,0:T(8,128)(2,1)S(1)}, bf16[2560,256]{1,0:T(8,128)(2,1)S(1)}, u32[]{:S(2)}, u32[]{:S(2)}) collective-permute-start(bf16[2560,256]{1,0:T(8,128)(2,1)S(1)} %get-tuple-element.37.refs_0_), channel_id=1, source_target_pairs={{0,4},{4,0},{8,12},{12,8},{16,20},{20,16},{24,28},{28,24},{1,5},{5... | collective-permute-start | bytes 3932168 | tf_op jit(solution)/shard_map/ppermute | solution.py:64
  78.4 14.6 %collective-permute-start.21 = (bf16[512,256]{1,0:T(8,128)(2,1)S(1)}, bf16[512,256]{1,0:T(8,128)(2,1)S(1)}, u32[]{:S(2)}, u32[]{:S(2)}) collective-permute-start(bf16[512,256]{1,0:T(8,128)(2,1)S(1)} %get-tuple-element.52), channel_id=1, source_target_pairs={{0,2},{2,3},{3,1},{1,0},{4,6},{6,7},{7,5},{5,4},{8,10},{10,11},{11... | collective-permute-start | bytes 786440 | tf_op jit(solution)/shard_map/ppermute | solution.py:51
  86.1 21.8 %collective-permute-start.13 = (bf16[160,1920]{1,0:T(8,128)(2,1)S(1)}, bf16[160,1920]{1,0:T(8,128)(2,1)S(1)}, u32[]{:S(2)}, u32[]{:S(2)}) collective-permute-start(bf16[160,1920]{1,0:T(8,128)(2,1)S(1)} %get-tuple-element.39.refs_4_), channel_id=1, source_target_pairs={{0,8},{4,12},{8,0},{12,4},{16,24},{20,28},{24,16},{28,20},{1,9},{5... | collective-permute-start | bytes 1843208 | tf_op jit(solution)/shard_map/ppermute | solution.py:64
  86.6 12.0 %collective-permute-start.18 = (bf16[512,384]{1,0:T(8,128)(2,1)S(1)}, bf16[512,384]{1,0:T(8,128)(2,1)S(1)}, u32[]{:S(2)}, u32[]{:S(2)}) collective-permute-start(bf16[512,384]{1,0:T(8,128)(2,1)S(1)} %get-tuple-element.49), channel_id=1, source_target_pairs={{0,2},{2,3},{3,1},{1,0},{4,6},{6,7},{7,5},{5,4},{8,10},{10,11},{11... | collective-permute-start | bytes 1179656 | tf_op jit(solution)/shard_map/ppermute | solution.py:51
  93.0 12.2 %collective-permute-start.22 = (bf16[512,256]{1,0:T(8,128)(2,1)S(1)}, bf16[512,256]{1,0:T(8,128)(2,1)S(1)}, u32[]{:S(2)}, u32[]{:S(2)}) collective-permute-start(bf16[512,256]{1,0:T(8,128)(2,1)S(1)} %add.146), channel_id=1, source_target_pairs={{0,2},{2,3},{3,1},{1,0},{4,6},{6,7},{7,5},{5,4},{8,10},{10,11},{11... | collective-permute-start | bytes 786440 | tf_op jit(solution)/shard_map/ppermute | solution.py:51
  93.8 32.4 %collective-permute-start.16 = (bf16[160,1920]{1,0:T(8,128)(2,1)}, bf16[160,1920]{1,0:T(8,128)(2,1)S(1)}, u32[]{:S(2)}, u32[]{:S(2)}) collective-permute-start(bf16[160,1920]{1,0:T(8,128)(2,1)} %get-tuple-element.48), channel_id=1, source_target_pairs={{0,16},{4,20},{8,24},{12,28},{16,0},{20,4},{24,8},{28,12},{1,17},{... | collective-permute-start | bytes 1843208 | tf_op jit(solution)/shard_map/ppermute | solution.py:64
  98.7 23.4 %collective-permute-start.19 = (bf16[512,384]{1,0:T(8,128)(2,1)S(1)}, bf16[512,384]{1,0:T(8,128)(2,1)S(1)}, u32[]{:S(2)}, u32[]{:S(2)}) collective-permute-start(bf16[512,384]{1,0:T(8,128)(2,1)S(1)} %add.144), channel_id=1, source_target_pairs={{0,2},{2,3},{3,1},{1,0},{4,6},{6,7},{7,5},{5,4},{8,10},{10,11},{11... | collective-permute-start | bytes 1179656 | tf_op jit(solution)/shard_map/ppermute | solution.py:51
  105.3 11.8 %collective-permute-start.23 = (bf16[512,256]{1,0:T(8,128)(2,1)S(1)}, bf16[512,256]{1,0:T(8,128)(2,1)S(1)}, u32[]{:S(2)}, u32[]{:S(2)}) collective-permute-start(bf16[512,256]{1,0:T(8,128)(2,1)S(1)} %add.147), channel_id=1, source_target_pairs={{0,2},{2,3},{3,1},{1,0},{4,6},{6,7},{7,5},{5,4},{8,10},{10,11},{11... | collective-permute-start | bytes 786440 | tf_op jit(solution)/shard_map/ppermute | solution.py:51
  106.4 33.2 %collective-permute-start.12 = (bf16[160,1920]{1,0:T(8,128)(2,1)}, bf16[160,1920]{1,0:T(8,128)(2,1)}, u32[]{:S(2)}, u32[]{:S(2)}) collective-permute-start(bf16[160,1920]{1,0:T(8,128)(2,1)} %get-tuple-element.40.refs_0_), channel_id=1, source_target_pairs={{0,8},{4,12},{8,0},{12,4},{16,24},{20,28},{24,16},{28,20},{1,9},{5... | collective-permute-start | bytes 1843208 | tf_op jit(solution)/shard_map/ppermute | solution.py:64
  108.8 30.8 %collective-permute-start.14 = (bf16[160,1920]{1,0:T(8,128)(2,1)}, bf16[160,1920]{1,0:T(8,128)(2,1)}, u32[]{:S(2)}, u32[]{:S(2)}) collective-permute-start(bf16[160,1920]{1,0:T(8,128)(2,1)} %add.142), channel_id=1, source_target_pairs={{0,16},{4,20},{8,24},{12,28},{16,0},{20,4},{24,8},{28,12},{1,17},{... | collective-permute-start | bytes 1843208 | tf_op jit(solution)/shard_map/ppermute | solution.py:64
  118.6 16.8 %all-to-all-start.2 = ((bf16[8,128,256]{2,1,0:T(8,128)(2,1)}), bf16[8,128,256]{2,1,0:T(8,128)(2,1)S(1)}, u32[]{:S(2)}, u32[]{:S(2)}) async-start(bf16[8,128,256]{2,1,0:T(8,128)(2,1)} %bitcast.19), calls=%async_computation.2 | async-start | bytes 1048576 | tf_op jit(solution)/shard_map/all_to_all | solution.py:472
  122.2 11.5 %collective-permute-start.20 = (bf16[512,384]{1,0:T(8,128)(2,1)S(1)}, bf16[512,384]{1,0:T(8,128)(2,1)S(1)}, u32[]{:S(2)}, u32[]{:S(2)}) collective-permute-start(bf16[512,384]{1,0:T(8,128)(2,1)S(1)} %add.145), channel_id=1, source_target_pairs={{0,2},{2,3},{3,1},{1,0},{4,6},{6,7},{7,5},{5,4},{8,10},{10,11},{11... | collective-permute-start | bytes 1179656 | tf_op jit(solution)/shard_map/ppermute | solution.py:51
  124.3 20.3 %collective-permute-start.15 = (bf16[160,1920]{1,0:T(8,128)(2,1)}, bf16[160,1920]{1,0:T(8,128)(2,1)}, u32[]{:S(2)}, u32[]{:S(2)}) collective-permute-start(bf16[160,1920]{1,0:T(8,128)(2,1)} %copy-done.12), channel_id=1, source_target_pairs={{0,16},{4,20},{8,24},{12,28},{16,0},{20,4},{24,8},{28,12},{1,17},{... | collective-permute-start | bytes 1843208 | tf_op jit(solution)/shard_map/ppermute | solution.py:64
  127.2 17.4 %collective-permute-start.17 = (bf16[160,1920]{1,0:T(8,128)(2,1)}, bf16[160,1920]{1,0:T(8,128)(2,1)}, u32[]{:S(2)}, u32[]{:S(2)}) collective-permute-start(bf16[160,1920]{1,0:T(8,128)(2,1)} %add.143), channel_id=1, source_target_pairs={{0,8},{4,12},{8,0},{12,4},{16,24},{20,28},{24,16},{28,20},{1,9},{5... | collective-permute-start | bytes 1843208 | tf_op jit(solution)/shard_map/ppermute | solution.py:64
  135.3 18.1 %all-to-all-start.1 = ((bf16[8,128,384]{2,1,0:T(8,128)(2,1)}), bf16[8,128,384]{2,1,0:T(8,128)(2,1)S(1)}, u32[]{:S(2)}, u32[]{:S(2)}) async-start(bf16[8,128,384]{2,1,0:T(8,128)(2,1)} %bitcast.17), calls=%async_computation.1 | async-start | bytes 1572864 | tf_op jit(solution)/shard_map/all_to_all | solution.py:472
  154.0 4.2 %collective-permute-start.26 = (f32[256]{0:T(256)S(1)}, f32[256]{0:T(256)S(1)}, u32[]{:S(2)}, u32[]{:S(2)}) collective-permute-start(f32[256]{0:T(256)S(1)} %add_reduce_fusion), channel_id=1, source_target_pairs={{0,3},{1,0},{2,1},{3,2},{4,7},{5,4},{6,5},{7,6},{8,11},{9,8},{10,9... | collective-permute-start | bytes 3080 | tf_op jit(solution)/shard_map/ppermute | solution.py:57
  155.3 4.5 %collective-permute-start.25 = (f32[256]{0:T(256)S(1)}, f32[256]{0:T(256)S(1)}, u32[]{:S(2)}, u32[]{:S(2)}) collective-permute-start(f32[256]{0:T(256)S(1)} %add_reduce_fusion), channel_id=1, source_target_pairs={{0,2},{1,3},{2,0},{3,1},{4,6},{5,7},{6,4},{7,5},{8,10},{9,11},{10,... | collective-permute-start | bytes 3080 | tf_op jit(solution)/shard_map/ppermute | solution.py:57
  156.2 5.4 %collective-permute-start.24 = (f32[256]{0:T(256)S(1)}, f32[256]{0:T(256)S(1)}, u32[]{:S(2)}, u32[]{:S(2)}) collective-permute-start(f32[256]{0:T(256)S(1)} %add_reduce_fusion), channel_id=1, source_target_pairs={{0,1},{1,2},{2,3},{3,0},{4,5},{5,6},{6,7},{7,4},{8,9},{9,10},{10,1... | collective-permute-start | bytes 3080 | tf_op jit(solution)/shard_map/ppermute | solution.py:57
  (20 other events, 138.0 us)

commit v3 on v2

v3 whole, which is shorter than its diff:
```python
import functools

import jax
import jax.numpy as jnp
import numpy as np
from jax import lax
from jax.experimental import pallas as pl
from jax.experimental.pallas import tpu as pltpu
from jax.sharding import PartitionSpec as P

CAP = 128
SCALE = 10
HALVES = 2
VMEM_BYTES = 20 * 1024 * 1024


EPS_NORM = 1e-06
EPS_ADAM = 1e-08
FIRST_BIAS = 1.0 - 0.9**10
SECOND_BIAS = 1.0 - 0.95**10

F32, BF16 = jnp.float32, jnp.bfloat16


VMEM = pl.BlockSpec(memory_space=pltpu.VMEM)
SMEM = pl.BlockSpec(memory_space=pltpu.SMEM)
ANY = pl.BlockSpec(memory_space=pl.ANY)
NT = (((1,), (1,)), ((), ()))


def call(kernel, name, in_specs, out_shape, args, macs=0, scratch=(), aliases=None, after=()):
    count = len(args)

    def body(*refs):
        kernel(*refs[:count], *refs[count + len(after) :])

    return pl.pallas_call(
        body,
        in_specs=in_specs + [ANY] * len(after),
        out_specs=[VMEM] * len(out_shape),
        out_shape=out_shape,
        scratch_shapes=scratch,
        input_output_aliases=aliases or {},
        compiler_params=pltpu.CompilerParams(vmem_limit_bytes=VMEM_BYTES),
        cost_estimate=pl.CostEstimate(flops=macs // SCALE, bytes_accessed=0, transcendentals=0),
        name=name,
    )(*args, *after)


def ring_order(size):
    return list(range(0, size, 2)) + list(range(1, size, 2))[::-1]


def ring_pass(part, axis):
    size = lax.axis_size(axis)
    order = ring_order(size)
    return lax.ppermute(part, axis, [(order[i], order[(i + 1) % size]) for i in range(size)])


def others_over(axis, part):
    size = lax.axis_size(axis)
    return [
        lax.ppermute(part, axis, [(i, i ^ step) for i in range(size)])
        for step in range(1, size)
    ]


def swap_over(axis, bit, part):
    size = lax.axis_size(axis)
    return lax.ppermute(part, axis, [(i, i ^ bit) for i in range(size)])


def after_kernel(*refs):
    del refs


def after(x, *others):
    return pl.pallas_call(
        after_kernel,
        in_specs=[ANY] * (1 + len(others)),
        out_specs=ANY,
        out_shape=jax.ShapeDtypeStruct(x.shape, x.dtype),
        input_output_aliases={0: 0},
        compiler_params=pltpu.CompilerParams(vmem_limit_bytes=1024 * 1024),
        name="after",
    )(x, *others)


def weight_block(ref, rows, j, width):
    if len(ref.shape) == 2:
        return ref[rows, j * width : (j + 1) * width]
    return ref[j, rows]


def join_kernel(plan_ref, key_ref, value_ref, out_ref, sems):
    key_count, model_width, width = key_ref.shape
    copies = []
    for step in range(model_width // width):
        source_rows = pl.ds(pl.multiple_of(plan_ref[step] * width, width), width)
        rows = pl.ds(step * width, width)
        for j in range(key_count + 1):
            source = key_ref.at[j, source_rows, :] if j < key_count else value_ref.at[source_rows, :]
            if len(out_ref.shape) == 2:
                target = out_ref.at[rows, pl.ds(j * width, width)]
            else:
                target = out_ref.at[j, rows, :]
            copies.append(pltpu.make_async_copy(source, target, sems.at[step, j]))
            copies[-1].start()
    for copy in copies:
        copy.wait()


def join_weights(plan, key_weight, value_weight, after):
    key_count, model_width, width = key_weight.shape
    flat = width % 128 == 0
    shape = (model_width, (key_count + 1) * width) if flat else (key_count + 1, model_width, width)
    return call(
        join_kernel,
        "join_weights",
        [SMEM] + [ANY] * 2,
        [jax.ShapeDtypeStruct(shape, BF16)],
        [plan, key_weight, value_weight],
        scratch=[pltpu.SemaphoreType.DMA((model_width // width, key_count + 1))],
        after=after,
    )[0]


def partial_products(parts, weight_ref, first, j):
    width = parts[0].shape[1]
    if len(weight_ref.shape) == 2:
        rows = slice(first * width, (first + len(parts)) * width)
        whole = jnp.concatenate(parts, axis=1) if len(parts) > 1 else parts[0]
        weight = weight_block(weight_ref, rows, j, width)
        return jnp.dot(whole, weight, preferred_element_type=F32)
    return sum(
        jnp.dot(
            part,
            weight_block(weight_ref, slice((first + k) * width, (first + k + 1) * width), j, width),
            preferred_element_type=F32,
        )
        for k, part in enumerate(parts)
    )


def early_kernel(steps, plan_ref, weight_ref, *refs):
    *part_refs, acc_ref, turned_ref = refs
    width = acc_ref.shape[2]
    parts = [
        jnp.concatenate([part_refs[h * steps + step][...] for h in range(HALVES)], axis=0)
        for step in range(steps)
    ]
    for j in range(acc_ref.shape[0]):
        acc_ref[j] = partial_products(parts, weight_ref, 0, j)
    for step in range(steps):
        turned_ref[pl.ds(pl.multiple_of(plan_ref[step] * width, width), width), :] = parts[step].T


def forward_early(plan, weights, chains, key_count):
    steps = len(chains[0])
    half, width = chains[0][0].shape
    tok_count = half * HALVES
    return call(
        functools.partial(early_kernel, steps),
        "forward_early",
        [SMEM] + [VMEM] * (1 + HALVES * steps),
        [
            jax.ShapeDtypeStruct((key_count + 1, tok_count, width), F32),
            jax.ShapeDtypeStruct((weights.shape[-2], tok_count), BF16),
        ],
        [plan, weights] + [part for chain in chains for part in chain],
        macs=tok_count * steps * width * width * (key_count + 1),
    )


def late_kernel(step, plan_ref, weight_ref, *refs):
    part_refs, refs = refs[:HALVES], refs[HALVES:]
    acc_ref, _, state_ref, grad_ref, val_ref, turned_ref, sum_ref = refs
    key_count, tok_count, width = state_ref.shape
    part = jnp.concatenate([ref[...] for ref in part_refs], axis=0)
    row_sum = lambda x: jnp.sum(x, axis=1, keepdims=True)
    sums = [None] * (4 * key_count)
    for j in range(key_count + 1):
        val = acc_ref[j] + partial_products([part], weight_ref, step, j)
        if j == key_count:
            for k in range(key_count):
                sums[3 * key_count + k] = row_sum(grad_ref[k].astype(F32) * val)
            continue
        val_ref[j] = val
        state = state_ref[j].astype(F32)
        sums[j] = row_sum(state * state)
        sums[key_count + j] = row_sum(val * val)
        sums[2 * key_count + j] = row_sum(state * val)
    lane = lax.broadcasted_iota(jnp.int32, (tok_count, 128), 1)
    table = jnp.zeros((tok_count, 128), F32)
    for i, s in enumerate(sums):
        table = jnp.where(lane == i, s, table)
    sum_ref[...] = table.T[: 4 * key_count]
    turned_ref[pl.ds(pl.multiple_of(plan_ref[step] * width, width), width), :] = part.T


def forward_late(plan, weights, parts, acc, turned, states, grads):
    key_count, tok_count, width = states.shape
    return call(
        functools.partial(late_kernel, weights.shape[-2] // width - 1),
        "forward_late",
        [SMEM] + [VMEM] * (5 + HALVES),
        [
            jax.ShapeDtypeStruct(acc.shape, F32),
            jax.ShapeDtypeStruct(turned.shape, BF16),
            jax.ShapeDtypeStruct((4 * key_count, tok_count), F32),
        ],
        [plan, weights, *parts, acc, turned, states, grads],
        macs=tok_count * width * width * (key_count + 1),
        aliases={2 + HALVES: 0, 3 + HALVES: 1},
    )


def cot_kernel(sums_count, model_width, *refs):
    sum_refs, refs = refs[:sums_count], refs[sums_count:]
    val_ref, state_ref, grad_ref, joined_ref = refs
    key_count, tok_count, width = state_ref.shape
    half = tok_count // HALVES
    total = sum_refs[0][...]
    for ref in sum_refs[1:]:
        total = total + ref[...]
    root_width = jnp.sqrt(F32(model_width))
    state_sum, key_sum, cross_dot, out_dot = (
        total[i * key_count : (i + 1) * key_count] for i in range(4)
    )
    state_rs = lax.rsqrt(state_sum / model_width + EPS_NORM)
    key_rs = lax.rsqrt(key_sum / model_width + EPS_NORM)
    scores = cross_dot * state_rs * key_rs / root_width
    gate_val = 1.0 / (1.0 + jnp.exp(-scores))
    dscore = out_dot * gate_val * (1.0 - gate_val)
    lead = key_rs * dscore / root_width
    slope = key_rs * scores / root_width
    factors = jnp.concatenate([lead, state_rs, slope, gate_val], axis=0)
    filler = jnp.zeros((128 - 4 * key_count, half), F32)
    for h in range(HALVES):
        rows = slice(h * half, (h + 1) * half)
        table = jnp.concatenate([factors[:, rows], filler], axis=0).T
        column = lambda kind, j: table[:, kind * key_count + j : kind * key_count + j + 1]
        value_cot = None
        for j in range(key_count):
            state = state_ref[j, rows].astype(F32)
            inner = state * column(1, j) - val_ref[j, rows] * column(2, j)
            joined_ref[rows, j * width : (j + 1) * width] = (column(0, j) * inner).astype(BF16)
            gated = column(3, j) * grad_ref[j, rows].astype(F32)
            value_cot = gated if value_cot is None else value_cot + gated
        joined_ref[rows, key_count * width :] = value_cot.astype(BF16)


def cotangents(sums, vals, states, grads, model_width, after):
    key_count, tok_count, width = states.shape
    return call(
        functools.partial(cot_kernel, len(sums), model_width),
        "cotangents",
        [VMEM] * (len(sums) + 3),
        [jax.ShapeDtypeStruct((tok_count, (key_count + 1) * width), BF16)],
        [*sums, vals, states, grads],
        macs=tok_count * width,
        after=after,
    )[0]


def back_kernel(step, joined_ref, weight_ref, *refs):
    width = sum(ref.shape[1] for ref in refs)
    rows = slice(step * width, (step + 1) * width)
    if len(weight_ref.shape) == 2:
        term = lax.dot_general(
            joined_ref[...], weight_ref[rows], NT, preferred_element_type=F32
        )
    else:
        term = sum(
            lax.dot_general(
                joined_ref[:, j * width : (j + 1) * width],
                weight_ref[j, rows],
                NT,
                preferred_element_type=F32,
            )
            for j in range(weight_ref.shape[0])
        )
    start = 0
    for ref in refs:
        ref[...] = term[:, start : start + ref.shape[1]].astype(BF16)
        start += ref.shape[1]


def back(step, joined, weights, cuts, after=()):
    tok_count, columns = joined.shape
    return call(
        functools.partial(back_kernel, step),
        "back",
        [VMEM] * 2,
        [jax.ShapeDtypeStruct((tok_count, cut), BF16) for cut in cuts],
        [joined, weights],
        macs=tok_count * columns * sum(cuts),
        after=after,
    )


def outer_kernel(
    entry, plan_ref, joined_ref, other_joined_ref, turned_ref, other_turned_ref, *refs
):
    rows = sum(ref.shape[0] for ref in refs)
    block = pl.ds(pl.multiple_of(plan_ref[entry] * rows, rows), rows)
    product = jnp.dot(turned_ref[block, :], joined_ref[...], preferred_element_type=F32)
    product = product + jnp.dot(
        other_turned_ref[block, :], other_joined_ref[...], preferred_element_type=F32
    )
    start = 0
    for ref in refs:
        ref[...] = product[start : start + ref.shape[0]].astype(BF16)
        start += ref.shape[0]


def outer(entry, plan, rows, joined, other_joined, turned, other_turned, after=()):
    tok_count, columns = joined.shape
    return call(
        functools.partial(outer_kernel, entry),
        "outer",
        [SMEM] + [VMEM] * 4,
        [jax.ShapeDtypeStruct((r, columns), BF16) for r in (rows // 2, rows - rows // 2)],
        [plan, joined, other_joined, turned, other_turned],
        macs=2 * rows * tok_count * columns,
        after=after,
    )


def route_kernel(owned_rows, row_ref, slot_ref, out_ref):
    grams, tok_count = row_ref.shape
    groups = out_ref.shape[0]
    nt = functools.partial(lax.dot_general, dimension_numbers=NT, preferred_element_type=F32)
    flag = lambda x: x.astype(F32).astype(BF16)
    before = lax.broadcasted_iota(jnp.int32, (tok_count, tok_count), 0)
    before = flag(before <= lax.broadcasted_iota(jnp.int32, (tok_count, tok_count), 1))
    owners = lax.broadcasted_iota(jnp.int32, (groups, tok_count), 0)
    slots = lax.broadcasted_iota(jnp.int32, (groups * CAP, tok_count), 0)
    taken = jnp.zeros((groups, 1), F32)
    held = jnp.zeros((16, groups * CAP), F32)
    for n in range(grams):
        row = row_ref[n : n + 1, :]
        owner = row // owned_rows
        mine = owners == owner
        count = jnp.dot(flag(mine), before, preferred_element_type=F32) + taken
        taken = count[:, tok_count - 1 :]
        place = jnp.sum(jnp.where(mine, count, 0.0), axis=0, keepdims=True).astype(jnp.int32) - 1
        slot = owner * CAP + place
        slot_ref[n : n + 1, :] = slot
        local = row - owner * owned_rows + 1
        digits = jnp.concatenate([local // 128, local % 128], axis=0).astype(F32)
        digits = jnp.concatenate([digits, jnp.zeros((14, tok_count), F32)], axis=0).astype(BF16)
        held = held + nt(digits, flag(slots == slot))
    found = (held[0:1] * 128.0 + held[1:2]).astype(jnp.int32)
    for group in range(groups):
        out_ref[group : group + 1, :] = found[:, group * CAP : (group + 1) * CAP]


def route(rows, owned_rows, groups, after=()):
    return call(
        functools.partial(route_kernel, owned_rows),
        "route",
        [VMEM],
        [
            jax.ShapeDtypeStruct(rows.shape, jnp.int32),
            jax.ShapeDtypeStruct((groups, CAP), jnp.int32),
        ],
        [rows],
        macs=rows.size * rows.shape[1],
        after=after,
    )


def memory_kernel(h, rows_ref, out_ref):
    half = out_ref.shape[0]
    part = slice(h * half, (h + 1) * half)
    total = rows_ref[0, part].astype(F32)
    for n in range(1, rows_ref.shape[0]):
        total = total + rows_ref[n, part].astype(F32)
    out_ref[...] = total.astype(BF16)


def sum_rows(h, rows, after):
    _, tok_count, width = rows.shape
    return call(
        functools.partial(memory_kernel, h),
        "sum_rows",
        [VMEM],
        [jax.ShapeDtypeStruct((tok_count // HALVES, width), BF16)],
        [rows],
        macs=tok_count * width,
        after=after,
    )[0]


def sum_kernel(*refs):
    total = refs[0][...].astype(F32)
    for ref in refs[1:-1]:
        total = total + ref[...].astype(F32)
    refs[-1][...] = total.astype(refs[-1].dtype)


def add(*parts, after=(), dtype=BF16):
    return call(
        sum_kernel,
        "add",
        [VMEM] * len(parts),
        [jax.ShapeDtypeStruct(parts[0].shape, dtype)],
        parts,
        macs=parts[0].size,
        after=after,
    )[0]


def part_kernel(start, whole_ref, part_ref, out_ref):
    whole = whole_ref[:, start : start + part_ref.shape[1]]
    out_ref[...] = (whole.astype(F32) + part_ref[...].astype(F32)).astype(BF16)


def add_part(whole, part, start, after=()):
    return call(
        functools.partial(part_kernel, start),
        "add_part",
        [VMEM] * 2,
        [jax.ShapeDtypeStruct(part.shape, BF16)],
        [whole, part],
        macs=part.size,
        after=after,
    )[0]


def mark_kernel(slot_ref, out_ref):
    slots = lax.broadcasted_iota(jnp.int32, out_ref.shape, 0)
    marks = sum((slots == slot_ref[n : n + 1, :]).astype(F32) for n in range(slot_ref.shape[0]))
    out_ref[...] = marks.astype(BF16)


def mark_slots(slot_index, slot_count, after=()):
    return call(
        mark_kernel,
        "mark_slots",
        [VMEM],
        [jax.ShapeDtypeStruct((slot_count, slot_index.shape[1]), BF16)],
        [slot_index],
        macs=slot_count * slot_index.shape[1],
        after=after,
    )[0]


def pick_kernel(mark_ref, *refs):
    *refs, out_ref = refs
    count = len(refs) // 2
    start = 0
    for passing_ref, term_ref in zip(refs[:count], refs[count:]):
        total = (passing_ref[...].astype(F32) + term_ref[...].astype(F32)).astype(BF16)
        columns = slice(start, start + total.shape[1])
        product = jnp.dot(mark_ref[...], total, preferred_element_type=F32)
        out_ref[:, columns] = product.astype(BF16)
        start += total.shape[1]


def pick_rows(marks, passing, terms, after=()):
    slot_count, tok_count = marks.shape
    width = sum(part.shape[1] for part in passing)
    return call(
        pick_kernel,
        "pick_rows",
        [VMEM] * (1 + 2 * len(passing)),
        [jax.ShapeDtypeStruct((slot_count, width), BF16)],
        [marks, *passing, *terms],
        macs=slot_count * tok_count * width,
        after=after,
    )[0]


def place_kernel(row_ref, incoming_ref, grad_ref, sum_ref):
    rows = lax.broadcasted_iota(jnp.int32, (grad_ref.shape[0], row_ref.shape[1]), 0) + 1
    place = (rows == row_ref[...]).astype(F32).astype(BF16)
    grad = jnp.dot(place, incoming_ref[...], preferred_element_type=F32)
    grad_ref[...] = grad
    sums = jnp.sum(grad * grad, axis=1, keepdims=True)
    sum_ref[...] = jnp.broadcast_to(sums, (sums.shape[0], 128)).T[:1]


def place_rows(incoming_rows, incoming, owned_rows, after=()):
    cut = incoming.shape[1]
    return call(
        place_kernel,
        "place_rows",
        [VMEM] * 2,
        [
            jax.ShapeDtypeStruct((owned_rows, cut), F32),
            jax.ShapeDtypeStruct((1, owned_rows), F32),
        ],
        [incoming_rows, incoming],
        macs=incoming.size * owned_rows,
        after=after,
    )


def adam_kernel(model_width, tier_ref, mean_ref, second_ref, grad_ref, *refs):
    *sum_refs, new_mean_ref, new_second_ref, step_ref = refs
    row_sum = sum_refs[0][...]
    for ref in sum_refs[1:]:
        row_sum = row_sum + ref[...]
    scale = lax.rsqrt(row_sum / model_width + EPS_NORM)
    hot = (tier_ref[...] == 1).astype(F32)
    filler = jnp.zeros((126, scale.shape[1]), F32)
    table = jnp.concatenate([scale, hot, filler], axis=0).T
    is_hot = table[:, 1:2] > 0.5
    grad = grad_ref[...]
    mean_hot = 0.9 * mean_ref[...] + 0.1 * grad
    second_hot = 0.95 * second_ref[...] + 0.05 * grad * grad
    step_hot = mean_hot / FIRST_BIAS / (jnp.sqrt(second_hot / SECOND_BIAS) + EPS_ADAM)
    new_mean_ref[...] = jnp.where(is_hot, mean_hot, mean_ref[...])
    new_second_ref[...] = jnp.where(is_hot, second_hot, second_ref[...])
    step_ref[...] = jnp.where(is_hot, step_hot, grad * table[:, :1])


def adam(model_width, row_tier, adam_mean, adam_second, row_grad, row_sums):
    owned_rows, width = row_grad.shape
    tile = 128 if owned_rows % 128 == 0 else owned_rows
    rows = pl.BlockSpec((tile, width), lambda i: (i, 0))
    lanes = pl.BlockSpec((1, tile), lambda i: (0, i))
    return pl.pallas_call(
        functools.partial(adam_kernel, model_width),
        grid=(owned_rows // tile,),
        in_specs=[lanes] + [rows] * 3 + [lanes] * len(row_sums),
        out_specs=[rows] * 3,
        out_shape=[jax.ShapeDtypeStruct((owned_rows, width), F32)] * 3,
        compiler_params=pltpu.CompilerParams(vmem_limit_bytes=VMEM_BYTES),
        cost_estimate=pl.CostEstimate(flops=row_grad.size, bytes_accessed=0, transcendentals=0),
        name="adam",
    )(row_tier.reshape(1, -1), adam_mean, adam_second, row_grad, *row_sums)


def on_device(
    retrieved,
    branch_states,
    out_grad,
    key_weight,
    value_weight,
    key_grad_acc,
    value_grad_acc,
    row_index,
    row_tier,
    adam_mean,
    adam_second,
):
    tok_count, key_count, width = branch_states.shape
    groups = lax.axis_size("group")
    shards = lax.axis_size("tensor")
    model_width = width * shards
    owned_rows = adam_mean.shape[0]
    half = tok_count // HALVES
    me = lax.axis_index("group")
    line = lax.axis_index("tensor")
    order = ring_order(shards)
    behind = np.zeros((shards, shards), np.int32)
    for spot, device in enumerate(order):
        behind[device] = [order[(spot - step) % shards] for step in range(shards)]
    plan = jnp.concatenate(
        [
            lax.dynamic_index_in_dim(jnp.asarray(behind), line, 0, False),
            jnp.arange(groups, dtype=jnp.int32) ^ me,
        ]
    )

    by_row = lambda x: lax.optimization_barrier(jnp.transpose(x, (1, 0, 2)))
    rows = by_row(retrieved)
    chains = []
    for h in range(HALVES):
        chains.append([sum_rows(h, rows, chains[-1] if chains else ())])
    states, grads, _ = lax.optimization_barrier((branch_states, out_grad, chains[-1][0]))
    states, grads = by_row(states), by_row(grads)
    for step in range(shards - 1):
        if step == min(1, shards - 2):
            slot_index, slot_row = route(
                row_index.T, owned_rows, groups, (chains[-1][0], states, grads)
            )
            incoming_rows = lax.all_to_all(
                slot_row, "group", split_axis=0, concat_axis=0, tiled=True
            ).reshape(1, -1)
            chains[0][-1] = after(chains[0][-1], incoming_rows)
        for chain in chains:
            if step == shards - 2 and chain is chains[-1]:
                weights = join_weights(
                    plan, key_weight, value_weight, (incoming_rows, states, grads)
                )
                chain[-1] = after(chain[-1], weights)
            chain.append(ring_pass(chain[-1], "tensor"))
    acc, turned = forward_early(plan, weights, [chain[:-1] for chain in chains], key_count)
    vals, turned, sums = forward_late(
        plan, weights, [chain[-1] for chain in chains], acc, turned, states, grads
    )
    other_turned = swap_over("group", 1, turned)
    sums = [sums] + others_over("tensor", sums)

    lanes = -(-width // 256) * 128
    cuts = [lanes, width - lanes] if width > lanes else [width]
    joined = cotangents(sums, vals, states, grads, model_width, (other_turned,))
    other_joined = swap_over("group", 1, joined)
    first_term = back(1 % shards, joined, weights, [width])
    passing = [ring_pass(first_term[0], "tensor")]

    shard_rows = model_width // groups
    bits = [1 << k for k in range(1, groups.bit_length() - 1)]
    ways = [bits, bits[::-1]]
    mine, arrived, last, turns = [[], []], {}, (first_term[0],), 0

    def send(way, rel, part):
        bit = next(bit for bit in ways[way] if rel & bit)
        got = swap_over("group", bit, part)
        if rel == bit:
            mine[way].append(got)
        else:
            arrived.setdefault((way, rel ^ bit), []).append(got)

    def in_order(kernel, *args, **more):
        nonlocal last
        result = kernel(*args, after=last, **more)
        last = (result[0] if isinstance(result, (list, tuple)) else result,)
        return result

    def turn(between=()):
        nonlocal turns
        term = in_order(back, (turns + 2) % shards, joined, weights, cuts)
        parts = passing if len(passing) == len(cuts) else passing * len(cuts)
        start = 0
        for k, cut in enumerate(cuts):
            parts[k] = ring_pass(in_order(add_part, parts[k], term[k], start if parts is not passing else 0), "tensor")
            start += cut
            if k < len(between):
                between[k]()
        passing[:] = parts
        turns += 1

    def early_sum(way):
        early = in_order(add, *mine[way][:-1], dtype=F32)
        mine[way] = [early, mine[way][-1]]

    for level in range(len(bits), -1, -1):
        waiting = []
        for rel in range(0, groups, 2):
            if bin(rel).count("1") != level:
                continue
            follows = rel != groups - 2
            product = in_order(
                outer, shards + rel, plan, shard_rows, joined, other_joined, turned, other_turned
            )
            for way in range(2):
                if rel == 0:
                    mine[way].insert(0, product[way])
                elif (way, rel) in arrived:
                    waiting.append((way, rel, product[way]))
                else:
                    send(way, rel, product[way])
            if follows and rel and turns < shards - 3:
                turn()
        for way, rel, part in waiting:
            send(way, rel, in_order(add, part, *arrived.pop((way, rel))))
    own_term = in_order(back, 0, joined, weights, cuts)
    marks = in_order(mark_slots, slot_index, groups * CAP)
    sums_to_do = [functools.partial(early_sum, way) for way in range(2)]
    while turns < shards - 2:
        turn(sums_to_do if True else ())
        sums_to_do = () if True else sums_to_do
    weight_sum = jnp.concatenate([sum(p.astype(F32) for p in parts) for parts in mine], axis=0)
    key_grad = key_grad_acc + jnp.stack(
        [weight_sum[:, j * width : (j + 1) * width] for j in range(key_count)]
    )
    value_grad = value_grad_acc + weight_sum[:, key_count * width :]

    outgoing = pick_rows(marks, passing, own_term)
    incoming = lax.all_to_all(
        outgoing.reshape(groups, CAP, -1), "group", split_axis=0, concat_axis=0, tiled=True
    ).reshape(groups * CAP, -1)
    row_grad, row_part = place_rows(
        incoming_rows, incoming, owned_rows, (key_grad, value_grad)
    )
    row_sums = [row_part] + others_over("tensor", row_part)
    new_mean, new_second, row_step = adam(
        model_width, row_tier, adam_mean, adam_second, row_grad, row_sums
    )
    return (key_grad, value_grad, new_mean, new_second, row_step)


def solution(mesh):
    return jax.shard_map(
        on_device,
        mesh=mesh,
        in_specs=(
            P("group", None, "tensor"),
            P("group", None, "tensor"),
            P("group", None, "tensor"),
            P(None, None, "tensor"),
            P(None, "tensor"),
            P(None, "group", "tensor"),
            P("group", "tensor"),
            P("group", None),
            P("group"),
            P("group", "tensor"),
            P("group", "tensor"),
        ),
        out_specs=(
            P(None, "group", "tensor"),
            P("group", "tensor"),
            P("group", "tensor"),
            P("group", "tensor"),
            P("group", "tensor"),
        ),
        check_vma=False,
    )
```

time: 164 us -> 147 us (0.90)
  other arithmetic: 15.3 us -> 3.83 us
  starting transfers between devices: 51.7 us -> 46.9 us
    all_to_all x2 -> x1, waiting for transfers between devices: 4.09 us -> 13.6 us  [on_device(): lax.all_to_all(outgoing.reshape(groups, CAP, -1), 'group', split_axis=0,...]
    ppermute x9 -> x8, waiting for transfers between devices: 7.06 us -> 0.46 us  [swap_over(): return lax.ppermute(part, axis, [(i, i ^ bit) for i in range(size)])]
    ppermute x12 -> x11, starting transfers between devices: 27.3 us -> 23.1 us  [ring_pass(): lax.ppermute(part, axis, [(order[i], order[(i + 1) % size]) for i in rang...]
    reduce_sum x4 -> x0, other arithmetic: 4.05 us -> none  [the longest x2 3.47 us: on_device(): chains.append([jnp.sum(rows.astype(F32), axis=0).astype(BF16)])]
    all_to_all x2 -> x1, starting transfers between devices: 7.37 us -> 3.72 us  [on_device(): lax.all_to_all(outgoing.reshape(groups, CAP, -1), 'group', split_axis=0,...]
    ppermute x6, starting transfers between devices: 6.16 us -> 8.88 us  [others_over(): lax.ppermute(part, axis, [(i, i ^ step) for i in range(size)])]
    another operation x2 -> x0, other arithmetic: 2.43 us -> none
    transpose x1, local copies, waits for them, and re-layouts: 2.19 us -> 0.33 us  [on_device(): by_row = lambda x: lax.optimization_barrier(jnp.transpose(x, (1, 0, 2)))]
  transfers between devices with their start and end apart: 30 -> 27, of which waited for: 16 -> 14; matrix products, arithmetic and copies ran while one was open for 8% -> 3% of each run, Pallas kernels for 19% -> 20%
where the time goes in v3:
time: 147 us
  waiting for transfers between devices  48.1 us (33%)
  starting transfers between devices  46.9 us (32%)
  Pallas kernels  36.8 us (25%)
  local copies, waits for them, and re-layouts  10.3 us (7%)
  other arithmetic  3.83 us (3%)
    pallas_call x26, Pallas kernels, call(): pl.pallas_call(body, in_specs=in_specs + [ANY] * len(after), out_specs=[V...  35.1 us
    ppermute x11, starting transfers between devices, ring_pass(): lax.ppermute(part, axis, [(order[i], order[(i + 1) % size]) for i in rang...  23.1 us
    ppermute x11, waiting for transfers between devices, ring_pass(): lax.ppermute(part, axis, [(order[i], order[(i + 1) % size]) for i in rang...  22.9 us
    all_to_all x1, waiting for transfers between devices, on_device(): lax.all_to_all(outgoing.reshape(groups, CAP, -1), 'group', split_axis=0,...  13.6 us
    unnamed x29, local copies, waits for them, and re-layouts  9.28 us
    ppermute x6, starting transfers between devices, others_over(): lax.ppermute(part, axis, [(i, i ^ step) for i in range(size)])  8.88 us
    ppermute x8, starting transfers between devices, swap_over(): return lax.ppermute(part, axis, [(i, i ^ bit) for i in range(size)])  7.51 us
    ppermute x6, waiting for transfers between devices, others_over(): lax.ppermute(part, axis, [(i, i ^ step) for i in range(size)])  6.54 us
  transfers between devices with their start and end apart: 27, of which 14 were waited for; matrix products, arithmetic and copies ran while one was open for 3% of the time, Pallas kernels for 20%

profile of v3, /device:TPU:0, one launch (start us, length us, event | category | flops | bytes accessed | tf_op | source)
XLA Modules:
  0.0 146.9 jit_solution(8474563150645161452)
XLA Ops:
  2.2 4.1 %collective-permute-start = (bf16[256,640]{1,0:T(8,128)(2,1)S(1)}, bf16[256,640]{1,0:T(8,128)(2,1)}, u32[]{:S(2)}, u32[]{:S(2)}) collective-permute-start(bf16[256,640]{1,0:T(8,128)(2,1)S(1)} %sum_rows.2.refs_1_.refs_2_), channel_id=1, source_target_pairs={{0,2},{2,3},{3,1},{1,0},{4,6},{6,7},{7,5},{5,4},{8,10},{10,11},{11... | collective-permute-start | bytes 983048 | tf_op jit(solution)/shard_map/ppermute | solution.py:57
  9.9 3.7 %all-to-all-start = ((s32[8,1,128]{2,1,0:T(1,128)}), s32[8,1,128]{2,1,0:T(1,128)S(1)}, u32[]{:S(2)}, u32[]{:S(2)}) async-start(s32[8,1,128]{2,1,0:T(1,128)} %bitcast.6), calls=%async_computation | async-start | bytes 8192 | tf_op jit(solution)/shard_map/all_to_all | solution.py:581
  13.6 4.6 %all-to-all-done = s32[8,1,128]{2,1,0:T(1,128)S(1)} async-done(((s32[8,1,128]{2,1,0:T(1,128)}), s32[8,1,128]{2,1,0:T(1,128)S(1)}, u32[]{:S(2)}, u32[]{:S(2)}) %all-to-all-start) | async-done | bytes 4128 | tf_op jit(solution)/shard_map/all_to_all | solution.py:581
  18.6 2.9 %collective-permute-done.3.refs_6_ = bf16[256,640]{1,0:T(8,128)(2,1)} collective-permute-done((bf16[256,640]{1,0:T(8,128)(2,1)S(1)}, bf16[256,640]{1,0:T(8,128)(2,1)}, u32[]{:S(2)}, u32[]{:S(2)}) %collective-permute-start.3) | collective-permute-done | bytes 327712 | tf_op jit(solution)/shard_map/ppermute | solution.py:57
  21.4 3.5 %collective-permute-start.4 = (bf16[256,640]{1,0:T(8,128)(2,1)}, bf16[256,640]{1,0:T(8,128)(2,1)S(1)}, u32[]{:S(2)}, u32[]{:S(2)}) collective-permute-start(bf16[256,640]{1,0:T(8,128)(2,1)} %collective-permute-done.3.refs_6_), channel_id=1, source_target_pairs={{0,2},{2,3},{3,1},{1,0},{4,6},{6,7},{7,5},{5,4},{8,10},{10,11},{11... | collective-permute-start | bytes 983048 | tf_op jit(solution)/shard_map/ppermute | solution.py:57
  25.7 2.9 %copy-done = bf16[2,2560,640]{2,1,0:T(8,128)(2,1)S(1)} copy-done((bf16[2,2560,640]{2,1,0:T(8,128)(2,1)S(1)}, bf16[2,2560,640]{2,1,0:T(8,128)(2,1)}, u32[]{:S(2)}) %copy-start) | copy-done | bytes 6553624
  28.6 1.9 %copy-done.5 = bf16[2560,640]{1,0:T(8,128)(2,1)S(1)} copy-done((bf16[2560,640]{1,0:T(8,128)(2,1)S(1)}, bf16[2560,640]{1,0:T(8,128)(2,1)}, u32[]{:S(2)}) %copy-start.5) | copy-done | bytes 3276824
  32.8 3.3 %collective-permute-done.4.refs_0_ = bf16[256,640]{1,0:T(8,128)(2,1)S(1)} collective-permute-done((bf16[256,640]{1,0:T(8,128)(2,1)}, bf16[256,640]{1,0:T(8,128)(2,1)S(1)}, u32[]{:S(2)}, u32[]{:S(2)}) %collective-permute-start.4) | collective-permute-done | bytes 327712 | tf_op jit(solution)/shard_map/ppermute | solution.py:57
  36.1 2.8 %collective-permute-start.5 = (bf16[256,640]{1,0:T(8,128)(2,1)S(1)}, bf16[256,640]{1,0:T(8,128)(2,1)S(1)}, u32[]{:S(2)}, u32[]{:S(2)}) collective-permute-start(bf16[256,640]{1,0:T(8,128)(2,1)S(1)} %after.3.refs_7_), channel_id=1, source_target_pairs={{0,2},{2,3},{3,1},{1,0},{4,6},{6,7},{7,5},{5,4},{8,10},{10,11},{11... | collective-permute-start | bytes 983048 | tf_op jit(solution)/shard_map/ppermute | solution.py:57
  38.9 6.1 %forward_early.1 = (f32[3,512,640]{2,1,0:T(8,128)S(1)}, bf16[2560,512]{1,0:T(8,128)(2,1)S(1)}) custom-call(s32[12]{0:T(128)S(1)} %pad_add_fusion.refs_0_, bf16[2560,1920]{1,0:T(8,128)(2,1)S(1)} %join_weights.1.refs_1_, bf16[256,640]{1,0:T(8,128)(2,1)S(1)} %sum_rows.2.refs_1_.refs_2_, bf16[256,640]{1,0:T(8,128)(2,1)} %after.2.refs_3_, ...), custom_call_target="tpu_custom_call" | custom-call | flops 188743680 | tf_op jit(solution)/shard_map/forward_early/pallas_call | solution.py:37
  45.0 4.0 %collective-permute-done.5.refs_3_ = bf16[256,640]{1,0:T(8,128)(2,1)S(1)} collective-permute-done((bf16[256,640]{1,0:T(8,128)(2,1)S(1)}, bf16[256,640]{1,0:T(8,128)(2,1)S(1)}, u32[]{:S(2)}, u32[]{:S(2)}) %collective-permute-start.5) | collective-permute-done | bytes 327712 | tf_op jit(solution)/shard_map/ppermute | solution.py:57
  48.9 3.3 %forward_late.1 = (f32[3,512,640]{2,1,0:T(8,128)S(1)}, bf16[2560,512]{1,0:T(8,128)(2,1)S(1)}, f32[8,512]{1,0:T(8,128)S(1)}) custom-call(s32[12]{0:T(128)S(1)} %pad_add_fusion.refs_0_, bf16[2560,1920]{1,0:T(8,128)(2,1)S(1)} %join_weights.1.refs_1_, bf16[256,640]{1,0:T(8,128)(2,1)S(1)} %collective-permute-done.2.refs_2_, ...), custom_call_target="tpu_custom_call", output_to_operand_aliasing={{0}: (4, {}), {1}: (5, {})} | custom-call | flops 62914560 | tf_op jit(solution)/shard_map/forward_late/pallas_call | solution.py:37
  52.4 3.0 %collective-permute-start.8 = (f32[8,512]{1,0:T(8,128)S(1)}, f32[8,512]{1,0:T(8,128)S(1)}, u32[]{:S(2)}, u32[]{:S(2)}) collective-permute-start(f32[8,512]{1,0:T(8,128)S(1)} %get-tuple-element.38.refs_0_), channel_id=1, source_target_pairs={{0,3},{1,2},{2,1},{3,0},{4,7},{5,6},{6,5},{7,4},{8,11},{9,10},{10,... | collective-permute-start | bytes 49160 | tf_op jit(solution)/shard_map/ppermute | solution.py:63
  58.0 2.1 %collective-permute-done.7.refs_2_ = f32[8,512]{1,0:T(8,128)S(1)} collective-permute-done((f32[8,512]{1,0:T(8,128)S(1)}, f32[8,512]{1,0:T(8,128)S(1)}, u32[]{:S(2)}, u32[]{:S(2)}) %collective-permute-start.7) | collective-permute-done | bytes 16416 | tf_op jit(solution)/shard_map/ppermute | solution.py:63
  61.4 1.8 %back.4.refs_5_ = bf16[512,640]{1,0:T(8,128)(2,1)S(1)} custom-call(bf16[512,1920]{1,0:T(8,128)(2,1)S(1)} %cotangents.1.refs_0_.refs_1_, bf16[2560,1920]{1,0:T(8,128)(2,1)S(1)} %join_weights.1.refs_1_), custom_call_target="tpu_custom_call" | custom-call | flops 62914560 | tf_op jit(solution)/shard_map/back/pallas_call | solution.py:37
  63.2 2.2 %collective-permute-start.11 = (bf16[512,640]{1,0:T(8,128)(2,1)S(1)}, bf16[512,640]{1,0:T(8,128)(2,1)S(1)}, u32[]{:S(2)}, u32[]{:S(2)}) collective-permute-start(bf16[512,640]{1,0:T(8,128)(2,1)S(1)} %back.4.refs_5_), channel_id=1, source_target_pairs={{0,2},{2,3},{3,1},{1,0},{4,6},{6,7},{7,5},{5,4},{8,10},{10,11},{11... | collective-permute-start | bytes 1966088 | tf_op jit(solution)/shard_map/ppermute | solution.py:57
  65.4 2.1 %outer.4 = (bf16[160,1920]{1,0:T(8,128)(2,1)S(1)}, bf16[160,1920]{1,0:T(8,128)(2,1)S(1)}) custom-call(s32[12]{0:T(128)S(1)} %pad_add_fusion.refs_0_, bf16[512,1920]{1,0:T(8,128)(2,1)S(1)} %cotangents.1.refs_0_.refs_1_, bf16[512,1920]{1,0:T(8,128)(2,1)S(1)} %collective-permute-done.10.refs_2_, bf16[2560,512]{1,0:T(8,128)(2,1)S(1)} %get-tuple-element.40.refs_3_, ...), custom_call_target="tpu_custom_call" | custom-call | flops 62914560 | tf_op jit(solution)/shard_map/outer/pallas_call | solution.py:37
  70.6 2.1 %outer.5 = (bf16[160,1920]{1,0:T(8,128)(2,1)S(1)}, bf16[160,1920]{1,0:T(8,128)(2,1)S(1)}) custom-call(s32[12]{0:T(128)S(1)} %pad_add_fusion.refs_0_, bf16[512,1920]{1,0:T(8,128)(2,1)S(1)} %cotangents.1.refs_0_.refs_1_, bf16[512,1920]{1,0:T(8,128)(2,1)S(1)} %collective-permute-done.10.refs_2_, bf16[2560,512]{1,0:T(8,128)(2,1)S(1)} %get-tuple-element.40.refs_3_, ...), custom_call_target="tpu_custom_call" | custom-call | flops 62914560 | tf_op jit(solution)/shard_map/outer/pallas_call | solution.py:37
  73.2 1.8 %back.5 = (bf16[512,384]{1,0:T(8,128)(2,1)S(1)}, bf16[512,256]{1,0:T(8,128)(2,1)S(1)}) custom-call(bf16[512,1920]{1,0:T(8,128)(2,1)S(1)} %cotangents.1.refs_0_.refs_1_, bf16[2560,1920]{1,0:T(8,128)(2,1)S(1)} %join_weights.1.refs_1_, bf16[160,1920]{1,0:T(8,128)(2,1)S(1)} %get-tuple-element.42.refs_2_), custom_call_target="tpu_custom_call" | custom-call | flops 62914560 | tf_op jit(solution)/shard_map/back/pallas_call | solution.py:37
  75.0 5.5 %collective-permute-done.11.refs_0_ = bf16[512,640]{1,0:T(8,128)(2,1)S(1)} collective-permute-done((bf16[512,640]{1,0:T(8,128)(2,1)S(1)}, bf16[512,640]{1,0:T(8,128)(2,1)S(1)}, u32[]{:S(2)}, u32[]{:S(2)}) %collective-permute-start.11) | collective-permute-done | bytes 655392 | tf_op jit(solution)/shard_map/ppermute | solution.py:57
  80.7 2.9 %collective-permute-start.15 = (bf16[512,384]{1,0:T(8,128)(2,1)S(1)}, bf16[512,384]{1,0:T(8,128)(2,1)S(1)}, u32[]{:S(2)}, u32[]{:S(2)}) collective-permute-start(bf16[512,384]{1,0:T(8,128)(2,1)S(1)} %add_part.4.refs_2_), channel_id=1, source_target_pairs={{0,2},{2,3},{3,1},{1,0},{4,6},{6,7},{7,5},{5,4},{8,10},{10,11},{11... | collective-permute-start | bytes 1179656 | tf_op jit(solution)/shard_map/ppermute | solution.py:57
  83.7 2.1 %outer.6 = (bf16[160,1920]{1,0:T(8,128)(2,1)S(1)}, bf16[160,1920]{1,0:T(8,128)(2,1)S(1)}) custom-call(s32[12]{0:T(128)S(1)} %pad_add_fusion.refs_0_, bf16[512,1920]{1,0:T(8,128)(2,1)S(1)} %cotangents.1.refs_0_.refs_1_, bf16[512,1920]{1,0:T(8,128)(2,1)S(1)} %collective-permute-done.10.refs_2_, bf16[2560,512]{1,0:T(8,128)(2,1)S(1)} %get-tuple-element.40.refs_3_, ...), custom_call_target="tpu_custom_call" | custom-call | flops 62914560 | tf_op jit(solution)/shard_map/outer/pallas_call | solution.py:37
  89.8 2.1 %outer.7 = (bf16[160,1920]{1,0:T(8,128)(2,1)S(1)}, bf16[160,1920]{1,0:T(8,128)(2,1)S(1)}) custom-call(s32[12]{0:T(128)S(1)} %pad_add_fusion.refs_0_, bf16[512,1920]{1,0:T(8,128)(2,1)S(1)} %cotangents.1.refs_0_.refs_1_, bf16[512,1920]{1,0:T(8,128)(2,1)S(1)} %collective-permute-done.10.refs_2_, bf16[2560,512]{1,0:T(8,128)(2,1)S(1)} %get-tuple-element.40.refs_3_, ...), custom_call_target="tpu_custom_call" | custom-call | flops 62914560 | tf_op jit(solution)/shard_map/outer/pallas_call | solution.py:37
  91.9 1.8 %back.6 = (bf16[512,384]{1,0:T(8,128)(2,1)S(1)}, bf16[512,256]{1,0:T(8,128)(2,1)S(1)}) custom-call(bf16[512,1920]{1,0:T(8,128)(2,1)S(1)} %cotangents.1.refs_0_.refs_1_, bf16[2560,1920]{1,0:T(8,128)(2,1)S(1)} %join_weights.1.refs_1_, bf16[160,1920]{1,0:T(8,128)(2,1)S(1)} %get-tuple-element.48.refs_2_.refs_0_), custom_call_target="tpu_custom_call" | custom-call | flops 62914560 | tf_op jit(solution)/shard_map/back/pallas_call | solution.py:37
  94.1 1.8 %back.7 = (bf16[512,384]{1,0:T(8,128)(2,1)S(1)}, bf16[512,256]{1,0:T(8,128)(2,1)S(1)}) custom-call(bf16[512,1920]{1,0:T(8,128)(2,1)S(1)} %cotangents.1.refs_0_.refs_1_, bf16[2560,1920]{1,0:T(8,128)(2,1)S(1)} %join_weights.1.refs_1_, bf16[1024,512]{1,0:T(8,128)(2,1)S(1)} %mark_slots.1.refs_2_.refs_0_), custom_call_target="tpu_custom_call" | custom-call | flops 62914560 | tf_op jit(solution)/shard_map/back/pallas_call | solution.py:37
  98.7 3.4 %collective-permute-start.21 = (bf16[512,256]{1,0:T(8,128)(2,1)S(1)}, bf16[512,256]{1,0:T(8,128)(2,1)S(1)}, u32[]{:S(2)}, u32[]{:S(2)}) collective-permute-start(bf16[512,256]{1,0:T(8,128)(2,1)S(1)} %add_part.7.refs_2_), channel_id=1, source_target_pairs={{0,2},{2,3},{3,1},{1,0},{4,6},{6,7},{7,5},{5,4},{8,10},{10,11},{11... | collective-permute-start | bytes 786440 | tf_op jit(solution)/shard_map/ppermute | solution.py:57
  104.9 6.7 %collective-permute-done.21.refs_2_ = bf16[512,256]{1,0:T(8,128)(2,1)S(1)} collective-permute-done((bf16[512,256]{1,0:T(8,128)(2,1)S(1)}, bf16[512,256]{1,0:T(8,128)(2,1)S(1)}, u32[]{:S(2)}, u32[]{:S(2)}) %collective-permute-start.21) | collective-permute-done | bytes 262176 | tf_op jit(solution)/shard_map/ppermute | solution.py:57
  111.6 2.1 %pick_rows.1 = bf16[1024,640]{1,0:T(8,128)(2,1)} custom-call(bf16[1024,512]{1,0:T(8,128)(2,1)S(1)} %mark_slots.1.refs_2_.refs_0_, bf16[512,384]{1,0:T(8,128)(2,1)S(1)} %collective-permute-done.20.refs_1_, bf16[512,256]{1,0:T(8,128)(2,1)S(1)} %collective-permute-done.21.refs_2_, bf16[512,384]{1,0:T(8,128)(2,1)S(1)} %get-tuple-element.50.refs_1_.refs_3_, ...), custom_call_target="tpu_custom_call" | custom-call | flops 33554432 | tf_op jit(solution)/shard_map/pick_rows/pallas_call | solution.py:37
  113.7 3.7 %all-to-all-start.1 = ((bf16[8,128,640]{2,1,0:T(8,128)(2,1)}), bf16[8,128,640]{2,1,0:T(8,128)(2,1)S(1)}, u32[]{:S(2)}, u32[]{:S(2)}) async-start(bf16[8,128,640]{2,1,0:T(8,128)(2,1)} %bitcast.11), calls=%async_computation.1 | async-start | bytes 2621440 | tf_op jit(solution)/shard_map/all_to_all | solution.py:675
  122.1 13.6 %all-to-all-done.1 = bf16[8,128,640]{2,1,0:T(8,128)(2,1)S(1)} async-done(((bf16[8,128,640]{2,1,0:T(8,128)(2,1)}), bf16[8,128,640]{2,1,0:T(8,128)(2,1)S(1)}, u32[]{:S(2)}, u32[]{:S(2)}) %all-to-all-start.1) | async-done | bytes 1310752 | tf_op jit(solution)/shard_map/all_to_all | solution.py:675
  137.5 2.2 %collective-permute-start.24 = (f32[1,256]{1,0:T(1,128)S(1)}, f32[1,256]{1,0:T(1,128)S(1)}, u32[]{:S(2)}, u32[]{:S(2)}) collective-permute-start(f32[1,256]{1,0:T(1,128)S(1)} %get-tuple-element.57.refs_0_), channel_id=1, source_target_pairs={{0,3},{1,2},{2,1},{3,0},{4,7},{5,6},{6,5},{7,4},{8,11},{9,10},{10,... | collective-permute-start | bytes 3080 | tf_op jit(solution)/shard_map/ppermute | solution.py:63
  139.7 2.0 %collective-permute-start.23 = (f32[1,256]{1,0:T(1,128)S(1)}, f32[1,256]{1,0:T(1,128)S(1)}, u32[]{:S(2)}, u32[]{:S(2)}) collective-permute-start(f32[1,256]{1,0:T(1,128)S(1)} %get-tuple-element.57.refs_0_), channel_id=1, source_target_pairs={{0,2},{1,3},{2,0},{3,1},{4,6},{5,7},{6,4},{7,5},{8,10},{9,11},{10,... | collective-permute-start | bytes 3080 | tf_op jit(solution)/shard_map/ppermute | solution.py:63
  (88 shorter events, 38.0 us)
Async XLA Ops:
  2.1 5.9 %copy-start.12 = (bf16[512,2,640]{2,1,0:T(2,128)(2,1)S(1)}, bf16[512,2,640]{2,1,0:T(2,128)(2,1)}, u32[]{:S(2)}) copy-start(bf16[512,2,640]{2,1,0:T(2,128)(2,1)} %param.13) | copy-start | bytes 3932164
  2.2 16.0 %collective-permute-start = (bf16[256,640]{1,0:T(8,128)(2,1)S(1)}, bf16[256,640]{1,0:T(8,128)(2,1)}, u32[]{:S(2)}, u32[]{:S(2)}) collective-permute-start(bf16[256,640]{1,0:T(8,128)(2,1)S(1)} %sum_rows.2.refs_1_.refs_2_), channel_id=1, source_target_pairs={{0,2},{2,3},{3,1},{1,0},{4,6},{6,7},{7,5},{5,4},{8,10},{10,11},{11... | collective-permute-start | bytes 983048 | tf_op jit(solution)/shard_map/ppermute | solution.py:57
  6.4 15.0 %collective-permute-start.3 = (bf16[256,640]{1,0:T(8,128)(2,1)S(1)}, bf16[256,640]{1,0:T(8,128)(2,1)}, u32[]{:S(2)}, u32[]{:S(2)}) collective-permute-start(bf16[256,640]{1,0:T(8,128)(2,1)S(1)} %sum_rows.3.refs_1_.refs_5_), channel_id=1, source_target_pairs={{0,2},{2,3},{3,1},{1,0},{4,6},{6,7},{7,5},{5,4},{8,10},{10,11},{11... | collective-permute-start | bytes 983048 | tf_op jit(solution)/shard_map/ppermute | solution.py:57
  9.9 8.3 %all-to-all-start = ((s32[8,1,128]{2,1,0:T(1,128)}), s32[8,1,128]{2,1,0:T(1,128)S(1)}, u32[]{:S(2)}, u32[]{:S(2)}) async-start(s32[8,1,128]{2,1,0:T(1,128)} %bitcast.6), calls=%async_computation | async-start | bytes 8192 | tf_op jit(solution)/shard_map/all_to_all | solution.py:581
  18.2 13.8 %collective-permute-start.1 = (bf16[256,640]{1,0:T(8,128)(2,1)}, bf16[256,640]{1,0:T(8,128)(2,1)S(1)}, u32[]{:S(2)}, u32[]{:S(2)}) collective-permute-start(bf16[256,640]{1,0:T(8,128)(2,1)} %after.2.refs_3_), channel_id=1, source_target_pairs={{0,2},{2,3},{3,1},{1,0},{4,6},{6,7},{7,5},{5,4},{8,10},{10,11},{11... | collective-permute-start | bytes 983048 | tf_op jit(solution)/shard_map/ppermute | solution.py:57
  21.4 14.6 %collective-permute-start.4 = (bf16[256,640]{1,0:T(8,128)(2,1)}, bf16[256,640]{1,0:T(8,128)(2,1)S(1)}, u32[]{:S(2)}, u32[]{:S(2)}) collective-permute-start(bf16[256,640]{1,0:T(8,128)(2,1)} %collective-permute-done.3.refs_6_), channel_id=1, source_target_pairs={{0,2},{2,3},{3,1},{1,0},{4,6},{6,7},{7,5},{5,4},{8,10},{10,11},{11... | collective-permute-start | bytes 983048 | tf_op jit(solution)/shard_map/ppermute | solution.py:57
  32.1 12.9 %collective-permute-start.2 = (bf16[256,640]{1,0:T(8,128)(2,1)S(1)}, bf16[256,640]{1,0:T(8,128)(2,1)S(1)}, u32[]{:S(2)}, u32[]{:S(2)}) collective-permute-start(bf16[256,640]{1,0:T(8,128)(2,1)S(1)} %collective-permute-done.1.refs_4_), channel_id=1, source_target_pairs={{0,2},{2,3},{3,1},{1,0},{4,6},{6,7},{7,5},{5,4},{8,10},{10,11},{11... | collective-permute-start | bytes 983048 | tf_op jit(solution)/shard_map/ppermute | solution.py:57
  36.1 12.9 %collective-permute-start.5 = (bf16[256,640]{1,0:T(8,128)(2,1)S(1)}, bf16[256,640]{1,0:T(8,128)(2,1)S(1)}, u32[]{:S(2)}, u32[]{:S(2)}) collective-permute-start(bf16[256,640]{1,0:T(8,128)(2,1)S(1)} %after.3.refs_7_), channel_id=1, source_target_pairs={{0,2},{2,3},{3,1},{1,0},{4,6},{6,7},{7,5},{5,4},{8,10},{10,11},{11... | collective-permute-start | bytes 983048 | tf_op jit(solution)/shard_map/ppermute | solution.py:57
  52.3 7.8 %collective-permute-start.9 = (bf16[2560,512]{1,0:T(8,128)(2,1)S(1)}, bf16[2560,512]{1,0:T(8,128)(2,1)S(1)}, u32[]{:S(2)}, u32[]{:S(2)}) collective-permute-start(bf16[2560,512]{1,0:T(8,128)(2,1)S(1)} %get-tuple-element.40.refs_3_), channel_id=1, source_target_pairs={{0,4},{4,0},{8,12},{12,8},{16,20},{20,16},{24,28},{28,24},{1,5},{5... | collective-permute-start | bytes 7864328 | tf_op jit(solution)/shard_map/ppermute | solution.py:70
  52.4 5.6 %collective-permute-start.8 = (f32[8,512]{1,0:T(8,128)S(1)}, f32[8,512]{1,0:T(8,128)S(1)}, u32[]{:S(2)}, u32[]{:S(2)}) collective-permute-start(f32[8,512]{1,0:T(8,128)S(1)} %get-tuple-element.38.refs_0_), channel_id=1, source_target_pairs={{0,3},{1,2},{2,1},{3,0},{4,7},{5,6},{6,5},{7,4},{8,11},{9,10},{10,... | collective-permute-start | bytes 49160 | tf_op jit(solution)/shard_map/ppermute | solution.py:63
  55.4 4.7 %collective-permute-start.7 = (f32[8,512]{1,0:T(8,128)S(1)}, f32[8,512]{1,0:T(8,128)S(1)}, u32[]{:S(2)}, u32[]{:S(2)}) collective-permute-start(f32[8,512]{1,0:T(8,128)S(1)} %get-tuple-element.38.refs_0_), channel_id=1, source_target_pairs={{0,2},{1,3},{2,0},{3,1},{4,6},{5,7},{6,4},{7,5},{8,10},{9,11},{10,... | collective-permute-start | bytes 49160 | tf_op jit(solution)/shard_map/ppermute | solution.py:63
  55.7 4.4 %collective-permute-start.6 = (f32[8,512]{1,0:T(8,128)S(1)}, f32[8,512]{1,0:T(8,128)S(1)}, u32[]{:S(2)}, u32[]{:S(2)}) collective-permute-start(f32[8,512]{1,0:T(8,128)S(1)} %get-tuple-element.38.refs_0_), channel_id=1, source_target_pairs={{0,1},{1,0},{2,3},{3,2},{4,5},{5,4},{6,7},{7,6},{8,9},{9,8},{10,11... | collective-permute-start | bytes 49160 | tf_op jit(solution)/shard_map/ppermute | solution.py:63
  61.3 4.1 %collective-permute-start.10 = (bf16[512,1920]{1,0:T(8,128)(2,1)S(1)}, bf16[512,1920]{1,0:T(8,128)(2,1)S(1)}, u32[]{:S(2)}, u32[]{:S(2)}) collective-permute-start(bf16[512,1920]{1,0:T(8,128)(2,1)S(1)} %cotangents.1.refs_0_.refs_1_), channel_id=1, source_target_pairs={{0,4},{4,0},{8,12},{12,8},{16,20},{20,16},{24,28},{28,24},{1,5},{5... | collective-permute-start | bytes 5898248 | tf_op jit(solution)/shard_map/ppermute | solution.py:70
  63.2 17.4 %collective-permute-start.11 = (bf16[512,640]{1,0:T(8,128)(2,1)S(1)}, bf16[512,640]{1,0:T(8,128)(2,1)S(1)}, u32[]{:S(2)}, u32[]{:S(2)}) collective-permute-start(bf16[512,640]{1,0:T(8,128)(2,1)S(1)} %back.4.refs_5_), channel_id=1, source_target_pairs={{0,2},{2,3},{3,1},{1,0},{4,6},{6,7},{7,5},{5,4},{8,10},{10,11},{11... | collective-permute-start | bytes 1966088 | tf_op jit(solution)/shard_map/ppermute | solution.py:57
  67.5 19.8 %collective-permute-start.13 = (bf16[160,1920]{1,0:T(8,128)(2,1)S(1)}, bf16[160,1920]{1,0:T(8,128)(2,1)S(1)}, u32[]{:S(2)}, u32[]{:S(2)}) collective-permute-start(bf16[160,1920]{1,0:T(8,128)(2,1)S(1)} %get-tuple-element.47), channel_id=1, source_target_pairs={{0,16},{4,20},{8,24},{12,28},{16,0},{20,4},{24,8},{28,12},{1,17},{... | collective-permute-start | bytes 1843208 | tf_op jit(solution)/shard_map/ppermute | solution.py:70
  69.1 19.2 %collective-permute-start.12 = (bf16[160,1920]{1,0:T(8,128)(2,1)S(1)}, bf16[160,1920]{1,0:T(8,128)(2,1)S(1)}, u32[]{:S(2)}, u32[]{:S(2)}) collective-permute-start(bf16[160,1920]{1,0:T(8,128)(2,1)S(1)} %get-tuple-element.41.refs_5_), channel_id=1, source_target_pairs={{0,8},{4,12},{8,0},{12,4},{16,24},{20,28},{24,16},{28,20},{1,9},{5... | collective-permute-start | bytes 1843208 | tf_op jit(solution)/shard_map/ppermute | solution.py:70
  72.6 25.3 %collective-permute-start.14 = (bf16[160,1920]{1,0:T(8,128)(2,1)S(1)}, bf16[160,1920]{1,0:T(8,128)(2,1)S(1)}, u32[]{:S(2)}, u32[]{:S(2)}) collective-permute-start(bf16[160,1920]{1,0:T(8,128)(2,1)S(1)} %get-tuple-element.42.refs_2_), channel_id=1, source_target_pairs={{0,8},{4,12},{8,0},{12,4},{16,24},{20,28},{24,16},{28,20},{1,9},{5... | collective-permute-start | bytes 1843208 | tf_op jit(solution)/shard_map/ppermute | solution.py:70
  80.7 15.2 %collective-permute-start.15 = (bf16[512,384]{1,0:T(8,128)(2,1)S(1)}, bf16[512,384]{1,0:T(8,128)(2,1)S(1)}, u32[]{:S(2)}, u32[]{:S(2)}) collective-permute-start(bf16[512,384]{1,0:T(8,128)(2,1)S(1)} %add_part.4.refs_2_), channel_id=1, source_target_pairs={{0,2},{2,3},{3,1},{1,0},{4,6},{6,7},{7,5},{5,4},{8,10},{10,11},{11... | collective-permute-start | bytes 1179656 | tf_op jit(solution)/shard_map/ppermute | solution.py:57
  85.7 18.0 %collective-permute-start.17 = (bf16[160,1920]{1,0:T(8,128)(2,1)S(1)}, bf16[160,1920]{1,0:T(8,128)(2,1)S(1)}, u32[]{:S(2)}, u32[]{:S(2)}) collective-permute-start(bf16[160,1920]{1,0:T(8,128)(2,1)S(1)} %get-tuple-element.53), channel_id=1, source_target_pairs={{0,16},{4,20},{8,24},{12,28},{16,0},{20,4},{24,8},{28,12},{1,17},{... | collective-permute-start | bytes 1843208 | tf_op jit(solution)/shard_map/ppermute | solution.py:70
  89.3 28.2 %collective-permute-start.16 = (bf16[160,1920]{1,0:T(8,128)(2,1)}, bf16[160,1920]{1,0:T(8,128)(2,1)}, u32[]{:S(2)}, u32[]{:S(2)}) collective-permute-start(bf16[160,1920]{1,0:T(8,128)(2,1)} %add.32.refs_5_), channel_id=1, source_target_pairs={{0,16},{4,20},{8,24},{12,28},{16,0},{20,4},{24,8},{28,12},{1,17},{... | collective-permute-start | bytes 1843208 | tf_op jit(solution)/shard_map/ppermute | solution.py:70
  89.8 8.9 %collective-permute-start.18 = (bf16[512,256]{1,0:T(8,128)(2,1)S(1)}, bf16[512,256]{1,0:T(8,128)(2,1)S(1)}, u32[]{:S(2)}, u32[]{:S(2)}) collective-permute-start(bf16[512,256]{1,0:T(8,128)(2,1)S(1)} %add_part.5.refs_5_), channel_id=1, source_target_pairs={{0,2},{2,3},{3,1},{1,0},{4,6},{6,7},{7,5},{5,4},{8,10},{10,11},{11... | collective-permute-start | bytes 786440 | tf_op jit(solution)/shard_map/ppermute | solution.py:57
  96.0 15.6 %collective-permute-start.20 = (bf16[512,384]{1,0:T(8,128)(2,1)S(1)}, bf16[512,384]{1,0:T(8,128)(2,1)S(1)}, u32[]{:S(2)}, u32[]{:S(2)}) collective-permute-start(bf16[512,384]{1,0:T(8,128)(2,1)S(1)} %add_part.6.refs_2_), channel_id=1, source_target_pairs={{0,2},{2,3},{3,1},{1,0},{4,6},{6,7},{7,5},{5,4},{8,10},{10,11},{11... | collective-permute-start | bytes 1179656 | tf_op jit(solution)/shard_map/ppermute | solution.py:57
  98.7 12.9 %collective-permute-start.21 = (bf16[512,256]{1,0:T(8,128)(2,1)S(1)}, bf16[512,256]{1,0:T(8,128)(2,1)S(1)}, u32[]{:S(2)}, u32[]{:S(2)}) collective-permute-start(bf16[512,256]{1,0:T(8,128)(2,1)S(1)} %add_part.7.refs_2_), channel_id=1, source_target_pairs={{0,2},{2,3},{3,1},{1,0},{4,6},{6,7},{7,5},{5,4},{8,10},{10,11},{11... | collective-permute-start | bytes 786440 | tf_op jit(solution)/shard_map/ppermute | solution.py:57
  102.1 16.6 %collective-permute-start.19 = (bf16[160,1920]{1,0:T(8,128)(2,1)}, bf16[160,1920]{1,0:T(8,128)(2,1)}, u32[]{:S(2)}, u32[]{:S(2)}) collective-permute-start(bf16[160,1920]{1,0:T(8,128)(2,1)} %add.31.refs_2_), channel_id=1, source_target_pairs={{0,8},{4,12},{8,0},{12,4},{16,24},{20,28},{24,16},{28,20},{1,9},{5... | collective-permute-start | bytes 1843208 | tf_op jit(solution)/shard_map/ppermute | solution.py:70
  113.7 21.9 %all-to-all-start.1 = ((bf16[8,128,640]{2,1,0:T(8,128)(2,1)}), bf16[8,128,640]{2,1,0:T(8,128)(2,1)S(1)}, u32[]{:S(2)}, u32[]{:S(2)}) async-start(bf16[8,128,640]{2,1,0:T(8,128)(2,1)} %bitcast.11), calls=%async_computation.1 | async-start | bytes 2621440 | tf_op jit(solution)/shard_map/all_to_all | solution.py:675
  122.1 15.4 %copy-start.1 = (f32[2,320,640]{2,1,0:T(8,128)}, f32[2,320,640]{2,1,0:T(8,128)S(1)}, u32[]{:S(2)}) copy-start(f32[2,320,640]{2,1,0:T(8,128)S(1)} %maximum_add_fusion.refs_2_) | copy-start | bytes 4915204
  136.8 8.4 %copy-start.6 = (f32[256,640]{1,0:T(8,128)S(1)}, f32[256,640]{1,0:T(8,128)}, u32[]{:S(2)}) copy-start(f32[256,640]{1,0:T(8,128)} %mean_ref.1) | copy-start | bytes 1966084
  136.8 8.4 %copy-start.7 = (f32[256,640]{1,0:T(8,128)S(1)}, f32[256,640]{1,0:T(8,128)}, u32[]{:S(2)}) copy-start(f32[256,640]{1,0:T(8,128)} %second_ref.1) | copy-start | bytes 1966084
  136.8 8.4 %copy-start.9 = (s32[256]{0:T(256)S(1)}, s32[256]{0:T(256)}, u32[]{:S(2)}) copy-start(s32[256]{0:T(256)} %param.20) | copy-start | bytes 3076
  137.5 5.4 %collective-permute-start.24 = (f32[1,256]{1,0:T(1,128)S(1)}, f32[1,256]{1,0:T(1,128)S(1)}, u32[]{:S(2)}, u32[]{:S(2)}) collective-permute-start(f32[1,256]{1,0:T(1,128)S(1)} %get-tuple-element.57.refs_0_), channel_id=1, source_target_pairs={{0,3},{1,2},{2,1},{3,0},{4,7},{5,6},{6,5},{7,4},{8,11},{9,10},{10,... | collective-permute-start | bytes 3080 | tf_op jit(solution)/shard_map/ppermute | solution.py:63
  139.7 4.5 %collective-permute-start.23 = (f32[1,256]{1,0:T(1,128)S(1)}, f32[1,256]{1,0:T(1,128)S(1)}, u32[]{:S(2)}, u32[]{:S(2)}) collective-permute-start(f32[1,256]{1,0:T(1,128)S(1)} %get-tuple-element.57.refs_0_), channel_id=1, source_target_pairs={{0,2},{1,3},{2,0},{3,1},{4,6},{5,7},{6,4},{7,5},{8,10},{9,11},{10,... | collective-permute-start | bytes 3080 | tf_op jit(solution)/shard_map/ppermute | solution.py:63
  141.7 3.6 %collective-permute-start.22 = (f32[1,256]{1,0:T(1,128)S(1)}, f32[1,256]{1,0:T(1,128)S(1)}, u32[]{:S(2)}, u32[]{:S(2)}) collective-permute-start(f32[1,256]{1,0:T(1,128)S(1)} %get-tuple-element.57.refs_0_), channel_id=1, source_target_pairs={{0,1},{1,0},{2,3},{3,2},{4,5},{5,4},{6,7},{7,6},{8,9},{9,8},{10,11... | collective-permute-start | bytes 3080 | tf_op jit(solution)/shard_map/ppermute | solution.py:63
  (9 other events, 19.4 us)

commit v4 on v3

--- a/solution.py
+++ b/solution.py
@@ -429,92 +429,103 @@
     )[0]
 
 
-def mark_kernel(slot_ref, out_ref):
-    slots = lax.broadcasted_iota(jnp.int32, out_ref.shape, 0)
+def mark_kernel(entry, plan_ref, slot_ref, out_ref):
+    slots = lax.broadcasted_iota(jnp.int32, out_ref.shape, 0) ^ (plan_ref[entry] * CAP)
     marks = sum((slots == slot_ref[n : n + 1, :]).astype(F32) for n in range(slot_ref.shape[0]))
     out_ref[...] = marks.astype(BF16)
 
 
-def mark_slots(slot_index, slot_count, after=()):
-    return call(
-        mark_kernel,
+def mark_slots(entry, plan, slot_index, slot_count, after=()):
+    return call(
+        functools.partial(mark_kernel, entry),
         "mark_slots",
-        [VMEM],
+        [SMEM, VMEM],
         [jax.ShapeDtypeStruct((slot_count, slot_index.shape[1]), BF16)],
-        [slot_index],
+        [plan, slot_index],
         macs=slot_count * slot_index.shape[1],
         after=after,
     )[0]
 
 
-def pick_kernel(mark_ref, *refs):
-    *refs, out_ref = refs
-    count = len(refs) // 2
+def pick_kernel(count, mark_ref, *refs):
+    out_refs = refs[2 * count :]
     start = 0
-    for passing_ref, term_ref in zip(refs[:count], refs[count:]):
+    for passing_ref, term_ref in zip(refs[:count], refs[count : 2 * count]):
         total = (passing_ref[...].astype(F32) + term_ref[...].astype(F32)).astype(BF16)
         columns = slice(start, start + total.shape[1])
-        product = jnp.dot(mark_ref[...], total, preferred_element_type=F32)
-        out_ref[:, columns] = product.astype(BF16)
+        product = jnp.dot(mark_ref[...], total, preferred_element_type=F32).astype(BF16)
+        for rel, ref in enumerate(out_refs):
+            ref[:, columns] = product[rel * CAP : (rel + 1) * CAP]
         start += total.shape[1]
 
 
-def pick_rows(marks, passing, terms, after=()):
+def pick_rows(marks, passing, terms, after):
     slot_count, tok_count = marks.shape
     width = sum(part.shape[1] for part in passing)
     return call(
-        pick_kernel,
+        functools.partial(pick_kernel, len(passing)),
         "pick_rows",
         [VMEM] * (1 + 2 * len(passing)),
-        [jax.ShapeDtypeStruct((slot_count, width), BF16)],
+        [jax.ShapeDtypeStruct((CAP, width), BF16)] * (slot_count // CAP),
         [marks, *passing, *terms],
         macs=slot_count * tok_count * width,
         after=after,
-    )[0]
-
-
-def place_kernel(row_ref, incoming_ref, grad_ref, sum_ref):
-    rows = lax.broadcasted_iota(jnp.int32, (grad_ref.shape[0], row_ref.shape[1]), 0) + 1
-    place = (rows == row_ref[...]).astype(F32).astype(BF16)
-    grad = jnp.dot(place, incoming_ref[...], preferred_element_type=F32)
+    )
+
+
+def place_kernel(entry, plan_ref, row_ref, *refs):
+    *incoming, grad_ref, sum_ref = refs
+    rows = lax.broadcasted_iota(jnp.int32, (grad_ref.shape[0], CAP), 0) + 1
+    places = []
+    for rel in range(len(incoming)):
+        source = pl.multiple_of(plan_ref[entry + rel] * CAP, CAP)
+        places.append((rows == row_ref[:, pl.ds(source, CAP)]).astype(F32).astype(BF16))
+    grad = jnp.dot(
+        jnp.concatenate(places, axis=1),
+        jnp.concatenate([ref[...] for ref in incoming], axis=0),
+        preferred_element_type=F32,
+    )
     grad_ref[...] = grad
     sums = jnp.sum(grad * grad, axis=1, keepdims=True)
     sum_ref[...] = jnp.broadcast_to(sums, (sums.shape[0], 128)).T[:1]
 
 
-def place_rows(incoming_rows, incoming, owned_rows, after=()):
-    cut = incoming.shape[1]
-    return call(
-        place_kernel,
+def place_rows(entry, plan, incoming_rows, incoming, owned_rows, after):
+    width = incoming[0].shape[1]
+    return call(
+        functools.partial(place_kernel, entry),
         "place_rows",
-        [VMEM] * 2,
+        [SMEM] + [VMEM] * (1 + len(incoming)),
         [
-            jax.ShapeDtypeStruct((owned_rows, cut), F32),
+            jax.ShapeDtypeStruct((owned_rows, width), F32),
             jax.ShapeDtypeStruct((1, owned_rows), F32),
         ],
-        [incoming_rows, incoming],
-        macs=incoming.size * owned_rows,
-        after=after,
-    )
-
-
-def adam_kernel(model_width, tier_ref, mean_ref, second_ref, grad_ref, *refs):
-    *sum_refs, new_mean_ref, new_second_ref, step_ref = refs
-    row_sum = sum_refs[0][...]
-    for ref in sum_refs[1:]:
-        row_sum = row_sum + ref[...]
-    scale = lax.rsqrt(row_sum / model_width + EPS_NORM)
-    hot = (tier_ref[...] == 1).astype(F32)
-    filler = jnp.zeros((126, scale.shape[1]), F32)
-    table = jnp.concatenate([scale, hot, filler], axis=0).T
-    is_hot = table[:, 1:2] > 0.5
+        [plan, incoming_rows, *incoming],
+        macs=incoming_rows.size * width * owned_rows,
+        after=after,
+    )
+
+
+def hot_kernel(tier_ref, mean_ref, second_ref, grad_ref, new_mean_ref, new_second_ref, step_ref):
+    hot = jnp.broadcast_to((tier_ref[...] == 1).astype(F32), (128, tier_ref.shape[1])).T
+    is_hot = hot[:, :1] > 0.5
     grad = grad_ref[...]
     mean_hot = 0.9 * mean_ref[...] + 0.1 * grad
     second_hot = 0.95 * second_ref[...] + 0.05 * grad * grad
     step_hot = mean_hot / FIRST_BIAS / (jnp.sqrt(second_hot / SECOND_BIAS) + EPS_ADAM)
     new_mean_ref[...] = jnp.where(is_hot, mean_hot, mean_ref[...])
     new_second_ref[...] = jnp.where(is_hot, second_hot, second_ref[...])
-    step_ref[...] = jnp.where(is_hot, step_hot, grad * table[:, :1])
+    step_ref[...] = jnp.where(is_hot, step_hot, grad)
+
+
+def cold_kernel(model_width, tier_ref, step_ref, *refs):
+    *sum_refs, out_ref = refs
+    row_sum = sum_refs[0][...]
+    for ref in sum_refs[1:]:
+        row_sum = row_sum + ref[...]
+    cold = lax.rsqrt(row_sum / model_width + EPS_NORM)
+    scale = jnp.where(tier_ref[...] == 1, 1.0, cold)
+    out_ref[...] = step_ref[...] * jnp.broadcast_to(scale, (128, scale.shape[1])).T[:, :1]
 
 
 def adam(model_width, row_tier, adam_mean, adam_second, row_grad, row_sums):
@@ -522,16 +533,29 @@
     tile = 128 if owned_rows % 128 == 0 else owned_rows
     rows = pl.BlockSpec((tile, width), lambda i: (i, 0))
     lanes = pl.BlockSpec((1, tile), lambda i: (0, i))
-    return pl.pallas_call(
-        functools.partial(adam_kernel, model_width),
+    tier = row_tier.reshape(1, -1)
+    shape = jax.ShapeDtypeStruct((owned_rows, width), F32)
+    make = functools.partial(
+        pl.pallas_call,
         grid=(owned_rows // tile,),
-        in_specs=[lanes] + [rows] * 3 + [lanes] * len(row_sums),
-        out_specs=[rows] * 3,
-        out_shape=[jax.ShapeDtypeStruct((owned_rows, width), F32)] * 3,
         compiler_params=pltpu.CompilerParams(vmem_limit_bytes=VMEM_BYTES),
         cost_estimate=pl.CostEstimate(flops=row_grad.size, bytes_accessed=0, transcendentals=0),
-        name="adam",
-    )(row_tier.reshape(1, -1), adam_mean, adam_second, row_grad, *row_sums)
+    )
+    new_mean, new_second, step = make(
+        hot_kernel,
+        in_specs=[lanes] + [rows] * 3,
+        out_specs=[rows] * 3,
+        out_shape=[shape] * 3,
+        name="adam_hot",
+    )(tier, adam_mean, adam_second, row_grad)
+    row_step = make(
+        functools.partial(cold_kernel, model_width),
+        in_specs=[lanes, rows] + [lanes] * len(row_sums),
+        out_specs=rows,
+        out_shape=shape,
+        name="adam_cold",
+    )(tier, step, *row_sums)
+    return new_mean, new_second, row_step
 
 
 def on_device(
@@ -632,6 +656,8 @@
             start += cut
             if k < len(between):
                 between[k]()
+        for rest in between[len(cuts) :]:
+            rest()
         passing[:] = parts
         turns += 1
 
@@ -644,7 +670,6 @@
         for rel in range(0, groups, 2):
             if bin(rel).count("1") != level:
                 continue
-            follows = rel != groups - 2
             product = in_order(
                 outer, shards + rel, plan, shard_rows, joined, other_joined, turned, other_turned
             )
@@ -655,28 +680,34 @@
                     waiting.append((way, rel, product[way]))
                 else:
                     send(way, rel, product[way])
-            if follows and rel and turns < shards - 3:
-                turn()
+        if 0 < level < len(bits) and turns < shards - 3:
+            turn()
         for way, rel, part in waiting:
             send(way, rel, in_order(add, part, *arrived.pop((way, rel))))
-    own_term = in_order(back, 0, joined, weights, cuts)
-    marks = in_order(mark_slots, slot_index, groups * CAP)
-    sums_to_do = [functools.partial(early_sum, way) for way in range(2)]
+    def finish(first):
+        nonlocal own_term, marks
+        if first:
+            own_term = in_order(back, 0, joined, weights, cuts)
+            early_sum(0)
+        else:
+            early_sum(1)
+            marks = in_order(mark_slots, shards, plan, slot_index, groups * CAP)
+
+    own_term = marks = None
     while turns < shards - 2:
-        turn(sums_to_do if True else ())
-        sums_to_do = () if True else sums_to_do
+        turn([functools.partial(finish, k == 0) for k in range(2)] if turns == shards - 3 else ())
     weight_sum = jnp.concatenate([sum(p.astype(F32) for p in parts) for parts in mine], axis=0)
     key_grad = key_grad_acc + jnp.stack(
         [weight_sum[:, j * width : (j + 1) * width] for j in range(key_count)]
     )
     value_grad = value_grad_acc + weight_sum[:, key_count * width :]
 
-    outgoing = pick_rows(marks, passing, own_term)
-    incoming = lax.all_to_all(
-        outgoing.reshape(groups, CAP, -1), "group", split_axis=0, concat_axis=0, tiled=True
-    ).reshape(groups * CAP, -1)
+    outgoing = pick_rows(marks, passing, own_term, ())
+    incoming = [outgoing[0]] + [None] * (groups - 1)
+    for rel in range(groups - 1, 0, -1):
+        incoming[rel] = swap_over("group", rel, outgoing[rel])
     row_grad, row_part = place_rows(
-        incoming_rows, incoming, owned_rows, (key_grad, value_grad)
+        shards, plan, incoming_rows, incoming, owned_rows, (key_grad, value_grad)
     )
     row_sums = [row_part] + others_over("tensor", row_part)
     new_mean, new_second, row_step = adam(

time: 147 us -> 141 us (0.959)
  waiting for transfers between devices: 48.1 us -> 40.4 us
  starting transfers between devices: 46.9 us -> 54 us
  other arithmetic: 3.83 us -> 0.73 us
  local copies, waits for them, and re-layouts: 10.3 us -> 8.09 us
    all_to_all x1 -> x0, waiting for transfers between devices: 13.6 us -> none  [on_device(): lax.all_to_all(outgoing.reshape(groups, CAP, -1), 'group', split_axis=0,...]
    ppermute x8 -> x15, waiting for transfers between devices: 0.46 us -> 10.5 us  [swap_over(): return lax.ppermute(part, axis, [(i, i ^ bit) for i in range(size)])]
    ppermute x8 -> x15, starting transfers between devices: 7.51 us -> 14.2 us  [swap_over(): return lax.ppermute(part, axis, [(i, i ^ bit) for i in range(size)])]
    ppermute x11, starting transfers between devices: 23.1 us -> 27.2 us  [ring_pass(): lax.ppermute(part, axis, [(order[i], order[(i + 1) % size]) for i in rang...]
    all_to_all x1 -> x0, starting transfers between devices: 3.72 us -> none  [on_device(): lax.all_to_all(outgoing.reshape(groups, CAP, -1), 'group', split_axis=0,...]
    add x2, other arithmetic: 2.51 us -> 0.27 us  [on_device(): sum((p.astype(F32) for p in parts))]
    unnamed x29 -> x25, local copies, waits for them, and re-layouts: 9.28 us -> 7.07 us
    ppermute x6, waiting for transfers between devices: 6.54 us -> 4.36 us  [others_over(): lax.ppermute(part, axis, [(i, i ^ step) for i in range(size)])]
  transfers between devices with their start and end apart: 27 -> 33, of which waited for: 14 -> 16; matrix products, arithmetic and copies ran while one was open for 3% -> 1% of each run, Pallas kernels for 20% -> 21%
where the time goes in v4:
time: 141 us; the launch traced here: 140 us
  starting transfers between devices  54 us (38%)
  waiting for transfers between devices  40.4 us (29%)
  Pallas kernels  36.1 us (26%)
  local copies, waits for them, and re-layouts  8.09 us (6%)
    pallas_call x26, Pallas kernels, call(): pl.pallas_call(body, in_specs=in_specs + [ANY] * len(after), out_specs=[V...  33.5 us
    ppermute x11, starting transfers between devices, ring_pass(): lax.ppermute(part, axis, [(order[i], order[(i + 1) % size]) for i in rang...  27.2 us
    ppermute x11, waiting for transfers between devices, ring_pass(): lax.ppermute(part, axis, [(order[i], order[(i + 1) % size]) for i in rang...  20.9 us
    ppermute x15, starting transfers between devices, swap_over(): return lax.ppermute(part, axis, [(i, i ^ bit) for i in range(size)])  14.2 us
    ppermute x15, waiting for transfers between devices, swap_over(): return lax.ppermute(part, axis, [(i, i ^ bit) for i in range(size)])  10.5 us
    ppermute x6, starting transfers between devices, others_over(): lax.ppermute(part, axis, [(i, i ^ step) for i in range(size)])  8.91 us
    unnamed x25, local copies, waits for them, and re-layouts  7.07 us
    all_to_all x1, waiting for transfers between devices, on_device(): lax.all_to_all(slot_row, 'group', split_axis=0, concat_axis=0, tiled=True)  4.58 us
  transfers between devices with their start and end apart: 33, of which 16 were waited for; matrix products, arithmetic and copies ran while one was open for 1% of the time, Pallas kernels for 21%

profile of v4, /device:TPU:0, one launch (start us, length us, event | category | flops | bytes accessed | tf_op | source)
XLA Modules:
  0.0 140.4 jit_solution(3638982451268899880)
XLA Ops:
  2.2 4.1 %collective-permute-start = (bf16[256,640]{1,0:T(8,128)(2,1)S(1)}, bf16[256,640]{1,0:T(8,128)(2,1)}, u32[]{:S(2)}, u32[]{:S(2)}) collective-permute-start(bf16[256,640]{1,0:T(8,128)(2,1)S(1)} %sum_rows.2.refs_1_.refs_2_), channel_id=1, source_target_pairs={{0,2},{2,3},{3,1},{1,0},{4,6},{6,7},{7,5},{5,4},{8,10},{10,11},{11... | collective-permute-start | bytes 983048 | tf_op jit(solution)/shard_map/ppermute | solution.py:57
  9.9 3.7 %all-to-all-start = ((s32[8,1,128]{2,1,0:T(1,128)}), s32[8,1,128]{2,1,0:T(1,128)S(1)}, u32[]{:S(2)}, u32[]{:S(2)}) async-start(s32[8,1,128]{2,1,0:T(1,128)} %bitcast.6), calls=%async_computation | async-start | bytes 8192 | tf_op jit(solution)/shard_map/all_to_all | solution.py:605
  13.6 4.6 %all-to-all-done = s32[8,1,128]{2,1,0:T(1,128)S(1)} async-done(((s32[8,1,128]{2,1,0:T(1,128)}), s32[8,1,128]{2,1,0:T(1,128)S(1)}, u32[]{:S(2)}, u32[]{:S(2)}) %all-to-all-start) | async-done | bytes 4128 | tf_op jit(solution)/shard_map/all_to_all | solution.py:605
  18.6 2.9 %collective-permute-done.3.refs_6_ = bf16[256,640]{1,0:T(8,128)(2,1)} collective-permute-done((bf16[256,640]{1,0:T(8,128)(2,1)S(1)}, bf16[256,640]{1,0:T(8,128)(2,1)}, u32[]{:S(2)}, u32[]{:S(2)}) %collective-permute-start.3) | collective-permute-done | bytes 327712 | tf_op jit(solution)/shard_map/ppermute | solution.py:57
  21.4 3.5 %collective-permute-start.4 = (bf16[256,640]{1,0:T(8,128)(2,1)}, bf16[256,640]{1,0:T(8,128)(2,1)S(1)}, u32[]{:S(2)}, u32[]{:S(2)}) collective-permute-start(bf16[256,640]{1,0:T(8,128)(2,1)} %collective-permute-done.3.refs_6_), channel_id=1, source_target_pairs={{0,2},{2,3},{3,1},{1,0},{4,6},{6,7},{7,5},{5,4},{8,10},{10,11},{11... | collective-permute-start | bytes 983048 | tf_op jit(solution)/shard_map/ppermute | solution.py:57
  25.7 2.9 %copy-done = bf16[2,2560,640]{2,1,0:T(8,128)(2,1)S(1)} copy-done((bf16[2,2560,640]{2,1,0:T(8,128)(2,1)S(1)}, bf16[2,2560,640]{2,1,0:T(8,128)(2,1)}, u32[]{:S(2)}) %copy-start) | copy-done | bytes 6553624
  28.6 1.9 %copy-done.3 = bf16[2560,640]{1,0:T(8,128)(2,1)S(1)} copy-done((bf16[2560,640]{1,0:T(8,128)(2,1)S(1)}, bf16[2560,640]{1,0:T(8,128)(2,1)}, u32[]{:S(2)}) %copy-start.3) | copy-done | bytes 3276824
  32.8 3.3 %collective-permute-done.4.refs_0_ = bf16[256,640]{1,0:T(8,128)(2,1)S(1)} collective-permute-done((bf16[256,640]{1,0:T(8,128)(2,1)}, bf16[256,640]{1,0:T(8,128)(2,1)S(1)}, u32[]{:S(2)}, u32[]{:S(2)}) %collective-permute-start.4) | collective-permute-done | bytes 327712 | tf_op jit(solution)/shard_map/ppermute | solution.py:57
  36.1 2.8 %collective-permute-start.5 = (bf16[256,640]{1,0:T(8,128)(2,1)S(1)}, bf16[256,640]{1,0:T(8,128)(2,1)S(1)}, u32[]{:S(2)}, u32[]{:S(2)}) collective-permute-start(bf16[256,640]{1,0:T(8,128)(2,1)S(1)} %after.3.refs_7_), channel_id=1, source_target_pairs={{0,2},{2,3},{3,1},{1,0},{4,6},{6,7},{7,5},{5,4},{8,10},{10,11},{11... | collective-permute-start | bytes 983048 | tf_op jit(solution)/shard_map/ppermute | solution.py:57
  38.9 6.1 %forward_early.1 = (f32[3,512,640]{2,1,0:T(8,128)S(1)}, bf16[2560,512]{1,0:T(8,128)(2,1)S(1)}) custom-call(s32[12]{0:T(128)S(1)} %pad_add_fusion.refs_0_, bf16[2560,1920]{1,0:T(8,128)(2,1)S(1)} %join_weights.1.refs_1_, bf16[256,640]{1,0:T(8,128)(2,1)S(1)} %sum_rows.2.refs_1_.refs_2_, bf16[256,640]{1,0:T(8,128)(2,1)} %after.2.refs_3_, ...), custom_call_target="tpu_custom_call" | custom-call | flops 188743680 | tf_op jit(solution)/shard_map/forward_early/pallas_call | solution.py:37
  45.0 4.0 %collective-permute-done.5.refs_3_ = bf16[256,640]{1,0:T(8,128)(2,1)S(1)} collective-permute-done((bf16[256,640]{1,0:T(8,128)(2,1)S(1)}, bf16[256,640]{1,0:T(8,128)(2,1)S(1)}, u32[]{:S(2)}, u32[]{:S(2)}) %collective-permute-start.5) | collective-permute-done | bytes 327712 | tf_op jit(solution)/shard_map/ppermute | solution.py:57
  48.9 3.3 %forward_late.1 = (f32[3,512,640]{2,1,0:T(8,128)S(1)}, bf16[2560,512]{1,0:T(8,128)(2,1)S(1)}, f32[8,512]{1,0:T(8,128)S(1)}) custom-call(s32[12]{0:T(128)S(1)} %pad_add_fusion.refs_0_, bf16[2560,1920]{1,0:T(8,128)(2,1)S(1)} %join_weights.1.refs_1_, bf16[256,640]{1,0:T(8,128)(2,1)S(1)} %collective-permute-done.2.refs_2_, ...), custom_call_target="tpu_custom_call", output_to_operand_aliasing={{0}: (4, {}), {1}: (5, {})} | custom-call | flops 62914560 | tf_op jit(solution)/shard_map/forward_late/pallas_call | solution.py:37
  52.4 3.0 %collective-permute-start.8 = (f32[8,512]{1,0:T(8,128)S(1)}, f32[8,512]{1,0:T(8,128)S(1)}, u32[]{:S(2)}, u32[]{:S(2)}) collective-permute-start(f32[8,512]{1,0:T(8,128)S(1)} %get-tuple-element.46.refs_0_), channel_id=1, source_target_pairs={{0,3},{1,2},{2,1},{3,0},{4,7},{5,6},{6,5},{7,4},{8,11},{9,10},{10,... | collective-permute-start | bytes 49160 | tf_op jit(solution)/shard_map/ppermute | solution.py:63
  58.0 2.1 %collective-permute-done.7.refs_2_ = f32[8,512]{1,0:T(8,128)S(1)} collective-permute-done((f32[8,512]{1,0:T(8,128)S(1)}, f32[8,512]{1,0:T(8,128)S(1)}, u32[]{:S(2)}, u32[]{:S(2)}) %collective-permute-start.7) | collective-permute-done | bytes 16416 | tf_op jit(solution)/shard_map/ppermute | solution.py:63
  61.4 1.8 %back.4.refs_5_ = bf16[512,640]{1,0:T(8,128)(2,1)S(1)} custom-call(bf16[512,1920]{1,0:T(8,128)(2,1)S(1)} %cotangents.1.refs_0_.refs_1_, bf16[2560,1920]{1,0:T(8,128)(2,1)S(1)} %join_weights.1.refs_1_), custom_call_target="tpu_custom_call" | custom-call | flops 62914560 | tf_op jit(solution)/shard_map/back/pallas_call | solution.py:37
  63.2 2.2 %collective-permute-start.13 = (bf16[512,640]{1,0:T(8,128)(2,1)S(1)}, bf16[512,640]{1,0:T(8,128)(2,1)S(1)}, u32[]{:S(2)}, u32[]{:S(2)}) collective-permute-start(bf16[512,640]{1,0:T(8,128)(2,1)S(1)} %back.4.refs_5_), channel_id=1, source_target_pairs={{0,2},{2,3},{3,1},{1,0},{4,6},{6,7},{7,5},{5,4},{8,10},{10,11},{11... | collective-permute-start | bytes 1966088 | tf_op jit(solution)/shard_map/ppermute | solution.py:57
  65.4 2.1 %outer.4 = (bf16[160,1920]{1,0:T(8,128)(2,1)S(1)}, bf16[160,1920]{1,0:T(8,128)(2,1)S(1)}) custom-call(s32[12]{0:T(128)S(1)} %pad_add_fusion.refs_0_, bf16[512,1920]{1,0:T(8,128)(2,1)S(1)} %cotangents.1.refs_0_.refs_1_, bf16[512,1920]{1,0:T(8,128)(2,1)S(1)} %collective-permute-done.10.refs_2_, bf16[2560,512]{1,0:T(8,128)(2,1)S(1)} %get-tuple-element.48.refs_3_, ...), custom_call_target="tpu_custom_call" | custom-call | flops 62914560 | tf_op jit(solution)/shard_map/outer/pallas_call | solution.py:37
  70.6 2.1 %outer.5 = (bf16[160,1920]{1,0:T(8,128)(2,1)S(1)}, bf16[160,1920]{1,0:T(8,128)(2,1)S(1)}) custom-call(s32[12]{0:T(128)S(1)} %pad_add_fusion.refs_0_, bf16[512,1920]{1,0:T(8,128)(2,1)S(1)} %cotangents.1.refs_0_.refs_1_, bf16[512,1920]{1,0:T(8,128)(2,1)S(1)} %collective-permute-done.10.refs_2_, bf16[2560,512]{1,0:T(8,128)(2,1)S(1)} %get-tuple-element.48.refs_3_, ...), custom_call_target="tpu_custom_call" | custom-call | flops 62914560 | tf_op jit(solution)/shard_map/outer/pallas_call | solution.py:37
  73.2 2.1 %outer.6 = (bf16[160,1920]{1,0:T(8,128)(2,1)S(1)}, bf16[160,1920]{1,0:T(8,128)(2,1)S(1)}) custom-call(s32[12]{0:T(128)S(1)} %pad_add_fusion.refs_0_, bf16[512,1920]{1,0:T(8,128)(2,1)S(1)} %cotangents.1.refs_0_.refs_1_, bf16[512,1920]{1,0:T(8,128)(2,1)S(1)} %collective-permute-done.10.refs_2_, bf16[2560,512]{1,0:T(8,128)(2,1)S(1)} %get-tuple-element.48.refs_3_, ...), custom_call_target="tpu_custom_call" | custom-call | flops 62914560 | tf_op jit(solution)/shard_map/outer/pallas_call | solution.py:37
  75.3 1.8 %back.5 = (bf16[512,384]{1,0:T(8,128)(2,1)S(1)}, bf16[512,256]{1,0:T(8,128)(2,1)S(1)}) custom-call(bf16[512,1920]{1,0:T(8,128)(2,1)S(1)} %cotangents.1.refs_0_.refs_1_, bf16[2560,1920]{1,0:T(8,128)(2,1)S(1)} %join_weights.1.refs_1_, bf16[160,1920]{1,0:T(8,128)(2,1)S(1)} %get-tuple-element.51.refs_2_.refs_0_), custom_call_target="tpu_custom_call" | custom-call | flops 62914560 | tf_op jit(solution)/shard_map/back/pallas_call | solution.py:37
  77.1 3.4 %collective-permute-done.13.refs_0_ = bf16[512,640]{1,0:T(8,128)(2,1)S(1)} collective-permute-done((bf16[512,640]{1,0:T(8,128)(2,1)S(1)}, bf16[512,640]{1,0:T(8,128)(2,1)S(1)}, u32[]{:S(2)}, u32[]{:S(2)}) %collective-permute-start.13) | collective-permute-done | bytes 655392 | tf_op jit(solution)/shard_map/ppermute | solution.py:57
  80.7 2.9 %collective-permute-start.15 = (bf16[512,384]{1,0:T(8,128)(2,1)S(1)}, bf16[512,384]{1,0:T(8,128)(2,1)S(1)}, u32[]{:S(2)}, u32[]{:S(2)}) collective-permute-start(bf16[512,384]{1,0:T(8,128)(2,1)S(1)} %add_part.4.refs_2_), channel_id=1, source_target_pairs={{0,2},{2,3},{3,1},{1,0},{4,6},{6,7},{7,5},{5,4},{8,10},{10,11},{11... | collective-permute-start | bytes 1179656 | tf_op jit(solution)/shard_map/ppermute | solution.py:57
  86.5 1.9 %collective-permute-start.18 = (bf16[512,256]{1,0:T(8,128)(2,1)S(1)}, bf16[512,256]{1,0:T(8,128)(2,1)S(1)}, u32[]{:S(2)}, u32[]{:S(2)}) collective-permute-start(bf16[512,256]{1,0:T(8,128)(2,1)S(1)} %add_part.5.refs_2_), channel_id=1, source_target_pairs={{0,2},{2,3},{3,1},{1,0},{4,6},{6,7},{7,5},{5,4},{8,10},{10,11},{11... | collective-permute-start | bytes 786440 | tf_op jit(solution)/shard_map/ppermute | solution.py:57
  88.4 2.1 %outer.7 = (bf16[160,1920]{1,0:T(8,128)(2,1)S(1)}, bf16[160,1920]{1,0:T(8,128)(2,1)S(1)}) custom-call(s32[12]{0:T(128)S(1)} %pad_add_fusion.refs_0_, bf16[512,1920]{1,0:T(8,128)(2,1)S(1)} %cotangents.1.refs_0_.refs_1_, bf16[512,1920]{1,0:T(8,128)(2,1)S(1)} %collective-permute-done.10.refs_2_, bf16[2560,512]{1,0:T(8,128)(2,1)S(1)} %get-tuple-element.48.refs_3_, ...), custom_call_target="tpu_custom_call" | custom-call | flops 62914560 | tf_op jit(solution)/shard_map/outer/pallas_call | solution.py:37
  90.5 1.8 %back.6 = (bf16[512,384]{1,0:T(8,128)(2,1)S(1)}, bf16[512,256]{1,0:T(8,128)(2,1)S(1)}) custom-call(bf16[512,1920]{1,0:T(8,128)(2,1)S(1)} %cotangents.1.refs_0_.refs_1_, bf16[2560,1920]{1,0:T(8,128)(2,1)S(1)} %join_weights.1.refs_1_, bf16[160,1920]{1,0:T(8,128)(2,1)S(1)} %get-tuple-element.56.refs_2_.refs_0_), custom_call_target="tpu_custom_call" | custom-call | flops 62914560 | tf_op jit(solution)/shard_map/back/pallas_call | solution.py:37
  93.2 3.4 %collective-permute-start.20 = (bf16[512,384]{1,0:T(8,128)(2,1)S(1)}, bf16[512,384]{1,0:T(8,128)(2,1)S(1)}, u32[]{:S(2)}, u32[]{:S(2)}) collective-permute-start(bf16[512,384]{1,0:T(8,128)(2,1)S(1)} %add_part.6.refs_2_), channel_id=1, source_target_pairs={{0,2},{2,3},{3,1},{1,0},{4,6},{6,7},{7,5},{5,4},{8,10},{10,11},{11... | collective-permute-start | bytes 1179656 | tf_op jit(solution)/shard_map/ppermute | solution.py:57
  96.7 1.8 %back.7 = (bf16[512,384]{1,0:T(8,128)(2,1)S(1)}, bf16[512,256]{1,0:T(8,128)(2,1)S(1)}) custom-call(bf16[512,1920]{1,0:T(8,128)(2,1)S(1)} %cotangents.1.refs_0_.refs_1_, bf16[2560,1920]{1,0:T(8,128)(2,1)S(1)} %join_weights.1.refs_1_, bf16[512,384]{1,0:T(8,128)(2,1)S(1)} %add_part.6.refs_2_), custom_call_target="tpu_custom_call" | custom-call | flops 62914560 | tf_op jit(solution)/shard_map/back/pallas_call | solution.py:37
  98.8 3.7 %collective-permute-start.21 = (bf16[512,256]{1,0:T(8,128)(2,1)S(1)}, bf16[512,256]{1,0:T(8,128)(2,1)S(1)}, u32[]{:S(2)}, u32[]{:S(2)}) collective-permute-start(bf16[512,256]{1,0:T(8,128)(2,1)S(1)} %add_part.7.refs_2_), channel_id=1, source_target_pairs={{0,2},{2,3},{3,1},{1,0},{4,6},{6,7},{7,5},{5,4},{8,10},{10,11},{11... | collective-permute-start | bytes 786440 | tf_op jit(solution)/shard_map/ppermute | solution.py:57
  105.1 6.5 %collective-permute-done.21.refs_2_ = bf16[512,256]{1,0:T(8,128)(2,1)S(1)} collective-permute-done((bf16[512,256]{1,0:T(8,128)(2,1)S(1)}, bf16[512,256]{1,0:T(8,128)(2,1)S(1)}, u32[]{:S(2)}, u32[]{:S(2)}) %collective-permute-start.21) | collective-permute-done | bytes 262176 | tf_op jit(solution)/shard_map/ppermute | solution.py:57
  117.6 1.9 %collective-permute-start.27 = (bf16[128,640]{1,0:T(8,128)(2,1)S(1)}, bf16[128,640]{1,0:T(8,128)(2,1)S(1)}, u32[]{:S(2)}, u32[]{:S(2)}) collective-permute-start(bf16[128,640]{1,0:T(8,128)(2,1)S(1)} %get-tuple-element.70), channel_id=1, source_target_pairs={{0,24},{4,28},{8,16},{12,20},{16,8},{20,12},{24,0},{28,4},{1,25},{... | collective-permute-start | bytes 491528 | tf_op jit(solution)/shard_map/ppermute | solution.py:70
  122.3 8.6 %collective-permute-done.26.refs_7_ = bf16[128,640]{1,0:T(8,128)(2,1)S(1)} collective-permute-done((bf16[128,640]{1,0:T(8,128)(2,1)S(1)}, bf16[128,640]{1,0:T(8,128)(2,1)S(1)}, u32[]{:S(2)}, u32[]{:S(2)}) %collective-permute-start.26) | collective-permute-done | bytes 163872 | tf_op jit(solution)/shard_map/ppermute | solution.py:70
  132.2 2.3 %collective-permute-start.31 = (f32[1,256]{1,0:T(1,128)S(1)}, f32[1,256]{1,0:T(1,128)S(1)}, u32[]{:S(2)}, u32[]{:S(2)}) collective-permute-start(f32[1,256]{1,0:T(1,128)S(1)} %get-tuple-element.76.refs_0_), channel_id=1, source_target_pairs={{0,3},{1,2},{2,1},{3,0},{4,7},{5,6},{6,5},{7,4},{8,11},{9,10},{10,... | collective-permute-start | bytes 3080 | tf_op jit(solution)/shard_map/ppermute | solution.py:63
  (97 shorter events, 39.0 us)
Async XLA Ops:
  2.2 16.0 %collective-permute-start = (bf16[256,640]{1,0:T(8,128)(2,1)S(1)}, bf16[256,640]{1,0:T(8,128)(2,1)}, u32[]{:S(2)}, u32[]{:S(2)}) collective-permute-start(bf16[256,640]{1,0:T(8,128)(2,1)S(1)} %sum_rows.2.refs_1_.refs_2_), channel_id=1, source_target_pairs={{0,2},{2,3},{3,1},{1,0},{4,6},{6,7},{7,5},{5,4},{8,10},{10,11},{11... | collective-permute-start | bytes 983048 | tf_op jit(solution)/shard_map/ppermute | solution.py:57
  6.4 15.0 %collective-permute-start.3 = (bf16[256,640]{1,0:T(8,128)(2,1)S(1)}, bf16[256,640]{1,0:T(8,128)(2,1)}, u32[]{:S(2)}, u32[]{:S(2)}) collective-permute-start(bf16[256,640]{1,0:T(8,128)(2,1)S(1)} %sum_rows.3.refs_1_.refs_5_), channel_id=1, source_target_pairs={{0,2},{2,3},{3,1},{1,0},{4,6},{6,7},{7,5},{5,4},{8,10},{10,11},{11... | collective-permute-start | bytes 983048 | tf_op jit(solution)/shard_map/ppermute | solution.py:57
  9.9 8.3 %all-to-all-start = ((s32[8,1,128]{2,1,0:T(1,128)}), s32[8,1,128]{2,1,0:T(1,128)S(1)}, u32[]{:S(2)}, u32[]{:S(2)}) async-start(s32[8,1,128]{2,1,0:T(1,128)} %bitcast.6), calls=%async_computation | async-start | bytes 8192 | tf_op jit(solution)/shard_map/all_to_all | solution.py:605
  18.2 13.8 %collective-permute-start.1 = (bf16[256,640]{1,0:T(8,128)(2,1)}, bf16[256,640]{1,0:T(8,128)(2,1)S(1)}, u32[]{:S(2)}, u32[]{:S(2)}) collective-permute-start(bf16[256,640]{1,0:T(8,128)(2,1)} %after.2.refs_3_), channel_id=1, source_target_pairs={{0,2},{2,3},{3,1},{1,0},{4,6},{6,7},{7,5},{5,4},{8,10},{10,11},{11... | collective-permute-start | bytes 983048 | tf_op jit(solution)/shard_map/ppermute | solution.py:57
  21.4 14.6 %collective-permute-start.4 = (bf16[256,640]{1,0:T(8,128)(2,1)}, bf16[256,640]{1,0:T(8,128)(2,1)S(1)}, u32[]{:S(2)}, u32[]{:S(2)}) collective-permute-start(bf16[256,640]{1,0:T(8,128)(2,1)} %collective-permute-done.3.refs_6_), channel_id=1, source_target_pairs={{0,2},{2,3},{3,1},{1,0},{4,6},{6,7},{7,5},{5,4},{8,10},{10,11},{11... | collective-permute-start | bytes 983048 | tf_op jit(solution)/shard_map/ppermute | solution.py:57
  32.1 12.9 %collective-permute-start.2 = (bf16[256,640]{1,0:T(8,128)(2,1)S(1)}, bf16[256,640]{1,0:T(8,128)(2,1)S(1)}, u32[]{:S(2)}, u32[]{:S(2)}) collective-permute-start(bf16[256,640]{1,0:T(8,128)(2,1)S(1)} %collective-permute-done.1.refs_4_), channel_id=1, source_target_pairs={{0,2},{2,3},{3,1},{1,0},{4,6},{6,7},{7,5},{5,4},{8,10},{10,11},{11... | collective-permute-start | bytes 983048 | tf_op jit(solution)/shard_map/ppermute | solution.py:57
  36.1 12.9 %collective-permute-start.5 = (bf16[256,640]{1,0:T(8,128)(2,1)S(1)}, bf16[256,640]{1,0:T(8,128)(2,1)S(1)}, u32[]{:S(2)}, u32[]{:S(2)}) collective-permute-start(bf16[256,640]{1,0:T(8,128)(2,1)S(1)} %after.3.refs_7_), channel_id=1, source_target_pairs={{0,2},{2,3},{3,1},{1,0},{4,6},{6,7},{7,5},{5,4},{8,10},{10,11},{11... | collective-permute-start | bytes 983048 | tf_op jit(solution)/shard_map/ppermute | solution.py:57
  52.3 7.8 %collective-permute-start.9 = (bf16[2560,512]{1,0:T(8,128)(2,1)S(1)}, bf16[2560,512]{1,0:T(8,128)(2,1)S(1)}, u32[]{:S(2)}, u32[]{:S(2)}) collective-permute-start(bf16[2560,512]{1,0:T(8,128)(2,1)S(1)} %get-tuple-element.48.refs_3_), channel_id=1, source_target_pairs={{0,4},{4,0},{8,12},{12,8},{16,20},{20,16},{24,28},{28,24},{1,5},{5... | collective-permute-start | bytes 7864328 | tf_op jit(solution)/shard_map/ppermute | solution.py:70
  52.4 5.6 %collective-permute-start.8 = (f32[8,512]{1,0:T(8,128)S(1)}, f32[8,512]{1,0:T(8,128)S(1)}, u32[]{:S(2)}, u32[]{:S(2)}) collective-permute-start(f32[8,512]{1,0:T(8,128)S(1)} %get-tuple-element.46.refs_0_), channel_id=1, source_target_pairs={{0,3},{1,2},{2,1},{3,0},{4,7},{5,6},{6,5},{7,4},{8,11},{9,10},{10,... | collective-permute-start | bytes 49160 | tf_op jit(solution)/shard_map/ppermute | solution.py:63
  55.4 4.7 %collective-permute-start.7 = (f32[8,512]{1,0:T(8,128)S(1)}, f32[8,512]{1,0:T(8,128)S(1)}, u32[]{:S(2)}, u32[]{:S(2)}) collective-permute-start(f32[8,512]{1,0:T(8,128)S(1)} %get-tuple-element.46.refs_0_), channel_id=1, source_target_pairs={{0,2},{1,3},{2,0},{3,1},{4,6},{5,7},{6,4},{7,5},{8,10},{9,11},{10,... | collective-permute-start | bytes 49160 | tf_op jit(solution)/shard_map/ppermute | solution.py:63
  55.7 4.4 %collective-permute-start.6 = (f32[8,512]{1,0:T(8,128)S(1)}, f32[8,512]{1,0:T(8,128)S(1)}, u32[]{:S(2)}, u32[]{:S(2)}) collective-permute-start(f32[8,512]{1,0:T(8,128)S(1)} %get-tuple-element.46.refs_0_), channel_id=1, source_target_pairs={{0,1},{1,0},{2,3},{3,2},{4,5},{5,4},{6,7},{7,6},{8,9},{9,8},{10,11... | collective-permute-start | bytes 49160 | tf_op jit(solution)/shard_map/ppermute | solution.py:63
  61.3 4.1 %collective-permute-start.10 = (bf16[512,1920]{1,0:T(8,128)(2,1)S(1)}, bf16[512,1920]{1,0:T(8,128)(2,1)S(1)}, u32[]{:S(2)}, u32[]{:S(2)}) collective-permute-start(bf16[512,1920]{1,0:T(8,128)(2,1)S(1)} %cotangents.1.refs_0_.refs_1_), channel_id=1, source_target_pairs={{0,4},{4,0},{8,12},{12,8},{16,20},{20,16},{24,28},{28,24},{1,5},{5... | collective-permute-start | bytes 5898248 | tf_op jit(solution)/shard_map/ppermute | solution.py:70
  63.2 17.4 %collective-permute-start.13 = (bf16[512,640]{1,0:T(8,128)(2,1)S(1)}, bf16[512,640]{1,0:T(8,128)(2,1)S(1)}, u32[]{:S(2)}, u32[]{:S(2)}) collective-permute-start(bf16[512,640]{1,0:T(8,128)(2,1)S(1)} %back.4.refs_5_), channel_id=1, source_target_pairs={{0,2},{2,3},{3,1},{1,0},{4,6},{6,7},{7,5},{5,4},{8,10},{10,11},{11... | collective-permute-start | bytes 1966088 | tf_op jit(solution)/shard_map/ppermute | solution.py:57
  67.5 17.7 %collective-permute-start.12 = (bf16[160,1920]{1,0:T(8,128)(2,1)S(1)}, bf16[160,1920]{1,0:T(8,128)(2,1)S(1)}, u32[]{:S(2)}, u32[]{:S(2)}) collective-permute-start(bf16[160,1920]{1,0:T(8,128)(2,1)S(1)} %get-tuple-element.53), channel_id=1, source_target_pairs={{0,16},{4,20},{8,24},{12,28},{16,0},{20,4},{24,8},{28,12},{1,17},{... | collective-permute-start | bytes 1843208 | tf_op jit(solution)/shard_map/ppermute | solution.py:70
  69.1 16.7 %collective-permute-start.11 = (bf16[160,1920]{1,0:T(8,128)(2,1)S(1)}, bf16[160,1920]{1,0:T(8,128)(2,1)S(1)}, u32[]{:S(2)}, u32[]{:S(2)}) collective-permute-start(bf16[160,1920]{1,0:T(8,128)(2,1)S(1)} %get-tuple-element.49.refs_5_), channel_id=1, source_target_pairs={{0,8},{4,12},{8,0},{12,4},{16,24},{20,28},{24,16},{28,20},{1,9},{5... | collective-permute-start | bytes 1843208 | tf_op jit(solution)/shard_map/ppermute | solution.py:70
  72.7 25.8 %collective-permute-start.14 = (bf16[160,1920]{1,0:T(8,128)(2,1)S(1)}, bf16[160,1920]{1,0:T(8,128)(2,1)S(1)}, u32[]{:S(2)}, u32[]{:S(2)}) collective-permute-start(bf16[160,1920]{1,0:T(8,128)(2,1)S(1)} %get-tuple-element.50.refs_5_), channel_id=1, source_target_pairs={{0,8},{4,12},{8,0},{12,4},{16,24},{20,28},{24,16},{28,20},{1,9},{5... | collective-permute-start | bytes 1843208 | tf_op jit(solution)/shard_map/ppermute | solution.py:70
  80.7 12.4 %collective-permute-start.15 = (bf16[512,384]{1,0:T(8,128)(2,1)S(1)}, bf16[512,384]{1,0:T(8,128)(2,1)S(1)}, u32[]{:S(2)}, u32[]{:S(2)}) collective-permute-start(bf16[512,384]{1,0:T(8,128)(2,1)S(1)} %add_part.4.refs_2_), channel_id=1, source_target_pairs={{0,2},{2,3},{3,1},{1,0},{4,6},{6,7},{7,5},{5,4},{8,10},{10,11},{11... | collective-permute-start | bytes 1179656 | tf_op jit(solution)/shard_map/ppermute | solution.py:57
  83.6 20.4 %collective-permute-start.17 = (bf16[160,1920]{1,0:T(8,128)(2,1)S(1)}, bf16[160,1920]{1,0:T(8,128)(2,1)S(1)}, u32[]{:S(2)}, u32[]{:S(2)}) collective-permute-start(bf16[160,1920]{1,0:T(8,128)(2,1)S(1)} %get-tuple-element.60), channel_id=1, source_target_pairs={{0,16},{4,20},{8,24},{12,28},{16,0},{20,4},{24,8},{28,12},{1,17},{... | collective-permute-start | bytes 1843208 | tf_op jit(solution)/shard_map/ppermute | solution.py:70
  85.9 28.6 %collective-permute-start.16 = (bf16[160,1920]{1,0:T(8,128)(2,1)S(1)}, bf16[160,1920]{1,0:T(8,128)(2,1)S(1)}, u32[]{:S(2)}, u32[]{:S(2)}) collective-permute-start(bf16[160,1920]{1,0:T(8,128)(2,1)S(1)} %add.32.refs_5_), channel_id=1, source_target_pairs={{0,16},{4,20},{8,24},{12,28},{16,0},{20,4},{24,8},{28,12},{1,17},{... | collective-permute-start | bytes 1843208 | tf_op jit(solution)/shard_map/ppermute | solution.py:70
  86.5 12.2 %collective-permute-start.18 = (bf16[512,256]{1,0:T(8,128)(2,1)S(1)}, bf16[512,256]{1,0:T(8,128)(2,1)S(1)}, u32[]{:S(2)}, u32[]{:S(2)}) collective-permute-start(bf16[512,256]{1,0:T(8,128)(2,1)S(1)} %add_part.5.refs_2_), channel_id=1, source_target_pairs={{0,2},{2,3},{3,1},{1,0},{4,6},{6,7},{7,5},{5,4},{8,10},{10,11},{11... | collective-permute-start | bytes 786440 | tf_op jit(solution)/shard_map/ppermute | solution.py:57
  93.2 18.3 %collective-permute-start.20 = (bf16[512,384]{1,0:T(8,128)(2,1)S(1)}, bf16[512,384]{1,0:T(8,128)(2,1)S(1)}, u32[]{:S(2)}, u32[]{:S(2)}) collective-permute-start(bf16[512,384]{1,0:T(8,128)(2,1)S(1)} %add_part.6.refs_2_), channel_id=1, source_target_pairs={{0,2},{2,3},{3,1},{1,0},{4,6},{6,7},{7,5},{5,4},{8,10},{10,11},{11... | collective-permute-start | bytes 1179656 | tf_op jit(solution)/shard_map/ppermute | solution.py:57
  98.8 12.7 %collective-permute-start.21 = (bf16[512,256]{1,0:T(8,128)(2,1)S(1)}, bf16[512,256]{1,0:T(8,128)(2,1)S(1)}, u32[]{:S(2)}, u32[]{:S(2)}) collective-permute-start(bf16[512,256]{1,0:T(8,128)(2,1)S(1)} %add_part.7.refs_2_), channel_id=1, source_target_pairs={{0,2},{2,3},{3,1},{1,0},{4,6},{6,7},{7,5},{5,4},{8,10},{10,11},{11... | collective-permute-start | bytes 786440 | tf_op jit(solution)/shard_map/ppermute | solution.py:57
  102.5 13.7 %collective-permute-start.19 = (bf16[160,1920]{1,0:T(8,128)(2,1)S(1)}, bf16[160,1920]{1,0:T(8,128)(2,1)S(1)}, u32[]{:S(2)}, u32[]{:S(2)}) collective-permute-start(bf16[160,1920]{1,0:T(8,128)(2,1)S(1)} %add.31.refs_2_), channel_id=1, source_target_pairs={{0,8},{4,12},{8,0},{12,4},{16,24},{20,28},{24,16},{28,20},{1,9},{5... | collective-permute-start | bytes 1843208 | tf_op jit(solution)/shard_map/ppermute | solution.py:70
  112.6 5.0 %collective-permute-start.22 = (bf16[128,640]{1,0:T(8,128)(2,1)S(1)}, bf16[128,640]{1,0:T(8,128)(2,1)S(1)}, u32[]{:S(2)}, u32[]{:S(2)}) collective-permute-start(bf16[128,640]{1,0:T(8,128)(2,1)S(1)} %get-tuple-element.65), channel_id=1, source_target_pairs={{0,4},{4,0},{8,12},{12,8},{16,20},{20,16},{24,28},{28,24},{1,5},{5... | collective-permute-start | bytes 491528 | tf_op jit(solution)/shard_map/ppermute | solution.py:70
  112.6 7.1 %collective-permute-start.23 = (bf16[128,640]{1,0:T(8,128)(2,1)S(1)}, bf16[128,640]{1,0:T(8,128)(2,1)S(1)}, u32[]{:S(2)}, u32[]{:S(2)}) collective-permute-start(bf16[128,640]{1,0:T(8,128)(2,1)S(1)} %get-tuple-element.66), channel_id=1, source_target_pairs={{0,8},{4,12},{8,0},{12,4},{16,24},{20,28},{24,16},{28,20},{1,9},{5... | collective-permute-start | bytes 491528 | tf_op jit(solution)/shard_map/ppermute | solution.py:70
  114.2 8.1 %collective-permute-start.24 = (bf16[128,640]{1,0:T(8,128)(2,1)S(1)}, bf16[128,640]{1,0:T(8,128)(2,1)S(1)}, u32[]{:S(2)}, u32[]{:S(2)}) collective-permute-start(bf16[128,640]{1,0:T(8,128)(2,1)S(1)} %get-tuple-element.67), channel_id=1, source_target_pairs={{0,12},{4,8},{8,4},{12,0},{16,28},{20,24},{24,20},{28,16},{1,13},{... | collective-permute-start | bytes 491528 | tf_op jit(solution)/shard_map/ppermute | solution.py:70
  114.5 7.8 %collective-permute-start.25 = (bf16[128,640]{1,0:T(8,128)(2,1)S(1)}, bf16[128,640]{1,0:T(8,128)(2,1)S(1)}, u32[]{:S(2)}, u32[]{:S(2)}) collective-permute-start(bf16[128,640]{1,0:T(8,128)(2,1)S(1)} %get-tuple-element.68), channel_id=1, source_target_pairs={{0,16},{4,20},{8,24},{12,28},{16,0},{20,4},{24,8},{28,12},{1,17},{... | collective-permute-start | bytes 491528 | tf_op jit(solution)/shard_map/ppermute | solution.py:70
  116.2 14.7 %collective-permute-start.26 = (bf16[128,640]{1,0:T(8,128)(2,1)S(1)}, bf16[128,640]{1,0:T(8,128)(2,1)S(1)}, u32[]{:S(2)}, u32[]{:S(2)}) collective-permute-start(bf16[128,640]{1,0:T(8,128)(2,1)S(1)} %get-tuple-element.69), channel_id=1, source_target_pairs={{0,20},{4,16},{8,28},{12,24},{16,4},{20,0},{24,12},{28,8},{1,21},{... | collective-permute-start | bytes 491528 | tf_op jit(solution)/shard_map/ppermute | solution.py:70
  117.6 13.4 %collective-permute-start.27 = (bf16[128,640]{1,0:T(8,128)(2,1)S(1)}, bf16[128,640]{1,0:T(8,128)(2,1)S(1)}, u32[]{:S(2)}, u32[]{:S(2)}) collective-permute-start(bf16[128,640]{1,0:T(8,128)(2,1)S(1)} %get-tuple-element.70), channel_id=1, source_target_pairs={{0,24},{4,28},{8,16},{12,20},{16,8},{20,12},{24,0},{28,4},{1,25},{... | collective-permute-start | bytes 491528 | tf_op jit(solution)/shard_map/ppermute | solution.py:70
  119.7 11.2 %collective-permute-start.28 = (bf16[128,640]{1,0:T(8,128)(2,1)S(1)}, bf16[128,640]{1,0:T(8,128)(2,1)S(1)}, u32[]{:S(2)}, u32[]{:S(2)}) collective-permute-start(bf16[128,640]{1,0:T(8,128)(2,1)S(1)} %get-tuple-element.71), channel_id=1, source_target_pairs={{0,28},{4,24},{8,20},{12,16},{16,12},{20,8},{24,4},{28,0},{1,29},{... | collective-permute-start | bytes 491528 | tf_op jit(solution)/shard_map/ppermute | solution.py:70
  132.2 6.0 %collective-permute-start.31 = (f32[1,256]{1,0:T(1,128)S(1)}, f32[1,256]{1,0:T(1,128)S(1)}, u32[]{:S(2)}, u32[]{:S(2)}) collective-permute-start(f32[1,256]{1,0:T(1,128)S(1)} %get-tuple-element.76.refs_0_), channel_id=1, source_target_pairs={{0,3},{1,2},{2,1},{3,0},{4,7},{5,6},{6,5},{7,4},{8,11},{9,10},{10,... | collective-permute-start | bytes 3080 | tf_op jit(solution)/shard_map/ppermute | solution.py:63
  134.5 4.5 %collective-permute-start.30 = (f32[1,256]{1,0:T(1,128)S(1)}, f32[1,256]{1,0:T(1,128)S(1)}, u32[]{:S(2)}, u32[]{:S(2)}) collective-permute-start(f32[1,256]{1,0:T(1,128)S(1)} %get-tuple-element.76.refs_0_), channel_id=1, source_target_pairs={{0,2},{1,3},{2,0},{3,1},{4,6},{5,7},{6,4},{7,5},{8,10},{9,11},{10,... | collective-permute-start | bytes 3080 | tf_op jit(solution)/shard_map/ppermute | solution.py:63
  (13 other events, 68.5 us)

commit v5 on v4

--- a/solution.py
+++ b/solution.py
@@ -172,46 +172,51 @@
     )
 
 
-def late_kernel(step, plan_ref, weight_ref, *refs):
-    part_refs, refs = refs[:HALVES], refs[HALVES:]
-    acc_ref, _, state_ref, grad_ref, val_ref, turned_ref, sum_ref = refs
-    key_count, tok_count, width = state_ref.shape
-    part = jnp.concatenate([ref[...] for ref in part_refs], axis=0)
+def late_kernel(h, step, plan_ref, weight_ref, part_ref, acc_ref, _, state_ref, grad_ref, *refs):
+    val_ref, turned_ref, sum_ref = refs[h > 0 :]
+    half, width = part_ref.shape
+    key_count = state_ref.shape[0]
+    rows = slice(h * half, (h + 1) * half)
+    part = part_ref[...]
     row_sum = lambda x: jnp.sum(x, axis=1, keepdims=True)
     sums = [None] * (4 * key_count)
     for j in range(key_count + 1):
-        val = acc_ref[j] + partial_products([part], weight_ref, step, j)
+        val = acc_ref[j, rows] + partial_products([part], weight_ref, step, j)
         if j == key_count:
             for k in range(key_count):
-                sums[3 * key_count + k] = row_sum(grad_ref[k].astype(F32) * val)
+                sums[3 * key_count + k] = row_sum(grad_ref[k, rows].astype(F32) * val)
             continue
-        val_ref[j] = val
-        state = state_ref[j].astype(F32)
+        val_ref[j, rows] = val
+        state = state_ref[j, rows].astype(F32)
         sums[j] = row_sum(state * state)
         sums[key_count + j] = row_sum(val * val)
         sums[2 * key_count + j] = row_sum(state * val)
-    lane = lax.broadcasted_iota(jnp.int32, (tok_count, 128), 1)
-    table = jnp.zeros((tok_count, 128), F32)
+    lane = lax.broadcasted_iota(jnp.int32, (half, 128), 1)
+    table = jnp.zeros((half, 128), F32)
     for i, s in enumerate(sums):
         table = jnp.where(lane == i, s, table)
-    sum_ref[...] = table.T[: 4 * key_count]
-    turned_ref[pl.ds(pl.multiple_of(plan_ref[step] * width, width), width), :] = part.T
-
-
-def forward_late(plan, weights, parts, acc, turned, states, grads):
-    key_count, tok_count, width = states.shape
-    return call(
-        functools.partial(late_kernel, weights.shape[-2] // width - 1),
+    if h:
+        sum_ref[:, : h * half] = refs[0][...]
+    sum_ref[:, rows] = table.T[: 4 * key_count]
+    place = pl.multiple_of(plan_ref[step] * width, width)
+    turned_ref[pl.ds(place, width), rows] = part.T
+
+
+def forward_late(h, plan, weights, part, acc, turned, states, grads, before):
+    key_count, _, width = states.shape
+    half = part.shape[0]
+    return call(
+        functools.partial(late_kernel, h, weights.shape[-2] // width - 1),
         "forward_late",
-        [SMEM] + [VMEM] * (5 + HALVES),
+        [SMEM] + [VMEM] * (6 + len(before)),
         [
             jax.ShapeDtypeStruct(acc.shape, F32),
             jax.ShapeDtypeStruct(turned.shape, BF16),
-            jax.ShapeDtypeStruct((4 * key_count, tok_count), F32),
+            jax.ShapeDtypeStruct((4 * key_count, (h + 1) * half), F32),
         ],
-        [plan, weights, *parts, acc, turned, states, grads],
-        macs=tok_count * width * width * (key_count + 1),
-        aliases={2 + HALVES: 0, 3 + HALVES: 1},
+        [plan, weights, part, acc, turned, states, grads, *before],
+        macs=half * width * width * (key_count + 1),
+        aliases={3: 0, 4: 1},
     )
 
 
@@ -614,9 +619,13 @@
                 chain[-1] = after(chain[-1], weights)
             chain.append(ring_pass(chain[-1], "tensor"))
     acc, turned = forward_early(plan, weights, [chain[:-1] for chain in chains], key_count)
-    vals, turned, sums = forward_late(
-        plan, weights, [chain[-1] for chain in chains], acc, turned, states, grads
-    )
+    sums = []
+    for h, chain in enumerate(chains):
+        acc, turned, here = forward_late(
+            h, plan, weights, chain[-1], acc, turned, states, grads, sums
+        )
+        sums = [here]
+    vals, sums = acc, sums[0]
     other_turned = swap_over("group", 1, turned)
     sums = [sums] + others_over("tensor", sums)
 

time: 141 us -> 140 us (level)
  blocking collectives: 0 us -> 8.18 us
  waiting for transfers between devices: 40.4 us -> 33.8 us
  starting transfers between devices: 54 us -> 50.9 us
    all_to_all x0 -> x1, blocking collectives: none -> 8.18 us  [on_device(): lax.all_to_all(slot_row, 'group', split_axis=0, concat_axis=0, tiled=True)]
    all_to_all x1 -> x0, waiting for transfers between devices: 4.58 us -> none  [on_device(): lax.all_to_all(slot_row, 'group', split_axis=0, concat_axis=0, tiled=True)]
    all_to_all x1 -> x0, starting transfers between devices: 3.72 us -> none  [on_device(): lax.all_to_all(slot_row, 'group', split_axis=0, concat_axis=0, tiled=True)]
    ppermute x11, waiting for transfers between devices: 20.9 us -> 18.2 us  [ring_pass(): lax.ppermute(part, axis, [(order[i], order[(i + 1) % size]) for i in rang...]
    pallas_call x26 -> x27, Pallas kernels: 33.5 us -> 33.9 us  [call(): pl.pallas_call(body, in_specs=in_specs + [ANY] * len(after), out_specs=[V...]
  transfers between devices with their start and end apart: 33 -> 32, of which waited for: 16 -> 15; matrix products, arithmetic and copies ran while one was open for 1% -> 1% of each run, Pallas kernels for 21% -> 22%
where the time goes in v5:
time: 140 us; the launch traced here: 139 us
  starting transfers between devices  50.9 us (36%)
  Pallas kernels  36.6 us (26%)
  waiting for transfers between devices  33.8 us (24%)
  blocking collectives  8.18 us (6%)
  local copies, waits for them, and re-layouts  8.1 us (6%)
    pallas_call x27, Pallas kernels, call(): pl.pallas_call(body, in_specs=in_specs + [ANY] * len(after), out_specs=[V...  33.9 us
    ppermute x11, starting transfers between devices, ring_pass(): lax.ppermute(part, axis, [(order[i], order[(i + 1) % size]) for i in rang...  27.8 us
    ppermute x11, waiting for transfers between devices, ring_pass(): lax.ppermute(part, axis, [(order[i], order[(i + 1) % size]) for i in rang...  18.2 us
    ppermute x15, starting transfers between devices, swap_over(): return lax.ppermute(part, axis, [(i, i ^ bit) for i in range(size)])  14.1 us
    ppermute x15, waiting for transfers between devices, swap_over(): return lax.ppermute(part, axis, [(i, i ^ bit) for i in range(size)])  10.6 us
    ppermute x6, starting transfers between devices, others_over(): lax.ppermute(part, axis, [(i, i ^ step) for i in range(size)])  8.91 us
    all_to_all x1, blocking collectives, on_device(): lax.all_to_all(slot_row, 'group', split_axis=0, concat_axis=0, tiled=True)  8.18 us
    unnamed x25, local copies, waits for them, and re-layouts  7.08 us
  transfers between devices with their start and end apart: 32, of which 15 were waited for; matrix products, arithmetic and copies ran while one was open for 1% of the time, Pallas kernels for 22%

profile of v5, /device:TPU:0, one launch (start us, length us, event | category | flops | bytes accessed | tf_op | source)
XLA Modules:
  0.0 139.2 jit_solution(9637285911007928781)
XLA Ops:
  2.2 4.1 %collective-permute-start.3 = (bf16[256,640]{1,0:T(8,128)(2,1)S(1)}, bf16[256,640]{1,0:T(8,128)(2,1)}, u32[]{:S(2)}, u32[]{:S(2)}) collective-permute-start(bf16[256,640]{1,0:T(8,128)(2,1)S(1)} %sum_rows.2.refs_1_.refs_2_), channel_id=1, source_target_pairs={{0,2},{2,3},{3,1},{1,0},{4,6},{6,7},{7,5},{5,4},{8,10},{10,11},{11... | collective-permute-start | bytes 983048 | tf_op jit(solution)/shard_map/ppermute | solution.py:57
  6.4 1.6 %collective-permute-start = (bf16[256,640]{1,0:T(8,128)(2,1)S(1)}, bf16[256,640]{1,0:T(8,128)(2,1)}, u32[]{:S(2)}, u32[]{:S(2)}) collective-permute-start(bf16[256,640]{1,0:T(8,128)(2,1)S(1)} %sum_rows.3.refs_1_.refs_5_), channel_id=1, source_target_pairs={{0,2},{2,3},{3,1},{1,0},{4,6},{6,7},{7,5},{5,4},{8,10},{10,11},{11... | collective-permute-start | bytes 983048 | tf_op jit(solution)/shard_map/ppermute | solution.py:57
  9.3 8.2 %all_to_all.9 = s32[8,1,128]{2,1,0:T(1,128)S(1)} all-to-all(s32[8,1,128]{2,1,0:T(1,128)S(1)} %bitcast.27), channel_id=1, replica_groups=mesh['group'=8,'tensor'=4] {'group'}, dimensions={0} | all-to-all | bytes 8192 | tf_op jit(solution)/shard_map/all_to_all | solution.py:610
  17.9 3.5 %collective-permute-done.refs_6_ = bf16[256,640]{1,0:T(8,128)(2,1)} collective-permute-done((bf16[256,640]{1,0:T(8,128)(2,1)S(1)}, bf16[256,640]{1,0:T(8,128)(2,1)}, u32[]{:S(2)}, u32[]{:S(2)}) %collective-permute-start) | collective-permute-done | bytes 327712 | tf_op jit(solution)/shard_map/ppermute | solution.py:57
  21.4 3.5 %collective-permute-start.1 = (bf16[256,640]{1,0:T(8,128)(2,1)}, bf16[256,640]{1,0:T(8,128)(2,1)S(1)}, u32[]{:S(2)}, u32[]{:S(2)}) collective-permute-start(bf16[256,640]{1,0:T(8,128)(2,1)} %collective-permute-done.refs_6_), channel_id=1, source_target_pairs={{0,2},{2,3},{3,1},{1,0},{4,6},{6,7},{7,5},{5,4},{8,10},{10,11},{11... | collective-permute-start | bytes 983048 | tf_op jit(solution)/shard_map/ppermute | solution.py:57
  25.6 3.0 %collective-permute-done.4.refs_4_ = bf16[256,640]{1,0:T(8,128)(2,1)} collective-permute-done((bf16[256,640]{1,0:T(8,128)(2,1)}, bf16[256,640]{1,0:T(8,128)(2,1)}, u32[]{:S(2)}, u32[]{:S(2)}) %collective-permute-start.4) | collective-permute-done | bytes 327712 | tf_op jit(solution)/shard_map/ppermute | solution.py:57
  28.6 3.4 %collective-permute-start.5 = (bf16[256,640]{1,0:T(8,128)(2,1)}, bf16[256,640]{1,0:T(8,128)(2,1)S(1)}, u32[]{:S(2)}, u32[]{:S(2)}) collective-permute-start(bf16[256,640]{1,0:T(8,128)(2,1)} %collective-permute-done.4.refs_4_), channel_id=1, source_target_pairs={{0,2},{2,3},{3,1},{1,0},{4,6},{6,7},{7,5},{5,4},{8,10},{10,11},{11... | collective-permute-start | bytes 983048 | tf_op jit(solution)/shard_map/ppermute | solution.py:57
  32.0 2.9 %copy-done = bf16[2,2560,640]{2,1,0:T(8,128)(2,1)S(1)} copy-done((bf16[2,2560,640]{2,1,0:T(8,128)(2,1)S(1)}, bf16[2,2560,640]{2,1,0:T(8,128)(2,1)}, u32[]{:S(2)}) %copy-start) | copy-done | bytes 6553624
  34.9 1.9 %copy-done.3 = bf16[2560,640]{1,0:T(8,128)(2,1)S(1)} copy-done((bf16[2560,640]{1,0:T(8,128)(2,1)S(1)}, bf16[2560,640]{1,0:T(8,128)(2,1)}, u32[]{:S(2)}) %copy-start.3) | copy-done | bytes 3276824
  39.1 6.2 %forward_early.1 = (f32[3,512,640]{2,1,0:T(8,128)S(1)}, bf16[2560,512]{1,0:T(8,128)(2,1)S(1)}) custom-call(s32[12]{0:T(128)S(1)} %pad_add_fusion.refs_0_, bf16[2560,1920]{1,0:T(8,128)(2,1)S(1)} %join_weights.1.refs_1_, bf16[256,640]{1,0:T(8,128)(2,1)S(1)} %sum_rows.2.refs_1_.refs_2_, bf16[256,640]{1,0:T(8,128)(2,1)} %after.3.refs_3_, ...), custom_call_target="tpu_custom_call" | custom-call | flops 188743680 | tf_op jit(solution)/shard_map/forward_early/pallas_call | solution.py:37
  45.3 2.1 %forward_late.2 = (f32[3,512,640]{2,1,0:T(8,128)S(1)}, bf16[2560,512]{1,0:T(8,128)(2,1)S(1)}, f32[8,256]{1,0:T(8,128)S(1)}) custom-call(s32[12]{0:T(128)S(1)} %pad_add_fusion.refs_0_, bf16[2560,1920]{1,0:T(8,128)(2,1)S(1)} %join_weights.1.refs_1_, bf16[256,640]{1,0:T(8,128)(2,1)S(1)} %collective-permute-done.5.refs_2_, ...), custom_call_target="tpu_custom_call", output_to_operand_aliasing={{0}: (3, {}), {1}: (4, {})} | custom-call | flops 31457280 | tf_op jit(solution)/shard_map/forward_late/pallas_call | solution.py:37
  48.4 2.1 %forward_late.3 = (f32[3,512,640]{2,1,0:T(8,128)S(1)}, bf16[2560,512]{1,0:T(8,128)(2,1)S(1)}, f32[8,512]{1,0:T(8,128)S(1)}) custom-call(s32[12]{0:T(128)S(1)} %pad_add_fusion.refs_0_, bf16[2560,1920]{1,0:T(8,128)(2,1)S(1)} %join_weights.1.refs_1_, bf16[256,640]{1,0:T(8,128)(2,1)S(1)} %collective-permute-done.2.refs_2_, ...), custom_call_target="tpu_custom_call", output_to_operand_aliasing={{0}: (3, {}), {1}: (4, {})} | custom-call | flops 31457280 | tf_op jit(solution)/shard_map/forward_late/pallas_call | solution.py:37
  50.6 3.6 %collective-permute-start.8 = (f32[8,512]{1,0:T(8,128)S(1)}, f32[8,512]{1,0:T(8,128)S(1)}, u32[]{:S(2)}, u32[]{:S(2)}) collective-permute-start(f32[8,512]{1,0:T(8,128)S(1)} %get-tuple-element.52.refs_0_), channel_id=1, source_target_pairs={{0,3},{1,2},{2,1},{3,0},{4,7},{5,6},{6,5},{7,4},{8,11},{9,10},{10,... | collective-permute-start | bytes 49160 | tf_op jit(solution)/shard_map/ppermute | solution.py:63
  56.2 2.6 %collective-permute-done.7.refs_2_ = f32[8,512]{1,0:T(8,128)S(1)} collective-permute-done((f32[8,512]{1,0:T(8,128)S(1)}, f32[8,512]{1,0:T(8,128)S(1)}, u32[]{:S(2)}, u32[]{:S(2)}) %collective-permute-start.7) | collective-permute-done | bytes 16416 | tf_op jit(solution)/shard_map/ppermute | solution.py:63
  60.2 1.8 %back.4.refs_5_ = bf16[512,640]{1,0:T(8,128)(2,1)S(1)} custom-call(bf16[512,1920]{1,0:T(8,128)(2,1)S(1)} %cotangents.1.refs_0_.refs_1_, bf16[2560,1920]{1,0:T(8,128)(2,1)S(1)} %join_weights.1.refs_1_), custom_call_target="tpu_custom_call" | custom-call | flops 62914560 | tf_op jit(solution)/shard_map/back/pallas_call | solution.py:37
  62.0 2.2 %collective-permute-start.13 = (bf16[512,640]{1,0:T(8,128)(2,1)S(1)}, bf16[512,640]{1,0:T(8,128)(2,1)S(1)}, u32[]{:S(2)}, u32[]{:S(2)}) collective-permute-start(bf16[512,640]{1,0:T(8,128)(2,1)S(1)} %back.4.refs_5_), channel_id=1, source_target_pairs={{0,2},{2,3},{3,1},{1,0},{4,6},{6,7},{7,5},{5,4},{8,10},{10,11},{11... | collective-permute-start | bytes 1966088 | tf_op jit(solution)/shard_map/ppermute | solution.py:57
  64.2 2.1 %outer.4 = (bf16[160,1920]{1,0:T(8,128)(2,1)S(1)}, bf16[160,1920]{1,0:T(8,128)(2,1)S(1)}) custom-call(s32[12]{0:T(128)S(1)} %pad_add_fusion.refs_0_, bf16[512,1920]{1,0:T(8,128)(2,1)S(1)} %cotangents.1.refs_0_.refs_1_, bf16[512,1920]{1,0:T(8,128)(2,1)S(1)} %collective-permute-done.10.refs_2_, bf16[2560,512]{1,0:T(8,128)(2,1)S(1)} %get-tuple-element.54.refs_3_, ...), custom_call_target="tpu_custom_call" | custom-call | flops 62914560 | tf_op jit(solution)/shard_map/outer/pallas_call | solution.py:37
  69.4 2.1 %outer.5 = (bf16[160,1920]{1,0:T(8,128)(2,1)S(1)}, bf16[160,1920]{1,0:T(8,128)(2,1)S(1)}) custom-call(s32[12]{0:T(128)S(1)} %pad_add_fusion.refs_0_, bf16[512,1920]{1,0:T(8,128)(2,1)S(1)} %cotangents.1.refs_0_.refs_1_, bf16[512,1920]{1,0:T(8,128)(2,1)S(1)} %collective-permute-done.10.refs_2_, bf16[2560,512]{1,0:T(8,128)(2,1)S(1)} %get-tuple-element.54.refs_3_, ...), custom_call_target="tpu_custom_call" | custom-call | flops 62914560 | tf_op jit(solution)/shard_map/outer/pallas_call | solution.py:37
  72.1 2.1 %outer.6 = (bf16[160,1920]{1,0:T(8,128)(2,1)S(1)}, bf16[160,1920]{1,0:T(8,128)(2,1)S(1)}) custom-call(s32[12]{0:T(128)S(1)} %pad_add_fusion.refs_0_, bf16[512,1920]{1,0:T(8,128)(2,1)S(1)} %cotangents.1.refs_0_.refs_1_, bf16[512,1920]{1,0:T(8,128)(2,1)S(1)} %collective-permute-done.10.refs_2_, bf16[2560,512]{1,0:T(8,128)(2,1)S(1)} %get-tuple-element.54.refs_3_, ...), custom_call_target="tpu_custom_call" | custom-call | flops 62914560 | tf_op jit(solution)/shard_map/outer/pallas_call | solution.py:37
  74.1 1.8 %back.5 = (bf16[512,384]{1,0:T(8,128)(2,1)S(1)}, bf16[512,256]{1,0:T(8,128)(2,1)S(1)}) custom-call(bf16[512,1920]{1,0:T(8,128)(2,1)S(1)} %cotangents.1.refs_0_.refs_1_, bf16[2560,1920]{1,0:T(8,128)(2,1)S(1)} %join_weights.1.refs_1_, bf16[160,1920]{1,0:T(8,128)(2,1)S(1)} %get-tuple-element.57.refs_2_.refs_0_), custom_call_target="tpu_custom_call" | custom-call | flops 62914560 | tf_op jit(solution)/shard_map/back/pallas_call | solution.py:37
  76.0 3.4 %collective-permute-done.13.refs_0_ = bf16[512,640]{1,0:T(8,128)(2,1)S(1)} collective-permute-done((bf16[512,640]{1,0:T(8,128)(2,1)S(1)}, bf16[512,640]{1,0:T(8,128)(2,1)S(1)}, u32[]{:S(2)}, u32[]{:S(2)}) %collective-permute-start.13) | collective-permute-done | bytes 655392 | tf_op jit(solution)/shard_map/ppermute | solution.py:57
  79.5 2.9 %collective-permute-start.15 = (bf16[512,384]{1,0:T(8,128)(2,1)S(1)}, bf16[512,384]{1,0:T(8,128)(2,1)S(1)}, u32[]{:S(2)}, u32[]{:S(2)}) collective-permute-start(bf16[512,384]{1,0:T(8,128)(2,1)S(1)} %add_part.4.refs_2_), channel_id=1, source_target_pairs={{0,2},{2,3},{3,1},{1,0},{4,6},{6,7},{7,5},{5,4},{8,10},{10,11},{11... | collective-permute-start | bytes 1179656 | tf_op jit(solution)/shard_map/ppermute | solution.py:57
  85.3 1.9 %collective-permute-start.18 = (bf16[512,256]{1,0:T(8,128)(2,1)S(1)}, bf16[512,256]{1,0:T(8,128)(2,1)S(1)}, u32[]{:S(2)}, u32[]{:S(2)}) collective-permute-start(bf16[512,256]{1,0:T(8,128)(2,1)S(1)} %add_part.5.refs_2_), channel_id=1, source_target_pairs={{0,2},{2,3},{3,1},{1,0},{4,6},{6,7},{7,5},{5,4},{8,10},{10,11},{11... | collective-permute-start | bytes 786440 | tf_op jit(solution)/shard_map/ppermute | solution.py:57
  87.3 2.1 %outer.7 = (bf16[160,1920]{1,0:T(8,128)(2,1)S(1)}, bf16[160,1920]{1,0:T(8,128)(2,1)S(1)}) custom-call(s32[12]{0:T(128)S(1)} %pad_add_fusion.refs_0_, bf16[512,1920]{1,0:T(8,128)(2,1)S(1)} %cotangents.1.refs_0_.refs_1_, bf16[512,1920]{1,0:T(8,128)(2,1)S(1)} %collective-permute-done.10.refs_2_, bf16[2560,512]{1,0:T(8,128)(2,1)S(1)} %get-tuple-element.54.refs_3_, ...), custom_call_target="tpu_custom_call" | custom-call | flops 62914560 | tf_op jit(solution)/shard_map/outer/pallas_call | solution.py:37
  89.3 1.8 %back.6 = (bf16[512,384]{1,0:T(8,128)(2,1)S(1)}, bf16[512,256]{1,0:T(8,128)(2,1)S(1)}) custom-call(bf16[512,1920]{1,0:T(8,128)(2,1)S(1)} %cotangents.1.refs_0_.refs_1_, bf16[2560,1920]{1,0:T(8,128)(2,1)S(1)} %join_weights.1.refs_1_, bf16[160,1920]{1,0:T(8,128)(2,1)S(1)} %get-tuple-element.62.refs_2_.refs_0_), custom_call_target="tpu_custom_call" | custom-call | flops 62914560 | tf_op jit(solution)/shard_map/back/pallas_call | solution.py:37
  92.1 3.4 %collective-permute-start.20 = (bf16[512,384]{1,0:T(8,128)(2,1)S(1)}, bf16[512,384]{1,0:T(8,128)(2,1)S(1)}, u32[]{:S(2)}, u32[]{:S(2)}) collective-permute-start(bf16[512,384]{1,0:T(8,128)(2,1)S(1)} %add_part.6.refs_2_), channel_id=1, source_target_pairs={{0,2},{2,3},{3,1},{1,0},{4,6},{6,7},{7,5},{5,4},{8,10},{10,11},{11... | collective-permute-start | bytes 1179656 | tf_op jit(solution)/shard_map/ppermute | solution.py:57
  95.5 1.8 %back.7 = (bf16[512,384]{1,0:T(8,128)(2,1)S(1)}, bf16[512,256]{1,0:T(8,128)(2,1)S(1)}) custom-call(bf16[512,1920]{1,0:T(8,128)(2,1)S(1)} %cotangents.1.refs_0_.refs_1_, bf16[2560,1920]{1,0:T(8,128)(2,1)S(1)} %join_weights.1.refs_1_, bf16[512,384]{1,0:T(8,128)(2,1)S(1)} %add_part.6.refs_2_), custom_call_target="tpu_custom_call" | custom-call | flops 62914560 | tf_op jit(solution)/shard_map/back/pallas_call | solution.py:37
  97.6 3.7 %collective-permute-start.21 = (bf16[512,256]{1,0:T(8,128)(2,1)S(1)}, bf16[512,256]{1,0:T(8,128)(2,1)S(1)}, u32[]{:S(2)}, u32[]{:S(2)}) collective-permute-start(bf16[512,256]{1,0:T(8,128)(2,1)S(1)} %add_part.7.refs_2_), channel_id=1, source_target_pairs={{0,2},{2,3},{3,1},{1,0},{4,6},{6,7},{7,5},{5,4},{8,10},{10,11},{11... | collective-permute-start | bytes 786440 | tf_op jit(solution)/shard_map/ppermute | solution.py:57
  103.9 6.5 %collective-permute-done.21.refs_2_ = bf16[512,256]{1,0:T(8,128)(2,1)S(1)} collective-permute-done((bf16[512,256]{1,0:T(8,128)(2,1)S(1)}, bf16[512,256]{1,0:T(8,128)(2,1)S(1)}, u32[]{:S(2)}, u32[]{:S(2)}) %collective-permute-start.21) | collective-permute-done | bytes 262176 | tf_op jit(solution)/shard_map/ppermute | solution.py:57
  116.4 1.8 %collective-permute-start.27 = (bf16[128,640]{1,0:T(8,128)(2,1)S(1)}, bf16[128,640]{1,0:T(8,128)(2,1)S(1)}, u32[]{:S(2)}, u32[]{:S(2)}) collective-permute-start(bf16[128,640]{1,0:T(8,128)(2,1)S(1)} %get-tuple-element.76), channel_id=1, source_target_pairs={{0,24},{4,28},{8,16},{12,20},{16,8},{20,12},{24,0},{28,4},{1,25},{... | collective-permute-start | bytes 491528 | tf_op jit(solution)/shard_map/ppermute | solution.py:70
  121.1 8.6 %collective-permute-done.26.refs_7_ = bf16[128,640]{1,0:T(8,128)(2,1)S(1)} collective-permute-done((bf16[128,640]{1,0:T(8,128)(2,1)S(1)}, bf16[128,640]{1,0:T(8,128)(2,1)S(1)}, u32[]{:S(2)}, u32[]{:S(2)}) %collective-permute-start.26) | collective-permute-done | bytes 163872 | tf_op jit(solution)/shard_map/ppermute | solution.py:70
  131.0 2.3 %collective-permute-start.31 = (f32[1,256]{1,0:T(1,128)S(1)}, f32[1,256]{1,0:T(1,128)S(1)}, u32[]{:S(2)}, u32[]{:S(2)}) collective-permute-start(f32[1,256]{1,0:T(1,128)S(1)} %get-tuple-element.82.refs_0_), channel_id=1, source_target_pairs={{0,3},{1,2},{2,1},{3,0},{4,7},{5,6},{6,5},{7,4},{8,11},{9,10},{10,... | collective-permute-start | bytes 3080 | tf_op jit(solution)/shard_map/ppermute | solution.py:63
  (97 shorter events, 37.3 us)
Async XLA Ops:
  2.2 15.3 %collective-permute-start.3 = (bf16[256,640]{1,0:T(8,128)(2,1)S(1)}, bf16[256,640]{1,0:T(8,128)(2,1)}, u32[]{:S(2)}, u32[]{:S(2)}) collective-permute-start(bf16[256,640]{1,0:T(8,128)(2,1)S(1)} %sum_rows.2.refs_1_.refs_2_), channel_id=1, source_target_pairs={{0,2},{2,3},{3,1},{1,0},{4,6},{6,7},{7,5},{5,4},{8,10},{10,11},{11... | collective-permute-start | bytes 983048 | tf_op jit(solution)/shard_map/ppermute | solution.py:57
  6.4 15.0 %collective-permute-start = (bf16[256,640]{1,0:T(8,128)(2,1)S(1)}, bf16[256,640]{1,0:T(8,128)(2,1)}, u32[]{:S(2)}, u32[]{:S(2)}) collective-permute-start(bf16[256,640]{1,0:T(8,128)(2,1)S(1)} %sum_rows.3.refs_1_.refs_5_), channel_id=1, source_target_pairs={{0,2},{2,3},{3,1},{1,0},{4,6},{6,7},{7,5},{5,4},{8,10},{10,11},{11... | collective-permute-start | bytes 983048 | tf_op jit(solution)/shard_map/ppermute | solution.py:57
  17.5 11.1 %collective-permute-start.4 = (bf16[256,640]{1,0:T(8,128)(2,1)}, bf16[256,640]{1,0:T(8,128)(2,1)}, u32[]{:S(2)}, u32[]{:S(2)}) collective-permute-start(bf16[256,640]{1,0:T(8,128)(2,1)} %after.3.refs_3_), channel_id=1, source_target_pairs={{0,2},{2,3},{3,1},{1,0},{4,6},{6,7},{7,5},{5,4},{8,10},{10,11},{11... | collective-permute-start | bytes 983048 | tf_op jit(solution)/shard_map/ppermute | solution.py:57
  21.4 16.9 %collective-permute-start.1 = (bf16[256,640]{1,0:T(8,128)(2,1)}, bf16[256,640]{1,0:T(8,128)(2,1)S(1)}, u32[]{:S(2)}, u32[]{:S(2)}) collective-permute-start(bf16[256,640]{1,0:T(8,128)(2,1)} %collective-permute-done.refs_6_), channel_id=1, source_target_pairs={{0,2},{2,3},{3,1},{1,0},{4,6},{6,7},{7,5},{5,4},{8,10},{10,11},{11... | collective-permute-start | bytes 983048 | tf_op jit(solution)/shard_map/ppermute | solution.py:57
  28.6 16.8 %collective-permute-start.5 = (bf16[256,640]{1,0:T(8,128)(2,1)}, bf16[256,640]{1,0:T(8,128)(2,1)S(1)}, u32[]{:S(2)}, u32[]{:S(2)}) collective-permute-start(bf16[256,640]{1,0:T(8,128)(2,1)} %collective-permute-done.4.refs_4_), channel_id=1, source_target_pairs={{0,2},{2,3},{3,1},{1,0},{4,6},{6,7},{7,5},{5,4},{8,10},{10,11},{11... | collective-permute-start | bytes 983048 | tf_op jit(solution)/shard_map/ppermute | solution.py:57
  38.4 10.0 %collective-permute-start.2 = (bf16[256,640]{1,0:T(8,128)(2,1)S(1)}, bf16[256,640]{1,0:T(8,128)(2,1)S(1)}, u32[]{:S(2)}, u32[]{:S(2)}) collective-permute-start(bf16[256,640]{1,0:T(8,128)(2,1)S(1)} %after.2.refs_7_), channel_id=1, source_target_pairs={{0,2},{2,3},{3,1},{1,0},{4,6},{6,7},{7,5},{5,4},{8,10},{10,11},{11... | collective-permute-start | bytes 983048 | tf_op jit(solution)/shard_map/ppermute | solution.py:57
  50.5 8.3 %collective-permute-start.9 = (bf16[2560,512]{1,0:T(8,128)(2,1)S(1)}, bf16[2560,512]{1,0:T(8,128)(2,1)S(1)}, u32[]{:S(2)}, u32[]{:S(2)}) collective-permute-start(bf16[2560,512]{1,0:T(8,128)(2,1)S(1)} %get-tuple-element.54.refs_3_), channel_id=1, source_target_pairs={{0,4},{4,0},{8,12},{12,8},{16,20},{20,16},{24,28},{28,24},{1,5},{5... | collective-permute-start | bytes 7864328 | tf_op jit(solution)/shard_map/ppermute | solution.py:70
  50.6 5.6 %collective-permute-start.8 = (f32[8,512]{1,0:T(8,128)S(1)}, f32[8,512]{1,0:T(8,128)S(1)}, u32[]{:S(2)}, u32[]{:S(2)}) collective-permute-start(f32[8,512]{1,0:T(8,128)S(1)} %get-tuple-element.52.refs_0_), channel_id=1, source_target_pairs={{0,3},{1,2},{2,1},{3,0},{4,7},{5,6},{6,5},{7,4},{8,11},{9,10},{10,... | collective-permute-start | bytes 49160 | tf_op jit(solution)/shard_map/ppermute | solution.py:63
  54.2 4.7 %collective-permute-start.7 = (f32[8,512]{1,0:T(8,128)S(1)}, f32[8,512]{1,0:T(8,128)S(1)}, u32[]{:S(2)}, u32[]{:S(2)}) collective-permute-start(f32[8,512]{1,0:T(8,128)S(1)} %get-tuple-element.52.refs_0_), channel_id=1, source_target_pairs={{0,2},{1,3},{2,0},{3,1},{4,6},{5,7},{6,4},{7,5},{8,10},{9,11},{10,... | collective-permute-start | bytes 49160 | tf_op jit(solution)/shard_map/ppermute | solution.py:63
  54.5 4.4 %collective-permute-start.6 = (f32[8,512]{1,0:T(8,128)S(1)}, f32[8,512]{1,0:T(8,128)S(1)}, u32[]{:S(2)}, u32[]{:S(2)}) collective-permute-start(f32[8,512]{1,0:T(8,128)S(1)} %get-tuple-element.52.refs_0_), channel_id=1, source_target_pairs={{0,1},{1,0},{2,3},{3,2},{4,5},{5,4},{6,7},{7,6},{8,9},{9,8},{10,11... | collective-permute-start | bytes 49160 | tf_op jit(solution)/shard_map/ppermute | solution.py:63
  60.1 4.1 %collective-permute-start.10 = (bf16[512,1920]{1,0:T(8,128)(2,1)S(1)}, bf16[512,1920]{1,0:T(8,128)(2,1)S(1)}, u32[]{:S(2)}, u32[]{:S(2)}) collective-permute-start(bf16[512,1920]{1,0:T(8,128)(2,1)S(1)} %cotangents.1.refs_0_.refs_1_), channel_id=1, source_target_pairs={{0,4},{4,0},{8,12},{12,8},{16,20},{20,16},{24,28},{28,24},{1,5},{5... | collective-permute-start | bytes 5898248 | tf_op jit(solution)/shard_map/ppermute | solution.py:70
  62.0 17.4 %collective-permute-start.13 = (bf16[512,640]{1,0:T(8,128)(2,1)S(1)}, bf16[512,640]{1,0:T(8,128)(2,1)S(1)}, u32[]{:S(2)}, u32[]{:S(2)}) collective-permute-start(bf16[512,640]{1,0:T(8,128)(2,1)S(1)} %back.4.refs_5_), channel_id=1, source_target_pairs={{0,2},{2,3},{3,1},{1,0},{4,6},{6,7},{7,5},{5,4},{8,10},{10,11},{11... | collective-permute-start | bytes 1966088 | tf_op jit(solution)/shard_map/ppermute | solution.py:57
  66.3 17.7 %collective-permute-start.12 = (bf16[160,1920]{1,0:T(8,128)(2,1)S(1)}, bf16[160,1920]{1,0:T(8,128)(2,1)S(1)}, u32[]{:S(2)}, u32[]{:S(2)}) collective-permute-start(bf16[160,1920]{1,0:T(8,128)(2,1)S(1)} %get-tuple-element.59), channel_id=1, source_target_pairs={{0,16},{4,20},{8,24},{12,28},{16,0},{20,4},{24,8},{28,12},{1,17},{... | collective-permute-start | bytes 1843208 | tf_op jit(solution)/shard_map/ppermute | solution.py:70
  67.9 16.7 %collective-permute-start.11 = (bf16[160,1920]{1,0:T(8,128)(2,1)S(1)}, bf16[160,1920]{1,0:T(8,128)(2,1)S(1)}, u32[]{:S(2)}, u32[]{:S(2)}) collective-permute-start(bf16[160,1920]{1,0:T(8,128)(2,1)S(1)} %get-tuple-element.55.refs_5_), channel_id=1, source_target_pairs={{0,8},{4,12},{8,0},{12,4},{16,24},{20,28},{24,16},{28,20},{1,9},{5... | collective-permute-start | bytes 1843208 | tf_op jit(solution)/shard_map/ppermute | solution.py:70
  71.5 25.8 %collective-permute-start.14 = (bf16[160,1920]{1,0:T(8,128)(2,1)S(1)}, bf16[160,1920]{1,0:T(8,128)(2,1)S(1)}, u32[]{:S(2)}, u32[]{:S(2)}) collective-permute-start(bf16[160,1920]{1,0:T(8,128)(2,1)S(1)} %get-tuple-element.56.refs_5_), channel_id=1, source_target_pairs={{0,8},{4,12},{8,0},{12,4},{16,24},{20,28},{24,16},{28,20},{1,9},{5... | collective-permute-start | bytes 1843208 | tf_op jit(solution)/shard_map/ppermute | solution.py:70
  79.5 12.4 %collective-permute-start.15 = (bf16[512,384]{1,0:T(8,128)(2,1)S(1)}, bf16[512,384]{1,0:T(8,128)(2,1)S(1)}, u32[]{:S(2)}, u32[]{:S(2)}) collective-permute-start(bf16[512,384]{1,0:T(8,128)(2,1)S(1)} %add_part.4.refs_2_), channel_id=1, source_target_pairs={{0,2},{2,3},{3,1},{1,0},{4,6},{6,7},{7,5},{5,4},{8,10},{10,11},{11... | collective-permute-start | bytes 1179656 | tf_op jit(solution)/shard_map/ppermute | solution.py:57
  82.4 20.4 %collective-permute-start.17 = (bf16[160,1920]{1,0:T(8,128)(2,1)S(1)}, bf16[160,1920]{1,0:T(8,128)(2,1)S(1)}, u32[]{:S(2)}, u32[]{:S(2)}) collective-permute-start(bf16[160,1920]{1,0:T(8,128)(2,1)S(1)} %get-tuple-element.66), channel_id=1, source_target_pairs={{0,16},{4,20},{8,24},{12,28},{16,0},{20,4},{24,8},{28,12},{1,17},{... | collective-permute-start | bytes 1843208 | tf_op jit(solution)/shard_map/ppermute | solution.py:70
  84.8 28.5 %collective-permute-start.16 = (bf16[160,1920]{1,0:T(8,128)(2,1)S(1)}, bf16[160,1920]{1,0:T(8,128)(2,1)S(1)}, u32[]{:S(2)}, u32[]{:S(2)}) collective-permute-start(bf16[160,1920]{1,0:T(8,128)(2,1)S(1)} %add.32.refs_5_), channel_id=1, source_target_pairs={{0,16},{4,20},{8,24},{12,28},{16,0},{20,4},{24,8},{28,12},{1,17},{... | collective-permute-start | bytes 1843208 | tf_op jit(solution)/shard_map/ppermute | solution.py:70
  85.3 12.2 %collective-permute-start.18 = (bf16[512,256]{1,0:T(8,128)(2,1)S(1)}, bf16[512,256]{1,0:T(8,128)(2,1)S(1)}, u32[]{:S(2)}, u32[]{:S(2)}) collective-permute-start(bf16[512,256]{1,0:T(8,128)(2,1)S(1)} %add_part.5.refs_2_), channel_id=1, source_target_pairs={{0,2},{2,3},{3,1},{1,0},{4,6},{6,7},{7,5},{5,4},{8,10},{10,11},{11... | collective-permute-start | bytes 786440 | tf_op jit(solution)/shard_map/ppermute | solution.py:57
  92.1 18.3 %collective-permute-start.20 = (bf16[512,384]{1,0:T(8,128)(2,1)S(1)}, bf16[512,384]{1,0:T(8,128)(2,1)S(1)}, u32[]{:S(2)}, u32[]{:S(2)}) collective-permute-start(bf16[512,384]{1,0:T(8,128)(2,1)S(1)} %add_part.6.refs_2_), channel_id=1, source_target_pairs={{0,2},{2,3},{3,1},{1,0},{4,6},{6,7},{7,5},{5,4},{8,10},{10,11},{11... | collective-permute-start | bytes 1179656 | tf_op jit(solution)/shard_map/ppermute | solution.py:57
  97.6 12.7 %collective-permute-start.21 = (bf16[512,256]{1,0:T(8,128)(2,1)S(1)}, bf16[512,256]{1,0:T(8,128)(2,1)S(1)}, u32[]{:S(2)}, u32[]{:S(2)}) collective-permute-start(bf16[512,256]{1,0:T(8,128)(2,1)S(1)} %add_part.7.refs_2_), channel_id=1, source_target_pairs={{0,2},{2,3},{3,1},{1,0},{4,6},{6,7},{7,5},{5,4},{8,10},{10,11},{11... | collective-permute-start | bytes 786440 | tf_op jit(solution)/shard_map/ppermute | solution.py:57
  101.3 13.7 %collective-permute-start.19 = (bf16[160,1920]{1,0:T(8,128)(2,1)S(1)}, bf16[160,1920]{1,0:T(8,128)(2,1)S(1)}, u32[]{:S(2)}, u32[]{:S(2)}) collective-permute-start(bf16[160,1920]{1,0:T(8,128)(2,1)S(1)} %add.31.refs_2_), channel_id=1, source_target_pairs={{0,8},{4,12},{8,0},{12,4},{16,24},{20,28},{24,16},{28,20},{1,9},{5... | collective-permute-start | bytes 1843208 | tf_op jit(solution)/shard_map/ppermute | solution.py:70
  111.4 5.0 %collective-permute-start.22 = (bf16[128,640]{1,0:T(8,128)(2,1)S(1)}, bf16[128,640]{1,0:T(8,128)(2,1)S(1)}, u32[]{:S(2)}, u32[]{:S(2)}) collective-permute-start(bf16[128,640]{1,0:T(8,128)(2,1)S(1)} %get-tuple-element.71), channel_id=1, source_target_pairs={{0,4},{4,0},{8,12},{12,8},{16,20},{20,16},{24,28},{28,24},{1,5},{5... | collective-permute-start | bytes 491528 | tf_op jit(solution)/shard_map/ppermute | solution.py:70
  111.4 7.1 %collective-permute-start.23 = (bf16[128,640]{1,0:T(8,128)(2,1)S(1)}, bf16[128,640]{1,0:T(8,128)(2,1)S(1)}, u32[]{:S(2)}, u32[]{:S(2)}) collective-permute-start(bf16[128,640]{1,0:T(8,128)(2,1)S(1)} %get-tuple-element.72), channel_id=1, source_target_pairs={{0,8},{4,12},{8,0},{12,4},{16,24},{20,28},{24,16},{28,20},{1,9},{5... | collective-permute-start | bytes 491528 | tf_op jit(solution)/shard_map/ppermute | solution.py:70
  113.0 8.1 %collective-permute-start.24 = (bf16[128,640]{1,0:T(8,128)(2,1)S(1)}, bf16[128,640]{1,0:T(8,128)(2,1)S(1)}, u32[]{:S(2)}, u32[]{:S(2)}) collective-permute-start(bf16[128,640]{1,0:T(8,128)(2,1)S(1)} %get-tuple-element.73), channel_id=1, source_target_pairs={{0,12},{4,8},{8,4},{12,0},{16,28},{20,24},{24,20},{28,16},{1,13},{... | collective-permute-start | bytes 491528 | tf_op jit(solution)/shard_map/ppermute | solution.py:70
  113.3 7.8 %collective-permute-start.25 = (bf16[128,640]{1,0:T(8,128)(2,1)S(1)}, bf16[128,640]{1,0:T(8,128)(2,1)S(1)}, u32[]{:S(2)}, u32[]{:S(2)}) collective-permute-start(bf16[128,640]{1,0:T(8,128)(2,1)S(1)} %get-tuple-element.74), channel_id=1, source_target_pairs={{0,16},{4,20},{8,24},{12,28},{16,0},{20,4},{24,8},{28,12},{1,17},{... | collective-permute-start | bytes 491528 | tf_op jit(solution)/shard_map/ppermute | solution.py:70
  115.0 14.7 %collective-permute-start.26 = (bf16[128,640]{1,0:T(8,128)(2,1)S(1)}, bf16[128,640]{1,0:T(8,128)(2,1)S(1)}, u32[]{:S(2)}, u32[]{:S(2)}) collective-permute-start(bf16[128,640]{1,0:T(8,128)(2,1)S(1)} %get-tuple-element.75), channel_id=1, source_target_pairs={{0,20},{4,16},{8,28},{12,24},{16,4},{20,0},{24,12},{28,8},{1,21},{... | collective-permute-start | bytes 491528 | tf_op jit(solution)/shard_map/ppermute | solution.py:70
  116.4 13.4 %collective-permute-start.27 = (bf16[128,640]{1,0:T(8,128)(2,1)S(1)}, bf16[128,640]{1,0:T(8,128)(2,1)S(1)}, u32[]{:S(2)}, u32[]{:S(2)}) collective-permute-start(bf16[128,640]{1,0:T(8,128)(2,1)S(1)} %get-tuple-element.76), channel_id=1, source_target_pairs={{0,24},{4,28},{8,16},{12,20},{16,8},{20,12},{24,0},{28,4},{1,25},{... | collective-permute-start | bytes 491528 | tf_op jit(solution)/shard_map/ppermute | solution.py:70
  118.5 11.2 %collective-permute-start.28 = (bf16[128,640]{1,0:T(8,128)(2,1)S(1)}, bf16[128,640]{1,0:T(8,128)(2,1)S(1)}, u32[]{:S(2)}, u32[]{:S(2)}) collective-permute-start(bf16[128,640]{1,0:T(8,128)(2,1)S(1)} %get-tuple-element.77), channel_id=1, source_target_pairs={{0,28},{4,24},{8,20},{12,16},{16,12},{20,8},{24,4},{28,0},{1,29},{... | collective-permute-start | bytes 491528 | tf_op jit(solution)/shard_map/ppermute | solution.py:70
  131.0 6.0 %collective-permute-start.31 = (f32[1,256]{1,0:T(1,128)S(1)}, f32[1,256]{1,0:T(1,128)S(1)}, u32[]{:S(2)}, u32[]{:S(2)}) collective-permute-start(f32[1,256]{1,0:T(1,128)S(1)} %get-tuple-element.82.refs_0_), channel_id=1, source_target_pairs={{0,3},{1,2},{2,1},{3,0},{4,7},{5,6},{6,5},{7,4},{8,11},{9,10},{10,... | collective-permute-start | bytes 3080 | tf_op jit(solution)/shard_map/ppermute | solution.py:63
  133.3 4.5 %collective-permute-start.30 = (f32[1,256]{1,0:T(1,128)S(1)}, f32[1,256]{1,0:T(1,128)S(1)}, u32[]{:S(2)}, u32[]{:S(2)}) collective-permute-start(f32[1,256]{1,0:T(1,128)S(1)} %get-tuple-element.82.refs_0_), channel_id=1, source_target_pairs={{0,2},{1,3},{2,0},{3,1},{4,6},{5,7},{6,4},{7,5},{8,10},{9,11},{10,... | collective-permute-start | bytes 3080 | tf_op jit(solution)/shard_map/ppermute | solution.py:63
  134.5 3.6 %collective-permute-start.29 = (f32[1,256]{1,0:T(1,128)S(1)}, f32[1,256]{1,0:T(1,128)S(1)}, u32[]{:S(2)}, u32[]{:S(2)}) collective-permute-start(f32[1,256]{1,0:T(1,128)S(1)} %get-tuple-element.82.refs_0_), channel_id=1, source_target_pairs={{0,1},{1,0},{2,3},{3,2},{4,5},{5,4},{6,7},{7,6},{8,9},{9,8},{10,11... | collective-permute-start | bytes 3080 | tf_op jit(solution)/shard_map/ppermute | solution.py:63
  (12 other events, 65.0 us)

commit v6 on v5

--- a/solution.py
+++ b/solution.py
@@ -704,7 +704,9 @@
 
     own_term = marks = None
     while turns < shards - 2:
-        turn([functools.partial(finish, k == 0) for k in range(2)] if turns == shards - 3 else ())
+        turn()
+    finish(True)
+    finish(False)
     weight_sum = jnp.concatenate([sum(p.astype(F32) for p in parts) for parts in mine], axis=0)
     key_grad = key_grad_acc + jnp.stack(
         [weight_sum[:, j * width : (j + 1) * width] for j in range(key_count)]
@@ -713,7 +715,7 @@
 
     outgoing = pick_rows(marks, passing, own_term, ())
     incoming = [outgoing[0]] + [None] * (groups - 1)
-    for rel in range(groups - 1, 0, -1):
+    for rel in range(1, groups):
         incoming[rel] = swap_over("group", rel, outgoing[rel])
     row_grad, row_part = place_rows(
         shards, plan, incoming_rows, incoming, owned_rows, (key_grad, value_grad)

time: 140 us -> 140 us (level)
    ppermute x11, starting transfers between devices: 27.8 us -> 26 us  [ring_pass(): lax.ppermute(part, axis, [(order[i], order[(i + 1) % size]) for i in rang...]
    ppermute x11, waiting for transfers between devices: 18.2 us -> 19.7 us  [ring_pass(): lax.ppermute(part, axis, [(order[i], order[(i + 1) % size]) for i in rang...]
  transfers between devices with their start and end apart: 32 -> 32, of which waited for: 15 -> 14; matrix products, arithmetic and copies ran while one was open for 1% -> 1% of each run, Pallas kernels for 22% -> 22%
where the time goes in v6:
time: 140 us; the launch traced here: 139 us
  starting transfers between devices  49.9 us (36%)
  Pallas kernels  36.6 us (26%)
  waiting for transfers between devices  34.7 us (25%)
  blocking collectives  8.18 us (6%)
  local copies, waits for them, and re-layouts  8.08 us (6%)
    pallas_call x27, Pallas kernels, call(): pl.pallas_call(body, in_specs=in_specs + [ANY] * len(after), out_specs=[V...  33.9 us
    ppermute x11, starting transfers between devices, ring_pass(): lax.ppermute(part, axis, [(order[i], order[(i + 1) % size]) for i in rang...  26 us
    ppermute x11, waiting for transfers between devices, ring_pass(): lax.ppermute(part, axis, [(order[i], order[(i + 1) % size]) for i in rang...  19.7 us
    ppermute x15, starting transfers between devices, swap_over(): return lax.ppermute(part, axis, [(i, i ^ bit) for i in range(size)])  15 us
    ppermute x15, waiting for transfers between devices, swap_over(): return lax.ppermute(part, axis, [(i, i ^ bit) for i in range(size)])  10.2 us
    ppermute x6, starting transfers between devices, others_over(): lax.ppermute(part, axis, [(i, i ^ step) for i in range(size)])  8.91 us
    all_to_all x1, blocking collectives, on_device(): lax.all_to_all(slot_row, 'group', split_axis=0, concat_axis=0, tiled=True)  8.18 us
    unnamed x25, local copies, waits for them, and re-layouts  7.07 us
  transfers between devices with their start and end apart: 32, of which 14 were waited for; matrix products, arithmetic and copies ran while one was open for 1% of the time, Pallas kernels for 22%

profile of v6, /device:TPU:0, one launch (start us, length us, event | category | flops | bytes accessed | tf_op | source)
XLA Modules:
  0.0 139.2 jit_solution(2823050827264933906)
XLA Ops:
  2.2 4.1 %collective-permute-start.3 = (bf16[256,640]{1,0:T(8,128)(2,1)S(1)}, bf16[256,640]{1,0:T(8,128)(2,1)}, u32[]{:S(2)}, u32[]{:S(2)}) collective-permute-start(bf16[256,640]{1,0:T(8,128)(2,1)S(1)} %sum_rows.2.refs_1_.refs_2_), channel_id=1, source_target_pairs={{0,2},{2,3},{3,1},{1,0},{4,6},{6,7},{7,5},{5,4},{8,10},{10,11},{11... | collective-permute-start | bytes 983048 | tf_op jit(solution)/shard_map/ppermute | solution.py:57
  6.4 1.6 %collective-permute-start = (bf16[256,640]{1,0:T(8,128)(2,1)S(1)}, bf16[256,640]{1,0:T(8,128)(2,1)}, u32[]{:S(2)}, u32[]{:S(2)}) collective-permute-start(bf16[256,640]{1,0:T(8,128)(2,1)S(1)} %sum_rows.3.refs_1_.refs_5_), channel_id=1, source_target_pairs={{0,2},{2,3},{3,1},{1,0},{4,6},{6,7},{7,5},{5,4},{8,10},{10,11},{11... | collective-permute-start | bytes 983048 | tf_op jit(solution)/shard_map/ppermute | solution.py:57
  9.3 8.2 %all_to_all.9 = s32[8,1,128]{2,1,0:T(1,128)S(1)} all-to-all(s32[8,1,128]{2,1,0:T(1,128)S(1)} %bitcast.27), channel_id=1, replica_groups=mesh['group'=8,'tensor'=4] {'group'}, dimensions={0} | all-to-all | bytes 8192 | tf_op jit(solution)/shard_map/all_to_all | solution.py:610
  17.9 3.5 %collective-permute-done.refs_6_ = bf16[256,640]{1,0:T(8,128)(2,1)} collective-permute-done((bf16[256,640]{1,0:T(8,128)(2,1)S(1)}, bf16[256,640]{1,0:T(8,128)(2,1)}, u32[]{:S(2)}, u32[]{:S(2)}) %collective-permute-start) | collective-permute-done | bytes 327712 | tf_op jit(solution)/shard_map/ppermute | solution.py:57
  21.4 3.5 %collective-permute-start.1 = (bf16[256,640]{1,0:T(8,128)(2,1)}, bf16[256,640]{1,0:T(8,128)(2,1)S(1)}, u32[]{:S(2)}, u32[]{:S(2)}) collective-permute-start(bf16[256,640]{1,0:T(8,128)(2,1)} %collective-permute-done.refs_6_), channel_id=1, source_target_pairs={{0,2},{2,3},{3,1},{1,0},{4,6},{6,7},{7,5},{5,4},{8,10},{10,11},{11... | collective-permute-start | bytes 983048 | tf_op jit(solution)/shard_map/ppermute | solution.py:57
  25.6 3.0 %collective-permute-done.4.refs_4_ = bf16[256,640]{1,0:T(8,128)(2,1)} collective-permute-done((bf16[256,640]{1,0:T(8,128)(2,1)}, bf16[256,640]{1,0:T(8,128)(2,1)}, u32[]{:S(2)}, u32[]{:S(2)}) %collective-permute-start.4) | collective-permute-done | bytes 327712 | tf_op jit(solution)/shard_map/ppermute | solution.py:57
  28.6 3.4 %collective-permute-start.5 = (bf16[256,640]{1,0:T(8,128)(2,1)}, bf16[256,640]{1,0:T(8,128)(2,1)S(1)}, u32[]{:S(2)}, u32[]{:S(2)}) collective-permute-start(bf16[256,640]{1,0:T(8,128)(2,1)} %collective-permute-done.4.refs_4_), channel_id=1, source_target_pairs={{0,2},{2,3},{3,1},{1,0},{4,6},{6,7},{7,5},{5,4},{8,10},{10,11},{11... | collective-permute-start | bytes 983048 | tf_op jit(solution)/shard_map/ppermute | solution.py:57
  32.0 2.9 %copy-done = bf16[2,2560,640]{2,1,0:T(8,128)(2,1)S(1)} copy-done((bf16[2,2560,640]{2,1,0:T(8,128)(2,1)S(1)}, bf16[2,2560,640]{2,1,0:T(8,128)(2,1)}, u32[]{:S(2)}) %copy-start) | copy-done | bytes 6553624
  34.9 1.9 %copy-done.3 = bf16[2560,640]{1,0:T(8,128)(2,1)S(1)} copy-done((bf16[2560,640]{1,0:T(8,128)(2,1)S(1)}, bf16[2560,640]{1,0:T(8,128)(2,1)}, u32[]{:S(2)}) %copy-start.3) | copy-done | bytes 3276824
  39.1 6.2 %forward_early.1 = (f32[3,512,640]{2,1,0:T(8,128)S(1)}, bf16[2560,512]{1,0:T(8,128)(2,1)S(1)}) custom-call(s32[12]{0:T(128)S(1)} %pad_add_fusion.refs_0_, bf16[2560,1920]{1,0:T(8,128)(2,1)S(1)} %join_weights.1.refs_1_, bf16[256,640]{1,0:T(8,128)(2,1)S(1)} %sum_rows.2.refs_1_.refs_2_, bf16[256,640]{1,0:T(8,128)(2,1)} %after.3.refs_3_, ...), custom_call_target="tpu_custom_call" | custom-call | flops 188743680 | tf_op jit(solution)/shard_map/forward_early/pallas_call | solution.py:37
  45.3 2.1 %forward_late.2 = (f32[3,512,640]{2,1,0:T(8,128)S(1)}, bf16[2560,512]{1,0:T(8,128)(2,1)S(1)}, f32[8,256]{1,0:T(8,128)S(1)}) custom-call(s32[12]{0:T(128)S(1)} %pad_add_fusion.refs_0_, bf16[2560,1920]{1,0:T(8,128)(2,1)S(1)} %join_weights.1.refs_1_, bf16[256,640]{1,0:T(8,128)(2,1)S(1)} %collective-permute-done.5.refs_2_, ...), custom_call_target="tpu_custom_call", output_to_operand_aliasing={{0}: (3, {}), {1}: (4, {})} | custom-call | flops 31457280 | tf_op jit(solution)/shard_map/forward_late/pallas_call | solution.py:37
  48.4 2.1 %forward_late.3 = (f32[3,512,640]{2,1,0:T(8,128)S(1)}, bf16[2560,512]{1,0:T(8,128)(2,1)S(1)}, f32[8,512]{1,0:T(8,128)S(1)}) custom-call(s32[12]{0:T(128)S(1)} %pad_add_fusion.refs_0_, bf16[2560,1920]{1,0:T(8,128)(2,1)S(1)} %join_weights.1.refs_1_, bf16[256,640]{1,0:T(8,128)(2,1)S(1)} %collective-permute-done.2.refs_2_, ...), custom_call_target="tpu_custom_call", output_to_operand_aliasing={{0}: (3, {}), {1}: (4, {})} | custom-call | flops 31457280 | tf_op jit(solution)/shard_map/forward_late/pallas_call | solution.py:37
  50.6 3.6 %collective-permute-start.8 = (f32[8,512]{1,0:T(8,128)S(1)}, f32[8,512]{1,0:T(8,128)S(1)}, u32[]{:S(2)}, u32[]{:S(2)}) collective-permute-start(f32[8,512]{1,0:T(8,128)S(1)} %get-tuple-element.52.refs_0_), channel_id=1, source_target_pairs={{0,3},{1,2},{2,1},{3,0},{4,7},{5,6},{6,5},{7,4},{8,11},{9,10},{10,... | collective-permute-start | bytes 49160 | tf_op jit(solution)/shard_map/ppermute | solution.py:63
  56.2 2.6 %collective-permute-done.7.refs_2_ = f32[8,512]{1,0:T(8,128)S(1)} collective-permute-done((f32[8,512]{1,0:T(8,128)S(1)}, f32[8,512]{1,0:T(8,128)S(1)}, u32[]{:S(2)}, u32[]{:S(2)}) %collective-permute-start.7) | collective-permute-done | bytes 16416 | tf_op jit(solution)/shard_map/ppermute | solution.py:63
  60.2 1.8 %back.4.refs_5_ = bf16[512,640]{1,0:T(8,128)(2,1)S(1)} custom-call(bf16[512,1920]{1,0:T(8,128)(2,1)S(1)} %cotangents.1.refs_0_.refs_1_, bf16[2560,1920]{1,0:T(8,128)(2,1)S(1)} %join_weights.1.refs_1_), custom_call_target="tpu_custom_call" | custom-call | flops 62914560 | tf_op jit(solution)/shard_map/back/pallas_call | solution.py:37
  62.0 2.2 %collective-permute-start.13 = (bf16[512,640]{1,0:T(8,128)(2,1)S(1)}, bf16[512,640]{1,0:T(8,128)(2,1)S(1)}, u32[]{:S(2)}, u32[]{:S(2)}) collective-permute-start(bf16[512,640]{1,0:T(8,128)(2,1)S(1)} %back.4.refs_5_), channel_id=1, source_target_pairs={{0,2},{2,3},{3,1},{1,0},{4,6},{6,7},{7,5},{5,4},{8,10},{10,11},{11... | collective-permute-start | bytes 1966088 | tf_op jit(solution)/shard_map/ppermute | solution.py:57
  64.2 2.1 %outer.4 = (bf16[160,1920]{1,0:T(8,128)(2,1)S(1)}, bf16[160,1920]{1,0:T(8,128)(2,1)S(1)}) custom-call(s32[12]{0:T(128)S(1)} %pad_add_fusion.refs_0_, bf16[512,1920]{1,0:T(8,128)(2,1)S(1)} %cotangents.1.refs_0_.refs_1_, bf16[512,1920]{1,0:T(8,128)(2,1)S(1)} %collective-permute-done.10.refs_2_, bf16[2560,512]{1,0:T(8,128)(2,1)S(1)} %get-tuple-element.54.refs_3_, ...), custom_call_target="tpu_custom_call" | custom-call | flops 62914560 | tf_op jit(solution)/shard_map/outer/pallas_call | solution.py:37
  69.4 2.1 %outer.5 = (bf16[160,1920]{1,0:T(8,128)(2,1)S(1)}, bf16[160,1920]{1,0:T(8,128)(2,1)S(1)}) custom-call(s32[12]{0:T(128)S(1)} %pad_add_fusion.refs_0_, bf16[512,1920]{1,0:T(8,128)(2,1)S(1)} %cotangents.1.refs_0_.refs_1_, bf16[512,1920]{1,0:T(8,128)(2,1)S(1)} %collective-permute-done.10.refs_2_, bf16[2560,512]{1,0:T(8,128)(2,1)S(1)} %get-tuple-element.54.refs_3_, ...), custom_call_target="tpu_custom_call" | custom-call | flops 62914560 | tf_op jit(solution)/shard_map/outer/pallas_call | solution.py:37
  71.5 2.1 %outer.6 = (bf16[160,1920]{1,0:T(8,128)(2,1)S(1)}, bf16[160,1920]{1,0:T(8,128)(2,1)S(1)}) custom-call(s32[12]{0:T(128)S(1)} %pad_add_fusion.refs_0_, bf16[512,1920]{1,0:T(8,128)(2,1)S(1)} %cotangents.1.refs_0_.refs_1_, bf16[512,1920]{1,0:T(8,128)(2,1)S(1)} %collective-permute-done.10.refs_2_, bf16[2560,512]{1,0:T(8,128)(2,1)S(1)} %get-tuple-element.54.refs_3_, ...), custom_call_target="tpu_custom_call" | custom-call | flops 62914560 | tf_op jit(solution)/shard_map/outer/pallas_call | solution.py:37
  73.5 1.8 %back.5 = (bf16[512,384]{1,0:T(8,128)(2,1)S(1)}, bf16[512,256]{1,0:T(8,128)(2,1)S(1)}) custom-call(bf16[512,1920]{1,0:T(8,128)(2,1)S(1)} %cotangents.1.refs_0_.refs_1_, bf16[2560,1920]{1,0:T(8,128)(2,1)S(1)} %join_weights.1.refs_1_, bf16[160,1920]{1,0:T(8,128)(2,1)S(1)} %get-tuple-element.57.refs_2_.refs_0_), custom_call_target="tpu_custom_call" | custom-call | flops 62914560 | tf_op jit(solution)/shard_map/back/pallas_call | solution.py:37
  75.3 4.0 %collective-permute-done.13.refs_0_ = bf16[512,640]{1,0:T(8,128)(2,1)S(1)} collective-permute-done((bf16[512,640]{1,0:T(8,128)(2,1)S(1)}, bf16[512,640]{1,0:T(8,128)(2,1)S(1)}, u32[]{:S(2)}, u32[]{:S(2)}) %collective-permute-start.13) | collective-permute-done | bytes 655392 | tf_op jit(solution)/shard_map/ppermute | solution.py:57
  79.5 2.9 %collective-permute-start.16 = (bf16[512,384]{1,0:T(8,128)(2,1)S(1)}, bf16[512,384]{1,0:T(8,128)(2,1)S(1)}, u32[]{:S(2)}, u32[]{:S(2)}) collective-permute-start(bf16[512,384]{1,0:T(8,128)(2,1)S(1)} %add_part.4.refs_2_), channel_id=1, source_target_pairs={{0,2},{2,3},{3,1},{1,0},{4,6},{6,7},{7,5},{5,4},{8,10},{10,11},{11... | collective-permute-start | bytes 1179656 | tf_op jit(solution)/shard_map/ppermute | solution.py:57
  86.5 2.1 %outer.7 = (bf16[160,1920]{1,0:T(8,128)(2,1)S(1)}, bf16[160,1920]{1,0:T(8,128)(2,1)S(1)}) custom-call(s32[12]{0:T(128)S(1)} %pad_add_fusion.refs_0_, bf16[512,1920]{1,0:T(8,128)(2,1)S(1)} %cotangents.1.refs_0_.refs_1_, bf16[512,1920]{1,0:T(8,128)(2,1)S(1)} %collective-permute-done.10.refs_2_, bf16[2560,512]{1,0:T(8,128)(2,1)S(1)} %get-tuple-element.54.refs_3_, ...), custom_call_target="tpu_custom_call" | custom-call | flops 62914560 | tf_op jit(solution)/shard_map/outer/pallas_call | solution.py:37
  88.5 1.8 %back.6 = (bf16[512,384]{1,0:T(8,128)(2,1)S(1)}, bf16[512,256]{1,0:T(8,128)(2,1)S(1)}) custom-call(bf16[512,1920]{1,0:T(8,128)(2,1)S(1)} %cotangents.1.refs_0_.refs_1_, bf16[2560,1920]{1,0:T(8,128)(2,1)S(1)} %join_weights.1.refs_1_, bf16[160,1920]{1,0:T(8,128)(2,1)S(1)} %get-tuple-element.62.refs_2_.refs_0_), custom_call_target="tpu_custom_call" | custom-call | flops 62914560 | tf_op jit(solution)/shard_map/back/pallas_call | solution.py:37
  92.1 3.4 %collective-permute-start.20 = (bf16[512,384]{1,0:T(8,128)(2,1)S(1)}, bf16[512,384]{1,0:T(8,128)(2,1)S(1)}, u32[]{:S(2)}, u32[]{:S(2)}) collective-permute-start(bf16[512,384]{1,0:T(8,128)(2,1)S(1)} %add_part.6.refs_2_), channel_id=1, source_target_pairs={{0,2},{2,3},{3,1},{1,0},{4,6},{6,7},{7,5},{5,4},{8,10},{10,11},{11... | collective-permute-start | bytes 1179656 | tf_op jit(solution)/shard_map/ppermute | solution.py:57
  95.5 2.1 %collective-permute-done.15.refs_0_ = bf16[512,256]{1,0:T(8,128)(2,1)S(1)} collective-permute-done((bf16[512,256]{1,0:T(8,128)(2,1)S(1)}, bf16[512,256]{1,0:T(8,128)(2,1)S(1)}, u32[]{:S(2)}, u32[]{:S(2)}) %collective-permute-start.15) | collective-permute-done | bytes 262176 | tf_op jit(solution)/shard_map/ppermute | solution.py:57
  97.6 3.7 %collective-permute-start.21 = (bf16[512,256]{1,0:T(8,128)(2,1)S(1)}, bf16[512,256]{1,0:T(8,128)(2,1)S(1)}, u32[]{:S(2)}, u32[]{:S(2)}) collective-permute-start(bf16[512,256]{1,0:T(8,128)(2,1)S(1)} %add_part.7.refs_2_), channel_id=1, source_target_pairs={{0,2},{2,3},{3,1},{1,0},{4,6},{6,7},{7,5},{5,4},{8,10},{10,11},{11... | collective-permute-start | bytes 786440 | tf_op jit(solution)/shard_map/ppermute | solution.py:57
  102.8 1.8 %back.7 = (bf16[512,384]{1,0:T(8,128)(2,1)S(1)}, bf16[512,256]{1,0:T(8,128)(2,1)S(1)}) custom-call(bf16[512,1920]{1,0:T(8,128)(2,1)S(1)} %cotangents.1.refs_0_.refs_1_, bf16[2560,1920]{1,0:T(8,128)(2,1)S(1)} %join_weights.1.refs_1_, bf16[512,256]{1,0:T(8,128)(2,1)S(1)} %add_part.7.refs_2_), custom_call_target="tpu_custom_call" | custom-call | flops 62914560 | tf_op jit(solution)/shard_map/back/pallas_call | solution.py:37
  105.8 4.5 %collective-permute-done.21.refs_2_ = bf16[512,256]{1,0:T(8,128)(2,1)S(1)} collective-permute-done((bf16[512,256]{1,0:T(8,128)(2,1)S(1)}, bf16[512,256]{1,0:T(8,128)(2,1)S(1)}, u32[]{:S(2)}, u32[]{:S(2)}) %collective-permute-start.21) | collective-permute-done | bytes 262176 | tf_op jit(solution)/shard_map/ppermute | solution.py:57
  116.3 1.8 %collective-permute-start.27 = (bf16[128,640]{1,0:T(8,128)(2,1)S(1)}, bf16[128,640]{1,0:T(8,128)(2,1)S(1)}, u32[]{:S(2)}, u32[]{:S(2)}) collective-permute-start(bf16[128,640]{1,0:T(8,128)(2,1)S(1)} %get-tuple-element.76), channel_id=1, source_target_pairs={{0,24},{4,28},{8,16},{12,20},{16,8},{20,12},{24,0},{28,4},{1,25},{... | collective-permute-start | bytes 491528 | tf_op jit(solution)/shard_map/ppermute | solution.py:70
  121.1 8.6 %collective-permute-done.26.refs_7_ = bf16[128,640]{1,0:T(8,128)(2,1)S(1)} collective-permute-done((bf16[128,640]{1,0:T(8,128)(2,1)S(1)}, bf16[128,640]{1,0:T(8,128)(2,1)S(1)}, u32[]{:S(2)}, u32[]{:S(2)}) %collective-permute-start.26) | collective-permute-done | bytes 163872 | tf_op jit(solution)/shard_map/ppermute | solution.py:70
  131.0 2.3 %collective-permute-start.31 = (f32[1,256]{1,0:T(1,128)S(1)}, f32[1,256]{1,0:T(1,128)S(1)}, u32[]{:S(2)}, u32[]{:S(2)}) collective-permute-start(f32[1,256]{1,0:T(1,128)S(1)} %get-tuple-element.82.refs_0_), channel_id=1, source_target_pairs={{0,3},{1,2},{2,1},{3,0},{4,7},{5,6},{6,5},{7,4},{8,11},{9,10},{10,... | collective-permute-start | bytes 3080 | tf_op jit(solution)/shard_map/ppermute | solution.py:63
  (97 shorter events, 38.5 us)
Async XLA Ops:
  2.2 15.3 %collective-permute-start.3 = (bf16[256,640]{1,0:T(8,128)(2,1)S(1)}, bf16[256,640]{1,0:T(8,128)(2,1)}, u32[]{:S(2)}, u32[]{:S(2)}) collective-permute-start(bf16[256,640]{1,0:T(8,128)(2,1)S(1)} %sum_rows.2.refs_1_.refs_2_), channel_id=1, source_target_pairs={{0,2},{2,3},{3,1},{1,0},{4,6},{6,7},{7,5},{5,4},{8,10},{10,11},{11... | collective-permute-start | bytes 983048 | tf_op jit(solution)/shard_map/ppermute | solution.py:57
  6.4 15.0 %collective-permute-start = (bf16[256,640]{1,0:T(8,128)(2,1)S(1)}, bf16[256,640]{1,0:T(8,128)(2,1)}, u32[]{:S(2)}, u32[]{:S(2)}) collective-permute-start(bf16[256,640]{1,0:T(8,128)(2,1)S(1)} %sum_rows.3.refs_1_.refs_5_), channel_id=1, source_target_pairs={{0,2},{2,3},{3,1},{1,0},{4,6},{6,7},{7,5},{5,4},{8,10},{10,11},{11... | collective-permute-start | bytes 983048 | tf_op jit(solution)/shard_map/ppermute | solution.py:57
  17.5 11.1 %collective-permute-start.4 = (bf16[256,640]{1,0:T(8,128)(2,1)}, bf16[256,640]{1,0:T(8,128)(2,1)}, u32[]{:S(2)}, u32[]{:S(2)}) collective-permute-start(bf16[256,640]{1,0:T(8,128)(2,1)} %after.3.refs_3_), channel_id=1, source_target_pairs={{0,2},{2,3},{3,1},{1,0},{4,6},{6,7},{7,5},{5,4},{8,10},{10,11},{11... | collective-permute-start | bytes 983048 | tf_op jit(solution)/shard_map/ppermute | solution.py:57
  21.4 16.9 %collective-permute-start.1 = (bf16[256,640]{1,0:T(8,128)(2,1)}, bf16[256,640]{1,0:T(8,128)(2,1)S(1)}, u32[]{:S(2)}, u32[]{:S(2)}) collective-permute-start(bf16[256,640]{1,0:T(8,128)(2,1)} %collective-permute-done.refs_6_), channel_id=1, source_target_pairs={{0,2},{2,3},{3,1},{1,0},{4,6},{6,7},{7,5},{5,4},{8,10},{10,11},{11... | collective-permute-start | bytes 983048 | tf_op jit(solution)/shard_map/ppermute | solution.py:57
  28.6 16.8 %collective-permute-start.5 = (bf16[256,640]{1,0:T(8,128)(2,1)}, bf16[256,640]{1,0:T(8,128)(2,1)S(1)}, u32[]{:S(2)}, u32[]{:S(2)}) collective-permute-start(bf16[256,640]{1,0:T(8,128)(2,1)} %collective-permute-done.4.refs_4_), channel_id=1, source_target_pairs={{0,2},{2,3},{3,1},{1,0},{4,6},{6,7},{7,5},{5,4},{8,10},{10,11},{11... | collective-permute-start | bytes 983048 | tf_op jit(solution)/shard_map/ppermute | solution.py:57
  38.4 10.0 %collective-permute-start.2 = (bf16[256,640]{1,0:T(8,128)(2,1)S(1)}, bf16[256,640]{1,0:T(8,128)(2,1)S(1)}, u32[]{:S(2)}, u32[]{:S(2)}) collective-permute-start(bf16[256,640]{1,0:T(8,128)(2,1)S(1)} %after.2.refs_7_), channel_id=1, source_target_pairs={{0,2},{2,3},{3,1},{1,0},{4,6},{6,7},{7,5},{5,4},{8,10},{10,11},{11... | collective-permute-start | bytes 983048 | tf_op jit(solution)/shard_map/ppermute | solution.py:57
  50.5 8.3 %collective-permute-start.9 = (bf16[2560,512]{1,0:T(8,128)(2,1)S(1)}, bf16[2560,512]{1,0:T(8,128)(2,1)S(1)}, u32[]{:S(2)}, u32[]{:S(2)}) collective-permute-start(bf16[2560,512]{1,0:T(8,128)(2,1)S(1)} %get-tuple-element.54.refs_3_), channel_id=1, source_target_pairs={{0,4},{4,0},{8,12},{12,8},{16,20},{20,16},{24,28},{28,24},{1,5},{5... | collective-permute-start | bytes 7864328 | tf_op jit(solution)/shard_map/ppermute | solution.py:70
  50.6 5.6 %collective-permute-start.8 = (f32[8,512]{1,0:T(8,128)S(1)}, f32[8,512]{1,0:T(8,128)S(1)}, u32[]{:S(2)}, u32[]{:S(2)}) collective-permute-start(f32[8,512]{1,0:T(8,128)S(1)} %get-tuple-element.52.refs_0_), channel_id=1, source_target_pairs={{0,3},{1,2},{2,1},{3,0},{4,7},{5,6},{6,5},{7,4},{8,11},{9,10},{10,... | collective-permute-start | bytes 49160 | tf_op jit(solution)/shard_map/ppermute | solution.py:63
  54.2 4.7 %collective-permute-start.7 = (f32[8,512]{1,0:T(8,128)S(1)}, f32[8,512]{1,0:T(8,128)S(1)}, u32[]{:S(2)}, u32[]{:S(2)}) collective-permute-start(f32[8,512]{1,0:T(8,128)S(1)} %get-tuple-element.52.refs_0_), channel_id=1, source_target_pairs={{0,2},{1,3},{2,0},{3,1},{4,6},{5,7},{6,4},{7,5},{8,10},{9,11},{10,... | collective-permute-start | bytes 49160 | tf_op jit(solution)/shard_map/ppermute | solution.py:63
  54.5 4.4 %collective-permute-start.6 = (f32[8,512]{1,0:T(8,128)S(1)}, f32[8,512]{1,0:T(8,128)S(1)}, u32[]{:S(2)}, u32[]{:S(2)}) collective-permute-start(f32[8,512]{1,0:T(8,128)S(1)} %get-tuple-element.52.refs_0_), channel_id=1, source_target_pairs={{0,1},{1,0},{2,3},{3,2},{4,5},{5,4},{6,7},{7,6},{8,9},{9,8},{10,11... | collective-permute-start | bytes 49160 | tf_op jit(solution)/shard_map/ppermute | solution.py:63
  60.1 4.1 %collective-permute-start.10 = (bf16[512,1920]{1,0:T(8,128)(2,1)S(1)}, bf16[512,1920]{1,0:T(8,128)(2,1)S(1)}, u32[]{:S(2)}, u32[]{:S(2)}) collective-permute-start(bf16[512,1920]{1,0:T(8,128)(2,1)S(1)} %cotangents.1.refs_0_.refs_1_), channel_id=1, source_target_pairs={{0,4},{4,0},{8,12},{12,8},{16,20},{20,16},{24,28},{28,24},{1,5},{5... | collective-permute-start | bytes 5898248 | tf_op jit(solution)/shard_map/ppermute | solution.py:70
  62.0 17.4 %collective-permute-start.13 = (bf16[512,640]{1,0:T(8,128)(2,1)S(1)}, bf16[512,640]{1,0:T(8,128)(2,1)S(1)}, u32[]{:S(2)}, u32[]{:S(2)}) collective-permute-start(bf16[512,640]{1,0:T(8,128)(2,1)S(1)} %back.4.refs_5_), channel_id=1, source_target_pairs={{0,2},{2,3},{3,1},{1,0},{4,6},{6,7},{7,5},{5,4},{8,10},{10,11},{11... | collective-permute-start | bytes 1966088 | tf_op jit(solution)/shard_map/ppermute | solution.py:57
  66.3 19.2 %collective-permute-start.12 = (bf16[160,1920]{1,0:T(8,128)(2,1)S(1)}, bf16[160,1920]{1,0:T(8,128)(2,1)S(1)}, u32[]{:S(2)}, u32[]{:S(2)}) collective-permute-start(bf16[160,1920]{1,0:T(8,128)(2,1)S(1)} %get-tuple-element.59), channel_id=1, source_target_pairs={{0,16},{4,20},{8,24},{12,28},{16,0},{20,4},{24,8},{28,12},{1,17},{... | collective-permute-start | bytes 1843208 | tf_op jit(solution)/shard_map/ppermute | solution.py:70
  67.9 17.8 %collective-permute-start.11 = (bf16[160,1920]{1,0:T(8,128)(2,1)S(1)}, bf16[160,1920]{1,0:T(8,128)(2,1)S(1)}, u32[]{:S(2)}, u32[]{:S(2)}) collective-permute-start(bf16[160,1920]{1,0:T(8,128)(2,1)S(1)} %get-tuple-element.55.refs_5_), channel_id=1, source_target_pairs={{0,8},{4,12},{8,0},{12,4},{16,24},{20,28},{24,16},{28,20},{1,9},{5... | collective-permute-start | bytes 1843208 | tf_op jit(solution)/shard_map/ppermute | solution.py:70
  79.5 12.4 %collective-permute-start.16 = (bf16[512,384]{1,0:T(8,128)(2,1)S(1)}, bf16[512,384]{1,0:T(8,128)(2,1)S(1)}, u32[]{:S(2)}, u32[]{:S(2)}) collective-permute-start(bf16[512,384]{1,0:T(8,128)(2,1)S(1)} %add_part.4.refs_2_), channel_id=1, source_target_pairs={{0,2},{2,3},{3,1},{1,0},{4,6},{6,7},{7,5},{5,4},{8,10},{10,11},{11... | collective-permute-start | bytes 1179656 | tf_op jit(solution)/shard_map/ppermute | solution.py:57
  82.4 18.9 %collective-permute-start.14 = (bf16[160,1920]{1,0:T(8,128)(2,1)S(1)}, bf16[160,1920]{1,0:T(8,128)(2,1)S(1)}, u32[]{:S(2)}, u32[]{:S(2)}) collective-permute-start(bf16[160,1920]{1,0:T(8,128)(2,1)S(1)} %get-tuple-element.56.refs_5_), channel_id=1, source_target_pairs={{0,8},{4,12},{8,0},{12,4},{16,24},{20,28},{24,16},{28,20},{1,9},{5... | collective-permute-start | bytes 1843208 | tf_op jit(solution)/shard_map/ppermute | solution.py:70
  83.9 20.8 %collective-permute-start.18 = (bf16[160,1920]{1,0:T(8,128)(2,1)S(1)}, bf16[160,1920]{1,0:T(8,128)(2,1)S(1)}, u32[]{:S(2)}, u32[]{:S(2)}) collective-permute-start(bf16[160,1920]{1,0:T(8,128)(2,1)S(1)} %get-tuple-element.67), channel_id=1, source_target_pairs={{0,16},{4,20},{8,24},{12,28},{16,0},{20,4},{24,8},{28,12},{1,17},{... | collective-permute-start | bytes 1843208 | tf_op jit(solution)/shard_map/ppermute | solution.py:70
  85.8 27.5 %collective-permute-start.17 = (bf16[160,1920]{1,0:T(8,128)(2,1)S(1)}, bf16[160,1920]{1,0:T(8,128)(2,1)S(1)}, u32[]{:S(2)}, u32[]{:S(2)}) collective-permute-start(bf16[160,1920]{1,0:T(8,128)(2,1)S(1)} %add.32.refs_5_), channel_id=1, source_target_pairs={{0,16},{4,20},{8,24},{12,28},{16,0},{20,4},{24,8},{28,12},{1,17},{... | collective-permute-start | bytes 1843208 | tf_op jit(solution)/shard_map/ppermute | solution.py:70
  86.4 11.2 %collective-permute-start.15 = (bf16[512,256]{1,0:T(8,128)(2,1)S(1)}, bf16[512,256]{1,0:T(8,128)(2,1)S(1)}, u32[]{:S(2)}, u32[]{:S(2)}) collective-permute-start(bf16[512,256]{1,0:T(8,128)(2,1)S(1)} %add_part.5.refs_2_), channel_id=1, source_target_pairs={{0,2},{2,3},{3,1},{1,0},{4,6},{6,7},{7,5},{5,4},{8,10},{10,11},{11... | collective-permute-start | bytes 786440 | tf_op jit(solution)/shard_map/ppermute | solution.py:57
  92.1 18.3 %collective-permute-start.20 = (bf16[512,384]{1,0:T(8,128)(2,1)S(1)}, bf16[512,384]{1,0:T(8,128)(2,1)S(1)}, u32[]{:S(2)}, u32[]{:S(2)}) collective-permute-start(bf16[512,384]{1,0:T(8,128)(2,1)S(1)} %add_part.6.refs_2_), channel_id=1, source_target_pairs={{0,2},{2,3},{3,1},{1,0},{4,6},{6,7},{7,5},{5,4},{8,10},{10,11},{11... | collective-permute-start | bytes 1179656 | tf_op jit(solution)/shard_map/ppermute | solution.py:57
  97.6 12.7 %collective-permute-start.21 = (bf16[512,256]{1,0:T(8,128)(2,1)S(1)}, bf16[512,256]{1,0:T(8,128)(2,1)S(1)}, u32[]{:S(2)}, u32[]{:S(2)}) collective-permute-start(bf16[512,256]{1,0:T(8,128)(2,1)S(1)} %add_part.7.refs_2_), channel_id=1, source_target_pairs={{0,2},{2,3},{3,1},{1,0},{4,6},{6,7},{7,5},{5,4},{8,10},{10,11},{11... | collective-permute-start | bytes 786440 | tf_op jit(solution)/shard_map/ppermute | solution.py:57
  101.3 13.7 %collective-permute-start.19 = (bf16[160,1920]{1,0:T(8,128)(2,1)S(1)}, bf16[160,1920]{1,0:T(8,128)(2,1)S(1)}, u32[]{:S(2)}, u32[]{:S(2)}) collective-permute-start(bf16[160,1920]{1,0:T(8,128)(2,1)S(1)} %add.31.refs_2_), channel_id=1, source_target_pairs={{0,8},{4,12},{8,0},{12,4},{16,24},{20,28},{24,16},{28,20},{1,9},{5... | collective-permute-start | bytes 1843208 | tf_op jit(solution)/shard_map/ppermute | solution.py:70
  111.4 5.0 %collective-permute-start.22 = (bf16[128,640]{1,0:T(8,128)(2,1)S(1)}, bf16[128,640]{1,0:T(8,128)(2,1)S(1)}, u32[]{:S(2)}, u32[]{:S(2)}) collective-permute-start(bf16[128,640]{1,0:T(8,128)(2,1)S(1)} %get-tuple-element.71), channel_id=1, source_target_pairs={{0,4},{4,0},{8,12},{12,8},{16,20},{20,16},{24,28},{28,24},{1,5},{5... | collective-permute-start | bytes 491528 | tf_op jit(solution)/shard_map/ppermute | solution.py:70
  111.4 7.1 %collective-permute-start.23 = (bf16[128,640]{1,0:T(8,128)(2,1)S(1)}, bf16[128,640]{1,0:T(8,128)(2,1)S(1)}, u32[]{:S(2)}, u32[]{:S(2)}) collective-permute-start(bf16[128,640]{1,0:T(8,128)(2,1)S(1)} %get-tuple-element.72), channel_id=1, source_target_pairs={{0,8},{4,12},{8,0},{12,4},{16,24},{20,28},{24,16},{28,20},{1,9},{5... | collective-permute-start | bytes 491528 | tf_op jit(solution)/shard_map/ppermute | solution.py:70
  113.0 8.1 %collective-permute-start.24 = (bf16[128,640]{1,0:T(8,128)(2,1)S(1)}, bf16[128,640]{1,0:T(8,128)(2,1)S(1)}, u32[]{:S(2)}, u32[]{:S(2)}) collective-permute-start(bf16[128,640]{1,0:T(8,128)(2,1)S(1)} %get-tuple-element.73), channel_id=1, source_target_pairs={{0,12},{4,8},{8,4},{12,0},{16,28},{20,24},{24,20},{28,16},{1,13},{... | collective-permute-start | bytes 491528 | tf_op jit(solution)/shard_map/ppermute | solution.py:70
  113.3 7.8 %collective-permute-start.25 = (bf16[128,640]{1,0:T(8,128)(2,1)S(1)}, bf16[128,640]{1,0:T(8,128)(2,1)S(1)}, u32[]{:S(2)}, u32[]{:S(2)}) collective-permute-start(bf16[128,640]{1,0:T(8,128)(2,1)S(1)} %get-tuple-element.74), channel_id=1, source_target_pairs={{0,16},{4,20},{8,24},{12,28},{16,0},{20,4},{24,8},{28,12},{1,17},{... | collective-permute-start | bytes 491528 | tf_op jit(solution)/shard_map/ppermute | solution.py:70
  115.0 14.7 %collective-permute-start.26 = (bf16[128,640]{1,0:T(8,128)(2,1)S(1)}, bf16[128,640]{1,0:T(8,128)(2,1)S(1)}, u32[]{:S(2)}, u32[]{:S(2)}) collective-permute-start(bf16[128,640]{1,0:T(8,128)(2,1)S(1)} %get-tuple-element.75), channel_id=1, source_target_pairs={{0,20},{4,16},{8,28},{12,24},{16,4},{20,0},{24,12},{28,8},{1,21},{... | collective-permute-start | bytes 491528 | tf_op jit(solution)/shard_map/ppermute | solution.py:70
  116.3 13.4 %collective-permute-start.27 = (bf16[128,640]{1,0:T(8,128)(2,1)S(1)}, bf16[128,640]{1,0:T(8,128)(2,1)S(1)}, u32[]{:S(2)}, u32[]{:S(2)}) collective-permute-start(bf16[128,640]{1,0:T(8,128)(2,1)S(1)} %get-tuple-element.76), channel_id=1, source_target_pairs={{0,24},{4,28},{8,16},{12,20},{16,8},{20,12},{24,0},{28,4},{1,25},{... | collective-permute-start | bytes 491528 | tf_op jit(solution)/shard_map/ppermute | solution.py:70
  118.5 11.2 %collective-permute-start.28 = (bf16[128,640]{1,0:T(8,128)(2,1)S(1)}, bf16[128,640]{1,0:T(8,128)(2,1)S(1)}, u32[]{:S(2)}, u32[]{:S(2)}) collective-permute-start(bf16[128,640]{1,0:T(8,128)(2,1)S(1)} %get-tuple-element.77), channel_id=1, source_target_pairs={{0,28},{4,24},{8,20},{12,16},{16,12},{20,8},{24,4},{28,0},{1,29},{... | collective-permute-start | bytes 491528 | tf_op jit(solution)/shard_map/ppermute | solution.py:70
  131.0 6.0 %collective-permute-start.31 = (f32[1,256]{1,0:T(1,128)S(1)}, f32[1,256]{1,0:T(1,128)S(1)}, u32[]{:S(2)}, u32[]{:S(2)}) collective-permute-start(f32[1,256]{1,0:T(1,128)S(1)} %get-tuple-element.82.refs_0_), channel_id=1, source_target_pairs={{0,3},{1,2},{2,1},{3,0},{4,7},{5,6},{6,5},{7,4},{8,11},{9,10},{10,... | collective-permute-start | bytes 3080 | tf_op jit(solution)/shard_map/ppermute | solution.py:63
  133.3 4.5 %collective-permute-start.30 = (f32[1,256]{1,0:T(1,128)S(1)}, f32[1,256]{1,0:T(1,128)S(1)}, u32[]{:S(2)}, u32[]{:S(2)}) collective-permute-start(f32[1,256]{1,0:T(1,128)S(1)} %get-tuple-element.82.refs_0_), channel_id=1, source_target_pairs={{0,2},{1,3},{2,0},{3,1},{4,6},{5,7},{6,4},{7,5},{8,10},{9,11},{10,... | collective-permute-start | bytes 3080 | tf_op jit(solution)/shard_map/ppermute | solution.py:63
  134.5 3.6 %collective-permute-start.29 = (f32[1,256]{1,0:T(1,128)S(1)}, f32[1,256]{1,0:T(1,128)S(1)}, u32[]{:S(2)}, u32[]{:S(2)}) collective-permute-start(f32[1,256]{1,0:T(1,128)S(1)} %get-tuple-element.82.refs_0_), channel_id=1, source_target_pairs={{0,1},{1,0},{2,3},{3,2},{4,5},{5,4},{6,7},{7,6},{8,9},{9,8},{10,11... | collective-permute-start | bytes 3080 | tf_op jit(solution)/shard_map/ppermute | solution.py:63
  (12 other events, 65.1 us)
